TPU v7x, 32 devices: a whole 2x2x4 slice. The times are simulated.
32 devices in a mesh: row: 4 (over y, core), col: 8 (over z, x).
Axes of the slice: x: 2, y: 2, z: 4, core: 2. Of those that a mesh axis runs over, the one named last changes fastest.
Arguments:
- child_fronts: float32 [2, 8192, 8192], P(None, 'row', 'col'), may hold values from 0 to 50
- parent_entries: float32 [8192, 8192], P('row', 'col'), may hold values from 0 to 50, as said below
- block_map: int32 [2, 30], replicated, may hold values from 0 to 31, as said below
Outputs:
- child_factored: float32 [2, 8192, 8192], P(None, 'row', 'col')
- parent_factored: float32 [8192, 8192], P('row', 'col')
Inputs may be any that keep to these rules, and one draw needn't show every extreme that they name: `parent_entries`: symmetric and positive definite. `block_map`: each row is strictly increasing, begins with 0, ends with 31 and never takes the value 30.
All inputs are finite; a program needn't handle non-finite values.
Results may differ from a plain program's by a relative error of at most 0.0003.
Values sent between devices are 32-bit elements; how exact they have to be, the bound alone decides.
No kernel may reach another device: no remote copies, remote signals or barrier semaphores. Data moves between devices by JAX's collectives and lax.ppermute only.
A program may use at most 192 MiB of HBM per device.

v0:
```python
import jax
import jax.numpy as jnp
from jax import lax
from jax.sharding import PartitionSpec as P

SEP = 512
BLK = 256


def broadcast(value, axis, source):
    kept = jnp.where(lax.axis_index(axis) == source, value, 0).astype(value.dtype)
    return lax.psum(kept, axis)


def from_behind(value, axis, steps):
    count = lax.axis_size(axis)
    first, last = (max(0, -steps), min(count, count - steps))
    return lax.ppermute(value, axis, [(source, source + steps) for source in range(first, last)])


def solve_lower(factor_mat, right_side):
    return jax.scipy.linalg.solve_triangular(factor_mat, right_side, lower=True)


def partial_factor(front_block):
    count_fronts = front_block.shape[0]
    rows_loc = front_block.shape[1]
    cols_loc = front_block.shape[2]
    row_pos = lax.axis_index("row") * rows_loc + jnp.arange(rows_loc)
    col_pos = lax.axis_index("col") * cols_loc + jnp.arange(cols_loc)
    sep_cols = broadcast(front_block[:, :, :SEP], "col", 0)
    pivot_block = sep_cols[:, :SEP, :]
    lower_factor = jax.vmap(jnp.linalg.cholesky)(pivot_block)
    top_rows = front_block[:, :SEP, :]
    factor_top = jax.vmap(solve_lower)(lower_factor, top_rows)
    panel_pair = jnp.concatenate([lower_factor, factor_top], axis=2)
    received = broadcast(panel_pair, "row", 0)
    factor_all = received[:, :, SEP:]
    left_rows = jax.vmap(solve_lower)(received[:, :, :SEP], jnp.swapaxes(sep_cols, 1, 2))
    update = jnp.einsum("bsi,bsj->bij", left_rows, factor_all, precision=lax.Precision.HIGHEST)
    schur_block = front_block - update
    sep_row = (row_pos < SEP)[None, :, None]
    sep_col = (col_pos < SEP)[None, None, :]
    contrib = jnp.where(sep_row | sep_col, 0.0, schur_block)
    padded_top = jnp.concatenate(
        [factor_top, jnp.zeros((count_fronts, rows_loc - SEP, cols_loc), jnp.float32)], axis=1
    )
    result = jnp.where(sep_row, padded_top, contrib)
    return (result, contrib)


def block_select(source_first, source_count, target_first, target_count, block_map):
    gap_blocks = SEP // BLK
    source_ids = source_first + jnp.arange(source_count)
    target_ids = target_first + jnp.arange(target_count)
    child_slots = gap_blocks + jnp.arange(block_map.shape[1])
    source_match = (source_ids[:, None] == child_slots[None, :]).astype(jnp.float32)
    target_match = (block_map[:, :, None] == target_ids[None, None, :]).astype(jnp.float32)
    return jnp.einsum("ki,biq->bkq", source_match, target_match)


def extend_add(contrib, block_map):
    count_children = contrib.shape[0]
    rows_loc = contrib.shape[1]
    cols_loc = contrib.shape[2]
    row_blocks = rows_loc // BLK
    col_blocks = cols_loc // BLK
    gap_blocks = SEP // BLK
    col_first = lax.axis_index("col") * col_blocks
    row_first = lax.axis_index("row") * row_blocks
    next_cols = from_behind(contrib[:, :, :SEP], "col", -1)
    widened = jnp.concatenate([contrib, next_cols], axis=2)
    wide_count = col_blocks + gap_blocks
    col_select = block_select(col_first, wide_count, col_first, col_blocks, block_map)
    widened = widened.reshape(count_children, rows_loc, wide_count, BLK)
    col_done = jnp.einsum("bxky,bkq->bxqy", widened, col_select, precision=lax.Precision.HIGHEST)
    col_done = col_done.reshape(count_children, rows_loc, cols_loc)
    next_rows = from_behind(col_done[:, :SEP, :], "row", -1)
    tall_rows = jnp.concatenate([col_done, next_rows], axis=1)
    tall_count = row_blocks + gap_blocks
    row_select = block_select(row_first, tall_count, row_first, row_blocks, block_map)
    tall_rows = tall_rows.reshape(count_children, tall_count, BLK, cols_loc)
    merged = jnp.einsum("bkxj,bkp->pxj", tall_rows, row_select, precision=lax.Precision.HIGHEST)
    return merged.reshape(rows_loc, cols_loc)


def local(child_fronts, parent_entries, block_map):
    child_result, child_contrib = partial_factor(child_fronts)
    parent_front = parent_entries + extend_add(child_contrib, block_map)
    parent_result, parent_contrib = partial_factor(parent_front[None])
    return (child_result, parent_result[0])


def solution(mesh):
    placed = (P(None, "row", "col"), P("row", "col"), P())
    return jax.shard_map(
        local,
        mesh=mesh,
        in_specs=placed,
        out_specs=(P(None, "row", "col"), P("row", "col")),
        check_vma=False,
    )
```

profile of v0, /device:TPU:14, one launch (start us, length us, event | category | flops | bytes accessed | tf_op | source)
XLA Modules:
  0.0 1767.6 jit_solution(8596493688739039203)
XLA Ops:
  7.2 17.3 copy.96
  24.6 8.4 slice_select_fusion
  33.2 269.8 %all-reduce.7.cloned.1.call-done = f32[2,2048,512]{1,2,0:T(8,128)} async-done(((f32[2,2048,512]{1,2,0:T(8,128)}), f32[2,2048,512]{1,2,0:T(8,128)}) %all-reduce.7.cloned.1.call-update) | async-done | bytes 8388624 | tf_op jit(solution)/shard_map/psum | solution.py:12
  306.3 2.7 fusion.60
  309.1 23.5 %custom-call.78 = f32[2,128,128]{2,1,0:T(8,128)S(1)} custom-call(f32[2,128,128]{2,1,0:T(8,128)S(1)} %cholesky.541), custom_call_target="Cholesky" | custom-call | tf_op jit(solution)/shard_map/vmap(jit(cholesky))/cholesky | solution.py:33
  332.6 19.7 %custom-call.79 = f32[2,1,128,128]{2,3,1,0:T(8,128)S(1)} custom-call(f32[2,1,128,128]{3,2,1,0:T(8,128)S(1)} %select_bitcast_fusion.2), custom_call_target="InvertDiagBlocksLowerTriangular" | custom-call | tf_op jit(solution)/shard_map/vmap(jit(cholesky))/cholesky | solution.py:33
  354.7 23.7 %custom-call.80 = f32[2,128,128]{2,1,0:T(8,128)S(1)} custom-call(f32[2,128,128]{2,1,0:T(8,128)S(1)} %cholesky.545), custom_call_target="Cholesky" | custom-call | tf_op jit(solution)/shard_map/vmap(jit(cholesky))/cholesky | solution.py:33
  378.4 19.7 %custom-call.81 = f32[2,1,128,128]{2,3,1,0:T(8,128)S(1)} custom-call(f32[2,1,128,128]{3,2,1,0:T(8,128)S(1)} %get-tuple-element.91), custom_call_target="InvertDiagBlocksLowerTriangular" | custom-call | tf_op jit(solution)/shard_map/vmap(jit(cholesky))/cholesky | solution.py:33
  401.0 23.5 %custom-call.82 = f32[2,128,128]{2,1,0:T(8,128)S(1)} custom-call(f32[2,128,128]{2,1,0:T(8,128)S(1)} %cholesky.550), custom_call_target="Cholesky" | custom-call | tf_op jit(solution)/shard_map/vmap(jit(cholesky))/cholesky | solution.py:33
  424.5 20.1 %custom-call.83 = f32[2,1,128,128]{2,3,1,0:T(8,128)S(1)} custom-call(f32[2,1,128,128]{3,2,1,0:T(8,128)S(1)} %get-tuple-element.89), custom_call_target="InvertDiagBlocksLowerTriangular" | custom-call | tf_op jit(solution)/shard_map/vmap(jit(cholesky))/cholesky | solution.py:33
  446.4 23.5 %custom-call.84 = f32[2,128,128]{2,1,0:T(8,128)S(1)} custom-call(f32[2,128,128]{2,1,0:T(8,128)S(1)} %convolution_subtract_fusion.4), custom_call_target="Cholesky" | custom-call | tf_op jit(solution)/shard_map/vmap(jit(cholesky))/cholesky | solution.py:33
  470.2 2.7 broadcast_select_fusion.1
  473.0 11.5 while.4
  484.5 78.8 %custom-call.85 = f32[2,4,128,128]{2,3,1,0:T(8,128)S(1)} custom-call(f32[2,4,128,128]{3,2,1,0:T(8,128)S(1)} %bitcast.380), custom_call_target="InvertDiagBlocksLowerTriangular" | custom-call | tf_op jit(solution)/shard_map/vmap(jit(_solve_triangular))/triangular_solve | solution.py:22
  563.3 2.5 fusion.89
  569.2 2.6 fusion.66
  573.8 3.6 fusion.69
  580.3 3.0 maximum_select_fusion
  586.3 2.5 copy.117
  597.6 6.1 broadcast_dynamic-update-slice_fusion
  603.7 99.4 %all-reduce.9.cloned.1.call-done = f32[2,512,1536]{2,1,0:T(8,128)} async-done(((f32[2,512,1536]{2,1,0:T(8,128)}), f32[2,512,1536]{2,1,0:T(8,128)}) %all-reduce.9.cloned.1.call-update) | async-done | bytes 6291472 | tf_op jit(solution)/shard_map/psum | solution.py:12
  705.1 7.7 while.5
  712.8 79.0 %custom-call.86 = f32[2,4,128,128]{2,3,1,0:T(8,128)S(1)} custom-call(f32[2,4,128,128]{3,2,1,0:T(8,128)S(1)} %bitcast.381), custom_call_target="InvertDiagBlocksLowerTriangular" | custom-call | tf_op jit(solution)/shard_map/vmap(jit(_solve_triangular))/triangular_solve | solution.py:22
  791.9 3.5 fusion.52
  795.4 3.7 convolution_subtract_fusion
  801.1 4.9 fusion.39
  808.0 5.4 fusion.42
  813.4 3.3 fusion.103
  816.7 38.7 %broadcast_select_fusion = (f32[2,2048,1024]{1,2,0:T(8,128)}, f32[2,2048,1024]{1,2,0:T(8,128)}) fusion(f32[2,2048,1024]{1,2,0:T(8,128)} %broadcast_dynamic-update-slice_fusion, pred[2048]{0:T(1024)(128)(4,1)S(1)} %add_compare_fusion, f32[2,2048,1024]{1,2,0:T(8,128)} %copy.96, f32[2,512,1536]{2,1,0:T(8,128)} %all-reduce.9.cloned.1.call-done, ...), kind=kOutput, calls=%fused_computation.22 | convolution fusion | flops 25788678144 | bytes 81790976 | tf_op jit(solution)/shard_map/bsi,bsj->bij/dot_general | solution.py:40
  855.4 7.9 slice.400
  863.3 2.5 collective-permute-start
  866.0 182.8 %collective-permute-done = f32[2,2048,512]{1,2,0:T(8,128)} collective-permute-done((f32[2,2048,512]{1,2,0:T(8,128)}, f32[2,2048,512]{1,2,0:T(8,128)}, u32[]{:S(2)}, u32[]{:S(2)}) %collective-permute-start) | collective-permute-done | bytes 8388640 | tf_op jit(solution)/shard_map/ppermute | solution.py:18
  1048.8 18.7 %pad_maximum_fusion = f32[2,2048,1536]{1,2,0:T(8,128)} fusion(f32[2,2048,512]{1,2,0:T(8,128)} %collective-permute-done, f32[2,2048,1024]{1,2,0:T(8,128)} %get-tuple-element.104), kind=kLoop, calls=%fused_computation.8 | loop fusion | flops 6291456 | bytes 50331648 | tf_op jit(solution)/shard_map/concatenate | solution.py:72
  1067.5 30.6 %copy.125 = f32[2,2048,6,256]{3,2,1,0:T(8,128)} copy(f32[2,2048,6,256]{1,3,2,0:T(8,128)} %bitcast.346) | data formatting | bytes 50331648 | tf_op jit(solution)/shard_map/reshape | solution.py:75
  1098.1 35.9 %convolution_bitcast_fusion = f32[2,2048,4,256]{3,2,1,0:T(4,128)} fusion(f32[2,4,6,1]{2,1,3,0:T(4,128)S(1)} %convolution_bitcast_fusion.14, f32[2,2048,6,256]{3,2,1,0:T(8,128)} %copy.125), kind=kOutput, calls=%fused_computation.11 | convolution fusion | flops 301989888 | bytes 41943232 | tf_op jit(solution)/shard_map/bxky,bkq->bxqy/dot_general | solution.py:76
  1134.0 20.6 %reshape.454 = f32[2,2048,1024]{2,1,0:T(8,128)} reshape(f32[2,2048,4,256]{3,2,1,0:T(4,128)} %convolution_bitcast_fusion) | data formatting | bytes 33554432 | tf_op jit(solution)/shard_map/reshape | solution.py:77
  1154.6 4.8 slice.401
  1161.3 9.5 copy.128
  1171.1 36.6 %collective-permute-done.1 = f32[2,512,1024]{2,1,0:T(8,128)} collective-permute-done((f32[2,512,1024]{2,1,0:T(8,128)}, f32[2,512,1024]{2,1,0:T(8,128)}, u32[]{:S(2)}, u32[]{:S(2)}) %collective-permute-start.1) | collective-permute-done | bytes 4194336 | tf_op jit(solution)/shard_map/ppermute | solution.py:18
  1207.7 19.2 %pad_maximum_fusion.1 = f32[2,2560,1024]{2,1,0:T(8,128)} fusion(f32[2,512,1024]{2,1,0:T(8,128)} %collective-permute-done.1, f32[2,2048,1024]{2,1,0:T(8,128)} %reshape.454), kind=kLoop, calls=%fused_computation.9 | loop fusion | flops 5242880 | bytes 41943040 | tf_op jit(solution)/shard_map/concatenate | solution.py:79
  1226.8 27.4 %copy.160 = f32[2,10,256,1024]{2,1,0,3:T(8,128)} copy(f32[2,10,256,1024]{3,2,1,0:T(8,128)} %bitcast.347) | data formatting | bytes 41943040 | tf_op jit(solution)/shard_map/reshape | solution.py:82
  1254.3 19.8 %fusion.150 = f32[8,256,1024,1]{1,0,3,2:T(8,128)S(1)} fusion(f32[2,10,8,1]{1,2,0,3:T(8,128)S(1)} %convolution_bitcast_fusion.13, f32[2,10,256,1024]{2,1,0,3:T(8,128)} %copy.160), kind=kOutput, calls=%fused_computation.279 | convolution fusion | flops 503316480 | bytes 29360768 | tf_op jit(solution)/shard_map/bkxj,bkp->pxj/dot_general | solution.py:83
  1274.0 7.5 copy.184
  1281.5 11.9 add.185
  1293.4 4.7 slice_select_fusion.1
  1298.4 155.0 %all-reduce.11.cloned.1.call-done = f32[1,2048,512]{1,2,0:T(8,128)} async-done(((f32[1,2048,512]{1,2,0:T(8,128)}), f32[1,2048,512]{1,2,0:T(8,128)}) %all-reduce.11.cloned.1.call-update) | async-done | bytes 4194320 | tf_op jit(solution)/shard_map/psum | solution.py:12
  1456.5 11.7 custom-call.87
  1468.4 9.8 custom-call.88
  1479.3 11.7 custom-call.89
  1492.4 10.2 custom-call.90
  1503.2 11.7 custom-call.91
  1515.6 9.8 custom-call.92
  1526.0 11.9 custom-call.93
  1541.4 8.1 while.6
  1549.6 39.3 %custom-call.94 = f32[1,4,128,128]{2,3,1,0:T(8,128)S(1)} custom-call(f32[1,4,128,128]{3,2,1,0:T(8,128)S(1)} %bitcast.383), custom_call_target="InvertDiagBlocksLowerTriangular" | custom-call | tf_op jit(solution)/shard_map/vmap(jit(_solve_triangular))/triangular_solve | solution.py:22
  1593.3 2.9 fusion.78
  1596.8 3.8 fusion.76
  1603.3 18.1 %copy.141 = f32[2,2048,1024]{2,1,0:T(8,128)} copy(f32[2,2048,1024]{1,2,0:T(8,128)} %get-tuple-element.103) | data formatting | bytes 33554432
  1625.7 3.4 broadcast_dynamic-update-slice_fusion.1
  1629.2 42.7 %all-reduce.13.cloned.1.call-done = f32[1,512,1536]{2,1,0:T(8,128)} async-done(((f32[1,512,1536]{2,1,0:T(8,128)}), f32[1,512,1536]{2,1,0:T(8,128)}) %all-reduce.13.cloned.1.call-update) | async-done | bytes 3145744 | tf_op jit(solution)/shard_map/psum | solution.py:12
  1673.3 7.8 while.7
  1681.0 39.5 %custom-call.95 = f32[1,4,128,128]{2,3,1,0:T(8,128)S(1)} custom-call(f32[1,4,128,128]{3,2,1,0:T(8,128)S(1)} %bitcast.382), custom_call_target="InvertDiagBlocksLowerTriangular" | custom-call | tf_op jit(solution)/shard_map/vmap(jit(_solve_triangular))/triangular_solve | solution.py:22
  1731.8 19.5 %select_select_fusion = f32[2048,1024]{0,1:T(8,128)} fusion(f32[2048,1024]{0,1:T(8,128)} %broadcast_dynamic-update-slice_fusion.1, f32[2048,1024]{0,1:T(8,128)S(1)} %bitcast.354, pred[2048]{0:T(1024)(128)(4,1)S(1)} %copy-done.15, f32[1,128,2048]{2,1,0:T(8,128)S(1)} %convolution_bitcast_fusion.1, f32[1,128,2048]{2,1,0:T(8,128)S(1)} %convolution_bitcast_fusion.2, ...), kind=kOutput, calls=%fused_computation.21 | convolution fusion | flops 12896436224 | bytes 31460352 | tf_op jit(solution)/shard_map/bsi,bsj->bij/dot_general | solution.py:40
  1751.4 9.2 copy.142
  (206 shorter events, 107.4 us)
Async XLA Ops:
  7.2 295.8 %all-reduce.7.cloned.1.call-start = ((), (), s32[]{:S(2)}) async-start(), calls=%async_computation | async-start | bytes 16777216 | tf_op jit(solution)/shard_map/psum | solution.py:12
  33.0 670.1 %all-reduce.9.cloned.1.call-start = ((), (), s32[]{:S(2)}) async-start(), calls=%async_computation.1 | async-start | bytes 12582912 | tf_op jit(solution)/shard_map/psum | solution.py:12
  303.0 1.6 slice-start.4
  309.1 44.0 %copy-start.6 = (f32[2,512,512]{2,1,0:T(8,128)}, f32[2,512,512]{2,1,0:T(8,128)S(1)}, u32[]{:S(2)}) copy-start(f32[2,512,512]{2,1,0:T(8,128)S(1)} %fusion.60) | copy-start | bytes 6291460
  353.9 0.8 copy-start.10
  563.3 5.8 copy-start.11
  573.7 6.6 copy-start.4
  579.3 1.0 copy-start.2
  583.3 870.0 %all-reduce.11.cloned.1.call-start = ((), (), s32[]{:S(2)}) async-start(), calls=%async_computation.2 | async-start | bytes 8388608 | tf_op jit(solution)/shard_map/psum | solution.py:12
  583.4 0.6 copy-start.16
  584.0 232.7 %copy-start.14 = (pred[2048]{0:T(1024)(128)(4,1)}, pred[2048]{0:T(1024)(128)(4,1)S(1)}, u32[]{:S(2)}) copy-start(pred[2048]{0:T(1024)(128)(4,1)S(1)} %add_compare_fusion) | copy-start | bytes 6148
  590.5 4.9 copy-start.8
  591.9 4.6 copy-start.7
  712.8 79.1 %copy-start.5 = (f32[2,512,512]{2,1,0:T(8,128)}, f32[2,512,512]{2,1,0:T(8,128)S(1)}, u32[]{:S(2)}) copy-start(f32[2,512,512]{2,1,0:T(8,128)S(1)} %get-tuple-element.301) | copy-start | bytes 6291460
  712.8 86.2 %copy-start.12 = (s32[4,2]{0,1:T(2,128)}, s32[4,2]{0,1:T(2,128)S(1)}, u32[]{:S(2)}) copy-start(s32[4,2]{0,1:T(2,128)S(1)} %get-tuple-element.306) | copy-start | bytes 100
  799.1 8.8 slice-start.2
  801.1 6.9 copy-start
  801.1 6.9 slice-start.3
  807.9 5.5 copy-start.1
  855.4 10.4 copy-start.18
  863.3 185.5 %collective-permute-start = (f32[2,2048,512]{1,2,0:T(8,128)}, f32[2,2048,512]{1,2,0:T(8,128)}, u32[]{:S(2)}, u32[]{:S(2)}) collective-permute-start(f32[2,2048,512]{1,2,0:T(8,128)} %slice.400), channel_id=1, source_target_pairs={{1,0},{2,1},{3,2},{4,3},{5,4},{6,5},{7,6},{9,8},{10,9},{11,10},{12... | collective-permute-start | bytes 25165832 | tf_op jit(solution)/shard_map/ppermute | solution.py:18
  1159.4 48.2 %collective-permute-start.1 = (f32[2,512,1024]{2,1,0:T(8,128)}, f32[2,512,1024]{2,1,0:T(8,128)}, u32[]{:S(2)}, u32[]{:S(2)}) collective-permute-start(f32[2,512,1024]{2,1,0:T(8,128)} %slice.401), channel_id=1, source_target_pairs={{8,0},{16,8},{24,16},{9,1},{17,9},{25,17},{10,2},{18,10},{26,18},{... | collective-permute-start | bytes 12582920 | tf_op jit(solution)/shard_map/ppermute | solution.py:18
  1298.2 373.7 %all-reduce.13.cloned.1.call-start = ((), (), s32[]{:S(2)}) async-start(), calls=%async_computation.3 | async-start | bytes 6291456 | tf_op jit(solution)/shard_map/psum | solution.py:12
  1478.7 62.7 %copy-start.13 = (s32[4,2]{0,1:T(2,128)S(1)}, s32[4,2]{0,1:T(2,128)}, u32[]{:S(2)}) copy-start(s32[4,2]{0,1:T(2,128)} %copy-done.12) | copy-start | bytes 100
  1549.6 43.7 %copy-start.9 = (f32[1,512,512]{2,1,0:T(8,128)}, f32[1,512,512]{2,1,0:T(8,128)S(1)}, u32[]{:S(2)}) copy-start(f32[1,512,512]{2,1,0:T(8,128)S(1)} %get-tuple-element.303) | copy-start | bytes 3145732
  1722.8 3.5 copy-start.3
  1725.2 6.5 slice-start
  1727.6 4.2 slice-start.1
  1728.7 3.1 copy-start.15
  1728.7 3.1 copy-start.17
Sparse Core Ops, SparseCore 0:
  33.1 269.8 all-reduce.6
  583.5 119.6 all-reduce.8
  1298.3 155.0 all-reduce.10
  1603.4 68.3 all-reduce.12
where the time goes:
time: 1780 us; the launch traced here: 1770 us
  waiting for transfers between devices  786 us (44%)
  other arithmetic  551 us (31%)
  local copies, waits for them, and re-layouts  221 us (12%)
  matrix products  187 us (11%)
  between operations  17.8 us (1%)
    psum x4, waiting for transfers between devices, broadcast(): return lax.psum(kept, axis)  567 us
    another operation x10, other arithmetic, solve_lower(): return jax.scipy.linalg.solve_triangular(factor_mat, right_side, lower=True)  243 us
    another operation x31, other arithmetic, partial_factor(): lower_factor = jax.vmap(jnp.linalg.cholesky)(pivot_block)  234 us
    ppermute x2, waiting for transfers between devices, from_behind(): lax.ppermute(value, axis, [(source, source + steps) for source in range(f...  219 us
    unnamed x63, local copies, waits for them, and re-layouts  73.2 us
    another operation x28, matrix products, solve_lower(): return jax.scipy.linalg.solve_triangular(factor_mat, right_side, lower=True)  64 us
    dot_general x2, matrix products, partial_factor(): jnp.einsum('bsi,bsj->bij', left_rows, factor_all, precision=lax.Precision...  58.2 us
    dot_general x1, matrix products, extend_add(): jnp.einsum('bxky,bkq->bxqy', widened, col_select, precision=lax.Precision...  35.9 us
  transfers between devices with their start and end apart: 6, of which 6 were waited for; matrix products, arithmetic and copies ran while one was open for 3% of the time, Pallas kernels for 0%

commit v1 on v0

v1 whole, which is shorter than its diff:
```python
import jax
import jax.numpy as jnp
from jax import lax
from jax.experimental import pallas as pl
from jax.experimental.pallas import tpu as pltpu
from jax.sharding import PartitionSpec as P

SEP = 512
BLK = 256
GAP = SEP // BLK
DB = 128
SUB = 8
VMEM = 56 * 2**20
F32 = jnp.float32
BF16 = jnp.bfloat16


def split(value):
    high = value.astype(BF16)
    return high, (value - high.astype(F32)).astype(BF16)


def dot(a, b, dims=((1,), (0,)), precision=None):
    return lax.dot_general(a, b, (dims, ((), ())), precision=precision, preferred_element_type=F32)


def dot3(a, b, dims=((1,), (0,))):
    return dot(a[0], b[0], dims) + (dot(a[0], b[1], dims) + dot(a[1], b[0], dims))


def dot_full(a, b, dims=((1,), (0,))):
    return dot(a, b, dims, lax.Precision.HIGHEST)


def factor_diag(tiles):
    shape = tiles[0][0].shape
    sub_iota = lax.broadcasted_iota(jnp.int32, shape, 1)
    left = [tile[0] for tile in tiles]
    right = [tile[1] for tile in tiles]
    done = []

    def row(tile, k):
        return jnp.broadcast_to(tile[:, k : k + 1, :], shape)

    for t in range(len(tiles)):
        first = t * SUB

        def lanes(tile, k, first=first):
            return jnp.broadcast_to(tile[:, :, first + k : first + k + 1], shape)

        cols = [lanes(left[t], k) for k in range(SUB)]
        a = [[row(cols[k], i) for k in range(i + 1)] for i in range(SUB)]
        inv = [None] * SUB
        low = [[None] * SUB for _ in range(SUB)]
        for j in range(SUB):
            inv[j] = lax.rsqrt(a[j][j])
            for i in range(j + 1, SUB):
                low[i][j] = a[i][j] * inv[j]
            for i in range(j + 1, SUB):
                for k in range(j + 1, i + 1):
                    a[i][k] = a[i][k] - low[i][j] * low[k][j]
        m = [[None] * SUB for _ in range(SUB)]
        for j in range(SUB):
            m[j][j] = inv[j]
            for i in range(j + 1, SUB):
                total = low[i][j] * m[j][j]
                for k in range(j + 1, i):
                    total = total + low[i][k] * m[k][j]
                m[i][j] = -inv[i] * total
        mcol = []
        for k in range(SUB):
            vec = jnp.zeros(shape, F32)
            for i in range(k, SUB):
                vec = jnp.where(sub_iota == i, m[i][k], vec)
            mcol.append(vec)
        new_left = mcol[0] * row(left[t], 0)
        new_right = mcol[0] * row(right[t], 0)
        for k in range(1, SUB):
            new_left = new_left + mcol[k] * row(left[t], k)
            new_right = new_right + mcol[k] * row(right[t], k)
        done.append(new_right)
        rows_left = [row(new_left, i) for i in range(SUB)]
        rows_right = [row(new_right, i) for i in range(SUB)]
        for s in range(t + 1, len(tiles)):
            raw = [lanes(left[s], k) for k in range(SUB)]
            for i in range(SUB):
                g = m[i][0] * raw[0]
                for k in range(1, i + 1):
                    g = g + m[i][k] * raw[k]
                left[s] = left[s] - g * rows_left[i]
                right[s] = right[s] - g * rows_right[i]
    return done


def chol_steps(work, diag, inv_ref, invt_ref):
    count = work.shape[0]
    steps = SEP // DB
    eye = (
        lax.broadcasted_iota(jnp.int32, (DB, DB), 0) == lax.broadcasted_iota(jnp.int32, (DB, DB), 1)
    ).astype(F32)
    for b in range(count):
        for k in range(steps):
            for j in range(steps):
                work[b, pl.ds(k * DB, DB), pl.ds(SEP + j * DB, DB)] = eye if j == k else jnp.zeros((DB, DB), F32)

    def step(k, carry):
        rows = pl.ds(pl.multiple_of(k * DB, DB), DB)
        for b in range(count):
            diag[b] = work[b, rows, rows]
        tiles = []
        for t in range(DB // SUB):
            unit = jnp.broadcast_to(eye[t * SUB : (t + 1) * SUB, :][None], (count, SUB, DB))
            tiles.append((diag[:, pl.ds(t * SUB, SUB), :], unit))
        outs = factor_diag(tiles)
        for t in range(DB // SUB):
            diag[:, pl.ds(t * SUB, SUB), :] = outs[t]
        for b in range(count):
            work[b, rows, :] = dot_full(diag[b], work[b, rows, :])

        def update(i, c):
            irows = pl.ds(pl.multiple_of(i * DB, DB), DB)
            for b in range(count):
                work[b, irows, :] = work[b, irows, :] - dot_full(work[b, rows, irows], work[b, rows, :], ((0,), (0,)))
            return c

        lax.fori_loop(k + 1, steps, update, 0)
        return carry

    lax.fori_loop(0, steps, step, 0)
    for b in range(count):
        inv = work[b, :, pl.ds(SEP, SEP)]
        inv_ref[b] = inv
        invt_ref[b] = inv.T


def call(kernel, grid, in_specs, out_shape, out_specs, scratch, args, flops, nbytes, aliases=None):
    return pl.pallas_call(
        kernel,
        out_shape=out_shape,
        grid_spec=pltpu.PrefetchScalarGridSpec(
            num_scalar_prefetch=1, grid=grid, in_specs=in_specs, out_specs=out_specs, scratch_shapes=scratch
        ),
        input_output_aliases=aliases or {},
        compiler_params=pltpu.CompilerParams(vmem_limit_bytes=VMEM),
        cost_estimate=pl.CostEstimate(flops=int(flops), bytes_accessed=int(nbytes), transcendentals=0),
    )(*args)


def shape_of(dims, dtype=F32):
    return jax.ShapeDtypeStruct(dims, dtype)


class Plan:
    def __init__(self, rows, cols, rows_loc, cols_loc):
        self.rows, self.cols, self.rows_loc, self.cols_loc = rows, cols, rows_loc, cols_loc
        self.row_blocks, self.col_blocks = rows_loc // BLK, cols_loc // BLK
        self.blocks = rows * rows_loc // BLK
        self.half = cols_loc // SEP
        assert cols == 2 * rows and rows_loc == 2 * cols_loc and rows_loc >= 2 * SEP and cols_loc >= SEP

    def r(self, s):
        return s[2 * self.blocks]

    def c(self, s):
        return s[2 * self.blocks + 1]

    def source(self, s, k, block):
        return s[k * self.blocks + block]

    def row_at(self, s, k, i):
        found = self.source(s, k, self.r(s) * self.row_blocks + i)
        return found >= 0, jnp.where(found >= 0, found - self.r(s) * self.row_blocks, 0)

    def col_at(self, s, k, j):
        found = self.source(s, k, self.c(s) * self.col_blocks + j)
        return found >= 0, jnp.where(found >= 0, found - self.c(s) * self.col_blocks, 0)

    def before_at(self, s, k, j):
        start = self.c(s) * self.col_blocks
        found = self.source(s, k, jnp.maximum(start - GAP + j, 0)) - start
        valid = (found >= 0) & (start > 0)
        return valid, jnp.where(valid, found, 0)


def child_factor(plan, scal, head_a, head_b):
    def kernel(s, a_ref, b_ref, inv_ref, invt_ref, work, diag):
        work[0, :, pl.ds(0, SEP)] = a_ref[...]
        work[1, :, pl.ds(0, SEP)] = b_ref[...]
        chol_steps(work, diag, inv_ref, invt_ref)

    block = pl.BlockSpec((SEP, SEP), lambda g, s: (0, 0))
    out = pl.BlockSpec((2, SEP, SEP), lambda g, s: (0, 0, 0))
    return call(
        kernel, (1,), [block, block], [shape_of((2, SEP, SEP))] * 2, [out, out],
        [pltpu.VMEM((2, SEP, 2 * SEP), F32), pltpu.VMEM((2, DB, DB), F32)],
        (scal, head_a, head_b), 3e10, 6 * 2**20,
    )


def parent_factor(plan, scal, pivot, rt, cols):
    def kernel(s, p_ref, ah, al, bh, bl, cah, cal, cbh, cbl, inv_ref, invt_ref, work, diag):
        total = p_ref[...]
        for k, (lh, ll, rh, rl) in enumerate(((ah, al, cah, cal), (bh, bl, cbh, cbl))):
            update = dot3((lh[...], ll[...]), (rh[...], rl[...]))
            keep = plan.source(s, k, 1) >= 0
            edge = lax.broadcasted_iota(jnp.int32, (SEP, SEP), 0) >= BLK
            edge = edge | (lax.broadcasted_iota(jnp.int32, (SEP, SEP), 1) >= BLK)
            total = total - jnp.where(edge & jnp.logical_not(keep), 0.0, update)
        work[0, :, pl.ds(0, SEP)] = total
        chol_steps(work, diag, inv_ref, invt_ref)

    pivot_spec = pl.BlockSpec((SEP, SEP), lambda g, s: (0, 0))
    left = pl.BlockSpec((SEP, SEP), lambda g, s: (2 * plan.half + 1, 0))
    right = pl.BlockSpec((SEP, SEP), lambda g, s: (0, plan.half + 1))
    out = pl.BlockSpec((1, SEP, SEP), lambda g, s: (0, 0, 0))
    return call(
        kernel, (1,), [pivot_spec] + [left] * 4 + [right] * 4, [shape_of((1, SEP, SEP))] * 2, [out, out],
        [pltpu.VMEM((1, SEP, 2 * SEP), F32), pltpu.VMEM((1, DB, DB), F32)],
        (scal, pivot, *rt[0], *rt[1], *cols[0], *cols[1]), 2.5e10, 6 * 2**20,
    )


def child_rows(plan, scal, k, own, other, after, head, invt):
    half = plan.half
    jobs = 2 * half + 2

    def kernel(s, o_ref, e_ref, x_ref, h_ref, l_ref, hi_ref, lo_ref, lh, ll):
        j = pl.program_id(0)

        @pl.when(j == 0)
        def _():
            lh[...], ll[...] = split(l_ref[0])

        side = j // half
        parity = plan.c(s) % 2
        value = jnp.where(side == parity, o_ref[...], e_ref[...])
        value = jnp.where(j == 2 * half, x_ref[...], jnp.where(j == 2 * half + 1, h_ref[...], value))
        hi_ref[...], lo_ref[...] = split(dot3(split(value), (lh[...], ll[...])))

    def own_at(j, s):
        return (jnp.clip(j - half * (plan.c(s) % 2), 0, half - 1), 0)

    def other_at(j, s):
        return (jnp.clip(j - half * (1 - plan.c(s) % 2), 0, half - 1), 0)

    blk = (SEP, SEP)
    out = pl.BlockSpec(blk, lambda j, s: (j, 0))
    return call(
        kernel, (jobs,),
        [pl.BlockSpec(blk, own_at), pl.BlockSpec(blk, other_at), pl.BlockSpec(blk, lambda j, s: (0, 0)),
         pl.BlockSpec(blk, lambda j, s: (1, 0)), pl.BlockSpec((1, SEP, SEP), lambda j, s: (k, 0, 0))],
        [shape_of((jobs * SEP, SEP), BF16)] * 2, [out, out], [pltpu.VMEM(blk, BF16)] * 2,
        (scal, own, other, after, head, invt), 6 * jobs * SEP**3, 8 * jobs * SEP**2,
    )


def child_cols(plan, scal, k, own, after, head, inv):
    half = plan.half
    jobs = half + 2

    def kernel(s, o_ref, x_ref, h_ref, l_ref, hi_ref, lo_ref, lh, ll):
        j = pl.program_id(0)

        @pl.when(j == 0)
        def _():
            lh[...], ll[...] = split(l_ref[0])

        @pl.when(j <= half)
        def _():
            value = jnp.where(j == half, x_ref[...], o_ref[...])
            hi_ref[...], lo_ref[...] = split(dot3((lh[...], ll[...]), split(value)))

        @pl.when(j == half + 1)
        def _():
            hi_ref[...], lo_ref[...] = split(dot3((lh[...], ll[...]), split(h_ref[...]), ((1,), (1,))))

    blk = (SEP, SEP)
    out = pl.BlockSpec(blk, lambda j, s: (0, j))
    return call(
        kernel, (jobs,),
        [pl.BlockSpec(blk, lambda j, s: (0, jnp.minimum(j, half - 1))), pl.BlockSpec(blk, lambda j, s: (0, 0)),
         pl.BlockSpec(blk, lambda j, s: (1, 0)), pl.BlockSpec((1, SEP, SEP), lambda j, s: (k, 0, 0))],
        [shape_of((SEP, jobs * SEP), BF16)] * 2, [out, out], [pltpu.VMEM(blk, BF16)] * 2,
        (scal, own, after, head, inv), 6 * jobs * SEP**3, 8 * jobs * SEP**2,
    )


def parent_rows(plan, scal, own, other, rt, cols, invt):
    count = plan.row_blocks
    in_half = count // 2

    def kernel(s, o_ref, e_ref, ah, al, bh, bl, cah, cal, cbh, cbl, l_ref, hi_ref, lo_ref, lh, ll, rh, rl):
        i = pl.program_id(0)

        @pl.when(i == 0)
        def _():
            lh[...], ll[...] = split(l_ref[0])
            for k, (high, low) in enumerate(((cah, cal), (cbh, cbl))):
                keep = plan.source(s, k, 1) >= 0
                lane = lax.broadcasted_iota(jnp.int32, (SEP, SEP), 1)
                drop = (lane >= BLK) & jnp.logical_not(keep)
                rh[k] = jnp.where(drop, 0.0, high[...].astype(F32)).astype(BF16)
                rl[k] = jnp.where(drop, 0.0, low[...].astype(F32)).astype(BF16)

        side = i // in_half
        value = jnp.where(side == plan.c(s) % 2, o_ref[...], e_ref[...])
        for k, (high, low) in enumerate(((ah, al), (bh, bl))):
            valid, _ = plan.row_at(s, k, i)
            value = value - jnp.where(valid, dot3((high[...], low[...]), (rh[k], rl[k])), 0.0)
        hi_ref[...], lo_ref[...] = split(dot3(split(value), (lh[...], ll[...])))

    def own_at(i, s):
        return (jnp.clip(i - in_half * (plan.c(s) % 2), 0, in_half - 1), 0)

    def other_at(i, s):
        return (jnp.clip(i - in_half * (1 - plan.c(s) % 2), 0, in_half - 1), 0)

    blk = (BLK, SEP)
    rows = [pl.BlockSpec(blk, lambda i, s, k=k: (plan.row_at(s, k, i)[1], 0)) for k in (0, 0, 1, 1)]
    head = pl.BlockSpec((SEP, SEP), lambda i, s: (0, plan.half + 1))
    out = pl.BlockSpec(blk, lambda i, s: (i, 0))
    return call(
        kernel, (count,),
        [pl.BlockSpec(blk, own_at), pl.BlockSpec(blk, other_at)] + rows + [head] * 4
        + [pl.BlockSpec((1, SEP, SEP), lambda i, s: (0, 0, 0))],
        [shape_of((plan.rows_loc, SEP), BF16)] * 2, [out, out],
        [pltpu.VMEM((SEP, SEP), BF16)] * 2 + [pltpu.VMEM((2, SEP, SEP), BF16)] * 2,
        (scal, own, other, *rt[0], *rt[1], *cols[0], *cols[1], invt),
        18 * plan.rows_loc * SEP**2, 16 * plan.rows_loc * SEP,
    )


def parent_cols(plan, scal, panel, rt, cols, inv):
    count = plan.col_blocks

    def kernel(s, p_ref, ah, al, bh, bl, cah, cal, cbh, cbl, l_ref, hi_ref, lo_ref, lh, ll, rh, rl):
        j = pl.program_id(0)

        @pl.when(j == 0)
        def _():
            lh[...], ll[...] = split(l_ref[0])
            for k, (high, low) in enumerate(((ah, al), (bh, bl))):
                keep = plan.source(s, k, 1) >= 0
                line = lax.broadcasted_iota(jnp.int32, (SEP, SEP), 0)
                drop = (line >= BLK) & jnp.logical_not(keep)
                rh[k] = jnp.where(drop, 0.0, high[...].astype(F32)).astype(BF16)
                rl[k] = jnp.where(drop, 0.0, low[...].astype(F32)).astype(BF16)

        value = p_ref[...]
        for k, (high, low) in enumerate(((cah, cal), (cbh, cbl))):
            valid, _ = plan.col_at(s, k, j)
            value = value - jnp.where(valid, dot3((rh[k], rl[k]), (high[...], low[...])), 0.0)
        hi_ref[...], lo_ref[...] = split(dot3((lh[...], ll[...]), split(value)))

    blk = (SEP, BLK)
    head = pl.BlockSpec((SEP, SEP), lambda j, s: (2 * plan.half + 1, 0))
    right = [pl.BlockSpec(blk, lambda j, s, k=k: (0, plan.col_at(s, k, j)[1])) for k in (0, 0, 1, 1)]
    out = pl.BlockSpec(blk, lambda j, s: (0, j))
    return call(
        kernel, (count,),
        [out] + [head] * 4 + right + [pl.BlockSpec((1, SEP, SEP), lambda j, s: (0, 0, 0))],
        [shape_of((SEP, plan.cols_loc), BF16)] * 2, [out, out],
        [pltpu.VMEM((SEP, SEP), BF16)] * 2 + [pltpu.VMEM((2, SEP, SEP), BF16)] * 2,
        (scal, panel, *rt[0], *rt[1], *cols[0], *cols[1], inv),
        18 * plan.cols_loc * SEP**2, 16 * plan.cols_loc * SEP,
    )


def child_result(plan, scal, k, fronts, rt, cols, result):
    wide = plan.cols_loc

    def kernel(s, a_ref, lh, ll, rh, rl, *rest):
        out_ref = rest[-1]
        i = pl.program_id(0)
        top = (plan.r(s) == 0) & (i < GAP)

        @pl.when(top)
        def _():
            rows = pl.ds(pl.multiple_of(jnp.minimum(i, GAP - 1) * BLK, BLK), BLK)
            out_ref[0] = rh[rows, :].astype(F32) + rl[rows, :].astype(F32)

        @pl.when(jnp.logical_not(top))
        def _():
            out_ref[0] = a_ref[0] - dot3((lh[...], ll[...]), (rh[...], rl[...]))

            @pl.when(plan.c(s) == 0)
            def _():
                out_ref[0, :, pl.ds(0, SEP)] = jnp.zeros((BLK, SEP), F32)

    block = pl.BlockSpec((1, BLK, wide), lambda i, s: (k, i, 0))
    left = pl.BlockSpec((BLK, SEP), lambda i, s: (i, 0))
    right = pl.BlockSpec((SEP, wide), lambda i, s: (0, 0))
    extra_specs = [] if result is None else [pl.BlockSpec(memory_space=pl.ANY)]
    extra = [] if result is None else [result]
    return call(
        kernel, (plan.row_blocks,), [block, left, left, right, right] + extra_specs,
        shape_of(fronts.shape), block, [], (scal, fronts, *rt, *cols, *extra),
        6 * plan.rows_loc * wide * SEP, 8 * plan.rows_loc * wide,
        aliases={} if result is None else {6: 0},
    )


def edge_sum(plan, scal, fronts, after, first, count):
    last = plan.row_blocks - 1
    inner = after is None

    def kernel(s, a_ref, b_ref, *rest):
        out_ref = rest[-1]
        i = pl.program_id(0) + first
        for j in range(GAP):
            total = jnp.zeros((BLK, BLK), F32)
            for k, ref in enumerate((a_ref, b_ref)):
                valid_row, at_row = plan.row_at(s, k, i)
                valid_col, at_col = plan.before_at(s, k, j)
                lanes = pl.ds(pl.multiple_of(at_col * BLK, BLK), BLK)
                value = ref[0, :, lanes]
                if not inner:
                    value = jnp.where(at_row > last, rest[k][0, :, lanes], value)
                total = total + jnp.where(valid_row & valid_col, value, 0.0)
            out_ref[:, pl.ds(j * BLK, BLK)] = total

    blk = (1, BLK, SEP)
    own = [pl.BlockSpec(blk, lambda g, s, k=k: (k, jnp.minimum(plan.row_at(s, k, g + first)[1], last), 0)) for k in (0, 1)]
    ext = [
        pl.BlockSpec(blk, lambda g, s, k=k: (k, jnp.clip(plan.row_at(s, k, g + first)[1] - last - 1, 0, GAP - 1), 0))
        for k in (0, 1)
    ]
    return call(
        kernel, (count,), own + ([] if inner else ext), shape_of((count * BLK, SEP)),
        pl.BlockSpec((BLK, SEP), lambda g, s: (g, 0)), [],
        (scal, fronts, fronts) + (() if inner else (after, after)), 1e6, 16 * count * BLK * SEP,
    )


def add_entries(plan, s, i, total_ref, refs, ext_refs, edge_ref, out_wide):
    last = plan.row_blocks - 1
    for k in (0, 1):
        valid_row, at_row = plan.row_at(s, k, i)
        for j in range(plan.col_blocks):
            valid_col, at_col = plan.col_at(s, k, j)
            here = valid_row & valid_col & (at_col < plan.col_blocks)

            @pl.when(here)
            def _(k=k, j=j, at_col=at_col, at_row=at_row):
                lanes = pl.ds(pl.multiple_of(at_col * BLK, BLK), BLK)
                value = refs[k][0, :, lanes]
                if ext_refs is not None:
                    value = jnp.where(at_row > last, ext_refs[k][0, :, lanes], value)
                total_ref[:, pl.ds(j * BLK, BLK)] += value

    @pl.when(plan.c(s) < plan.cols - 1)
    def _():
        total_ref[:, pl.ds(out_wide - SEP, SEP)] += edge_ref[...]


def panel_start(plan, scal, entries, fronts, edge):
    wide = plan.cols_loc

    def kernel(s, e_ref, a_ref, b_ref, x_ref, out_ref):
        out_ref[...] = e_ref[...]
        add_entries(plan, s, pl.program_id(0), out_ref, (a_ref, b_ref), None, x_ref, wide)

    blk = (BLK, wide)
    own = [
        pl.BlockSpec((1, BLK, wide), lambda g, s, k=k: (k, plan.row_at(s, k, g)[1], 0)) for k in (0, 1)
    ]
    here = pl.BlockSpec(blk, lambda g, s: (g, 0))
    return call(
        kernel, (GAP,), [here] + own + [pl.BlockSpec((BLK, SEP), lambda g, s: (g, 0))],
        shape_of((SEP, wide)), here, [], (scal, entries, fronts, fronts, edge), 1e6, 16 * SEP * wide,
    )


def parent_result(plan, scal, entries, fronts, after, edge_top, edge_rest, rt, cols, prt, pcols):
    wide = plan.cols_loc
    last = plan.row_blocks - 1
    lhs_blk = (BLK, SEP)

    def kernel(s, e_ref, a_ref, b_ref, xa_ref, xb_ref, t_ref, u_ref, ah, al, bh, bl, ph, pll, cah, cal, cbh, cbl,
               qh, ql, out_ref, rh, rl, edge):
        i = pl.program_id(0)
        top = (plan.r(s) == 0) & (i < GAP)

        @pl.when(i == 0)
        def _():
            for k, (high, low) in enumerate(((cah, cal), (cbh, cbl))):
                for j in range(plan.col_blocks):
                    valid, at = plan.col_at(s, k, j)
                    lanes = pl.ds(pl.multiple_of(at * BLK, BLK), BLK)
                    here = pl.ds(j * BLK, BLK)
                    rh[k, :, here] = jnp.where(valid, high[:, lanes].astype(F32), 0.0).astype(BF16)
                    rl[k, :, here] = jnp.where(valid, low[:, lanes].astype(F32), 0.0).astype(BF16)

        @pl.when(top)
        def _():
            rows = pl.ds(pl.multiple_of(jnp.minimum(i, GAP - 1) * BLK, BLK), BLK)
            out_ref[...] = qh[rows, :].astype(F32) + ql[rows, :].astype(F32)

        @pl.when(jnp.logical_not(top))
        def _():
            out_ref[...] = e_ref[...] - dot3((ph[...], pll[...]), (qh[...], ql[...]))
            for k, (high, low) in enumerate(((ah, al), (bh, bl))):
                valid, _ = plan.row_at(s, k, i)

                @pl.when(valid)
                def _(k=k, high=high, low=low):
                    out_ref[...] -= dot3((high[...], low[...]), (rh[k], rl[k]))

            edge[...] = jnp.where(i < GAP, t_ref[...], u_ref[...])
            add_entries(plan, s, i, out_ref, (a_ref, b_ref), (xa_ref, xb_ref), edge, wide)

            @pl.when(plan.c(s) == 0)
            def _():
                out_ref[:, pl.ds(0, SEP)] = jnp.zeros((BLK, SEP), F32)

    here = pl.BlockSpec((BLK, wide), lambda g, s: (g, 0))
    front = (1, BLK, wide)
    own = [pl.BlockSpec(front, lambda g, s, k=k: (k, jnp.minimum(plan.row_at(s, k, g)[1], last), 0)) for k in (0, 1)]
    ext = [
        pl.BlockSpec(front, lambda g, s, k=k: (k, jnp.clip(plan.row_at(s, k, g)[1] - last - 1, 0, GAP - 1), 0))
        for k in (0, 1)
    ]
    top_spec = pl.BlockSpec(lhs_blk, lambda g, s: (jnp.minimum(g, GAP - 1), 0))
    rest_spec = pl.BlockSpec(lhs_blk, lambda g, s: (jnp.maximum(g - GAP, 0), 0))
    rows = [pl.BlockSpec(lhs_blk, lambda g, s, k=k: (plan.row_at(s, k, g)[1], 0)) for k in (0, 0, 1, 1)]
    prow = pl.BlockSpec(lhs_blk, lambda g, s: (g, 0))
    right = pl.BlockSpec((SEP, wide + SEP), lambda g, s: (0, 0))
    pright = pl.BlockSpec((SEP, wide), lambda g, s: (0, 0))
    return call(
        kernel, (plan.row_blocks,),
        [here] + own + ext + [top_spec, rest_spec] + rows + [prow] * 2 + [right] * 4 + [pright] * 2,
        shape_of((plan.rows_loc, wide)), here,
        [pltpu.VMEM((2, SEP, wide), BF16)] * 2 + [pltpu.VMEM(lhs_blk, F32)],
        (scal, entries, fronts, fronts, after, after, edge_top, edge_rest, *rt[0], *rt[1], *prt, *cols[0], *cols[1], *pcols),
        18 * plan.rows_loc * wide * SEP, 24 * plan.rows_loc * wide,
    )


def send(plan, value, pairs):
    flat = [(a * plan.cols + b, c * plan.cols + d) for (a, b), (c, d) in pairs]
    return lax.ppermute(value, ("row", "col"), flat)


def grid_of(plan):
    return [(a, b) for a in range(plan.rows) for b in range(plan.cols)]


def row_broadcast(plan, r, value):
    stride = plan.rows // 2
    while stride:
        sent = send(plan, value, [((a, b), (a + stride, b)) for a, b in grid_of(plan) if a % (2 * stride) == 0])
        value = jnp.where(r % (2 * stride) == stride, sent, value)
        stride //= 2
    return value


def from_next_row(plan, value):
    return send(plan, value, [((a + 1, b), (a, b)) for a, b in grid_of(plan) if a + 1 < plan.rows])


def from_next_col(plan, value):
    return send(plan, value, [((a, b + 1), (a, b)) for a, b in grid_of(plan) if b + 1 < plan.cols])


def swap_cols(plan, value):
    return send(plan, value, [((a, b), (a, b ^ 1)) for a, b in grid_of(plan)])


def swap_rows(plan, value):
    return send(plan, value, [((a, b), (a ^ 1, b)) for a, b in grid_of(plan)])


def spread(plan, r, c, value):
    place = c // 2
    up = send(plan, value, [((a, b), (a, b + 2)) for a, b in grid_of(plan) if b // 2 == a and b + 2 < plan.cols])
    down = send(plan, value, [((a, b), (a, b - 2)) for a, b in grid_of(plan) if b // 2 == a and b >= 2])
    now = jnp.where(place > r, up, down)
    out = jnp.where(place == r, value, now)
    for step in range(2, plan.rows):
        pairs = []
        for a, b in grid_of(plan):
            if b // 2 == a + step - 1 and b + 2 < plan.cols:
                pairs.append(((a, b), (a, b + 2)))
            if b // 2 == a - step + 1 and b >= 2:
                pairs.append(((a, b), (a, b - 2)))
        now = send(plan, now, pairs)
        out = jnp.where(jnp.abs(place - r) == step, now, out)
    return out


def lead(plan, c, own, other, count):
    if count <= plan.cols_loc:
        return jnp.where(c % 2 == 0, own[:count], other[:count])
    return jnp.where(c % 2 == 0, jnp.concatenate([own, other]), jnp.concatenate([other, own]))[:count]


def local(plan, child_fronts, parent_entries, block_map):
    r, c = lax.axis_index("row"), lax.axis_index("col")
    slots = jnp.arange(block_map.shape[1], dtype=jnp.int32)[None, None, :] + GAP
    targets = jnp.arange(plan.blocks, dtype=jnp.int32)[None, :, None]
    source = jnp.max(jnp.where(block_map[:, None, :] == targets, slots, -1), axis=2)
    scal = jnp.concatenate([source.reshape(-1), jnp.stack([r, c]).astype(jnp.int32)])

    edge_top = from_next_col(plan, edge_sum(plan, scal, child_fronts, None, 0, GAP))
    after_rows = from_next_row(plan, child_fronts[:, :SEP, :])

    panels, own, other, heads, next_rows = [], [], [], [], []
    for k in (0, 1):
        panel = row_broadcast(plan, r, child_fronts[k, :SEP, :])
        panels.append(panel)
        own.append(spread(plan, r, c, panel.T))
        other.append(swap_cols(plan, own[k]))
        heads.append(row_broadcast(plan, r, lead(plan, c, own[k], other[k], 2 * SEP)))
        next_rows.append(from_next_row(plan, lead(plan, c, own[k], other[k], SEP)))
    mine = from_next_col(plan, jnp.where(r % 2 == 0, panels[0][:, :SEP], panels[1][:, :SEP]))
    theirs = swap_rows(plan, mine)
    next_cols = [jnp.where(r % 2 == 0, mine, theirs), jnp.where(r % 2 == 0, theirs, mine)]

    panel = row_broadcast(plan, r, panel_start(plan, scal, parent_entries, child_fronts, edge_top))
    parent_own = spread(plan, r, c, panel.T)
    parent_other = swap_cols(plan, parent_own)
    pivot = row_broadcast(plan, r, lead(plan, c, parent_own, parent_other, SEP))

    edge_rest = from_next_col(
        plan, edge_sum(plan, scal, child_fronts, after_rows, GAP, plan.row_blocks - GAP)
    )

    inv, invt = child_factor(plan, scal, heads[0], heads[1])
    rt = [child_rows(plan, scal, k, own[k], other[k], next_rows[k], heads[k], invt) for k in (0, 1)]
    cols = [child_cols(plan, scal, k, panels[k], next_cols[k], heads[k], inv) for k in (0, 1)]
    result = child_result(plan, scal, 0, child_fronts, rt[0], cols[0], None)
    result = child_result(plan, scal, 1, child_fronts, rt[1], cols[1], result)

    pinv, pinvt = parent_factor(plan, scal, pivot, rt, cols)
    prt = parent_rows(plan, scal, parent_own, parent_other, rt, cols, pinvt)
    pcols = parent_cols(plan, scal, panel, rt, cols, pinv)
    parent = parent_result(
        plan, scal, parent_entries, child_fronts, after_rows, edge_top, edge_rest, rt, cols, prt, pcols
    )
    return (result, parent)


def solution(mesh):
    placed = (P(None, "row", "col"), P("row", "col"), P())

    def run(child_fronts, parent_entries, block_map):
        plan = Plan(mesh.shape["row"], mesh.shape["col"], child_fronts.shape[1], child_fronts.shape[2])
        return local(plan, child_fronts, parent_entries, block_map)

    return jax.shard_map(
        run,
        mesh=mesh,
        in_specs=placed,
        out_specs=(P(None, "row", "col"), P("row", "col")),
        check_vma=False,
    )
```

time: 1780 us -> 689 us (0.39)
  other arithmetic: 551 us -> 53.3 us
  waiting for transfers between devices: 786 us -> 290 us
  Pallas kernels: 0 us -> 232 us
  matrix products: 187 us -> 0 us
  local copies, waits for them, and re-layouts: 221 us -> 35.7 us
  starting transfers between devices: 4.7 us -> 66.4 us
    psum x4 -> x0, waiting for transfers between devices: 567 us -> none  [broadcast(): return lax.psum(kept, axis)]
    another operation x41 -> x0, other arithmetic: 477 us -> none  [the longest x10 243 us: solve_lower(): return jax.scipy.linalg.solve_triangular(factor_mat, right_side, lower=True)]
    pallas_call x0 -> x14, Pallas kernels: none -> 232 us  [call(): pl.pallas_call(kernel, out_shape=out_shape, grid_spec=pltpu.PrefetchScala...]
    dot_general x6 -> x0, matrix products: 114 us -> none  [the longest x2 58.2 us: partial_factor(): jnp.einsum('bsi,bsj->bij', left_rows, factor_all, precision=lax.Precision...]
    reshape x3 -> x1, local copies, waits for them, and re-layouts: 78.6 us -> 0.08 us  [local(): source.reshape(-1)]
    another operation x40 -> x0, matrix products: 72.3 us -> none  [the longest x28 64 us: solve_lower(): return jax.scipy.linalg.solve_triangular(factor_mat, right_side, lower=True)]
    unnamed x63 -> x29, local copies, waits for them, and re-layouts: 73.2 us -> 1.17 us
    ppermute x2 -> x34, waiting for transfers between devices: 219 us -> 290 us  [send(): return lax.ppermute(value, ('row', 'col'), flat)]
  transfers between devices with their start and end apart: 6 -> 34, of which waited for: 6 -> 11; matrix products, arithmetic and copies ran while one was open for 3% -> 12% of each run, Pallas kernels for 0% -> 29%
where the time goes in v1:
time: 689 us; the launch traced here: 679 us
  waiting for transfers between devices  290 us (42%)
  Pallas kernels  232 us (34%)
  starting transfers between devices  66.4 us (10%)
  other arithmetic  53.3 us (8%)
  local copies, waits for them, and re-layouts  35.7 us (5%)
    ppermute x34, waiting for transfers between devices, send(): return lax.ppermute(value, ('row', 'col'), flat)  290 us
    pallas_call x14, Pallas kernels, call(): pl.pallas_call(kernel, out_shape=out_shape, grid_spec=pltpu.PrefetchScala...  232 us
    ppermute x34, starting transfers between devices, send(): return lax.ppermute(value, ('row', 'col'), flat)  66.4 us
    select_n x11, other arithmetic, row_broadcast(): value = jnp.where(r % (2 * stride) == stride, sent, value)  25.5 us
  transfers between devices with their start and end apart: 34, of which 11 were waited for; matrix products, arithmetic and copies ran while one was open for 12% of the time, Pallas kernels for 29%

profile of v1, /device:TPU:14, one launch (start us, length us, event | category | flops | bytes accessed | tf_op | source)
XLA Modules:
  0.0 678.8 jit_solution(975820376201505062)
XLA Ops:
  0.6 4.8 slice_bitcast_fusion
  9.1 3.1 shard_map.57
  12.2 2.4 collective-permute-start.23
  14.6 26.3 %collective-permute-done.23.x_ref.t_ref = f32[512,512]{1,0:T(8,128)S(1)} collective-permute-done((f32[512,512]{1,0:T(8,128)}, f32[512,512]{1,0:T(8,128)S(1)}, u32[]{:S(2)}, u32[]{:S(2)}) %collective-permute-start.23) | collective-permute-done | bytes 1048608 | tf_op jit(solution)/shard_map/ppermute | solution.py:541
  42.0 5.2 shard_map.59
  48.6 7.6 %collective-permute-done = f32[512,1024]{1,0:T(8,128)} collective-permute-done((f32[512,1024]{1,0:T(8,128)}, f32[512,1024]{1,0:T(8,128)}, u32[]{:S(2)}, u32[]{:S(2)}) %collective-permute-start) | collective-permute-done | bytes 2097184 | tf_op jit(solution)/shard_map/ppermute | solution.py:541
  56.2 6.8 %broadcast_select_fusion.7 = (f32[512,1024]{1,0:T(8,128)}, f32[512,1024]{1,0:T(8,128)}) fusion(f32[512,1024]{1,0:T(8,128)} %collective-permute-done.10, pred[]{:T(512)S(6)} %eq.82, f32[2,2048,1024]{2,1,0:T(8,128)} %b_ref.7, f32[512,1024]{1,0:T(8,128)} %collective-permute-done), kind=kLoop, calls=%fused_computation.16 | loop fusion | flops 1048576 | bytes 12582913 | tf_op jit(solution)/shard_map/jit(_where)/select_n | solution.py:552
  63.0 2.6 collective-permute-start.11
  65.6 2.6 collective-permute-start.1
  68.3 10.4 %collective-permute-done.25 = f32[512,1024]{1,0:T(8,128)} collective-permute-done((f32[512,1024]{1,0:T(8,128)}, f32[512,1024]{1,0:T(8,128)}, u32[]{:S(2)}, u32[]{:S(2)}) %collective-permute-start.25) | collective-permute-done | bytes 2097184 | tf_op jit(solution)/shard_map/ppermute | solution.py:541
  78.6 3.3 broadcast_select_fusion.6
  82.0 2.6 collective-permute-start.26
  84.5 2.0 broadcast_select_fusion.10.o_ref
  87.8 2.0 collective-permute-start.12
  89.8 3.5 broadcast_select_fusion.11.o_ref
  94.6 2.0 collective-permute-start.2
  96.6 2.0 broadcast_select_fusion.9.p_ref
  99.9 24.9 %collective-permute-done.13 = f32[1024,512]{0,1:T(8,128)} collective-permute-done((f32[1024,512]{0,1:T(8,128)S(1)}, f32[1024,512]{0,1:T(8,128)}, u32[]{:S(2)}, u32[]{:S(2)}) %collective-permute-start.13) | collective-permute-done | bytes 2097184 | tf_op jit(solution)/shard_map/ppermute | solution.py:541
  125.6 2.0 broadcast_select_fusion.13
  127.6 2.6 collective-permute-start.14
  130.2 39.5 %collective-permute-done.3 = f32[1024,512]{0,1:T(8,128)} collective-permute-done((f32[1024,512]{0,1:T(8,128)}, f32[1024,512]{0,1:T(8,128)}, u32[]{:S(2)}, u32[]{:S(2)}) %collective-permute-start.3) | collective-permute-done | bytes 2097184 | tf_op jit(solution)/shard_map/ppermute | solution.py:541
  169.7 2.0 broadcast_select_fusion.14
  171.8 2.6 collective-permute-start.4
  174.3 40.2 %collective-permute-done.28 = f32[1024,512]{0,1:T(8,128)S(1)} collective-permute-done((f32[1024,512]{0,1:T(8,128)S(1)}, f32[1024,512]{0,1:T(8,128)S(1)}, u32[]{:S(2)}, u32[]{:S(2)}) %collective-permute-start.28) | collective-permute-done | bytes 2097184 | tf_op jit(solution)/shard_map/ppermute | solution.py:541
  215.0 2.6 collective-permute-start.29
  217.6 2.0 collective-permute-start.15
  219.7 2.0 collective-permute-start.5
  221.7 34.3 %collective-permute-done.29 = f32[1024,512]{0,1:T(8,128)} collective-permute-done((f32[1024,512]{0,1:T(8,128)S(1)}, f32[1024,512]{0,1:T(8,128)}, u32[]{:S(2)}, u32[]{:S(2)}) %collective-permute-start.29) | collective-permute-done | bytes 2097184 | tf_op jit(solution)/shard_map/ppermute | solution.py:541
  256.0 2.0 collective-permute-start.30
  258.0 3.2 select_select_fusion.1
  261.8 3.9 select_select_fusion.2
  267.1 4.8 slice.41
  273.9 3.2 select_select_fusion
  277.7 32.3 %collective-permute-done.16 = f32[1024,512]{0,1:T(8,128)} collective-permute-done((f32[1024,512]{0,1:T(8,128)S(1)}, f32[1024,512]{0,1:T(8,128)}, u32[]{:S(2)}, u32[]{:S(2)}) %collective-permute-start.16) | collective-permute-done | bytes 2097184 | tf_op jit(solution)/shard_map/ppermute | solution.py:541
  313.8 45.8 %collective-permute-done.6 = f32[1024,512]{0,1:T(8,128)} collective-permute-done((f32[1024,512]{0,1:T(8,128)}, f32[1024,512]{0,1:T(8,128)}, u32[]{:S(2)}, u32[]{:S(2)}) %collective-permute-start.6) | collective-permute-done | bytes 2097184 | tf_op jit(solution)/shard_map/ppermute | solution.py:541
  359.6 2.0 broadcast_select_fusion.1
  366.2 25.0 %collective-permute-done.19 = f32[512,512]{1,0:T(8,128)S(1)} collective-permute-done((f32[512,512]{1,0:T(8,128)S(1)}, f32[512,512]{1,0:T(8,128)S(1)}, u32[]{:S(2)}, u32[]{:S(2)}) %collective-permute-start.19) | collective-permute-done | bytes 1048608 | tf_op jit(solution)/shard_map/ppermute | solution.py:541
  391.2 2.4 slice_select_fusion.1
  396.9 3.2 collective-permute-start.18
  401.8 2.6 collective-permute-start.9
  404.4 2.8 slice_select_fusion.3
  407.2 3.4 collective-permute-done.32
  414.6 4.7 collective-permute-start.33
  419.3 6.9 %shard_map.58 = f32[1536,512]{1,0:T(8,128)} custom-call(s32[66]{0:T(128)} %pad_add_fusion.s, f32[2,2048,1024]{2,1,0:T(8,128)} %b_ref.7, f32[2,2048,1024]{2,1,0:T(8,128)} %b_ref.7, f32[2,512,1024]{2,1,0:T(8,128)} %collective-permute-done.22.rest_0_.rest_1_.xa_ref.xb_ref, f32[2,512,1024]{2,1,0:T(8,128)} %collective-permute-done.22.rest_0_.rest_1_.xa_ref.xb_ref), custom_call_target="tpu_custom_call" | custom-call | flops 1000000 | bytes 12582912 | tf_op jit(solution)/shard_map/pallas_call | solution.py:137
  429.8 3.1 copy.24.o_ref
  434.6 2.9 copy.30.e_ref
  437.5 3.1 copy.25.e_ref
  442.4 4.4 collective-permute-start.24
  446.8 2.5 copy.31.x_ref
  449.4 2.5 copy.26.x_ref
  453.5 2.0 broadcast_select_fusion.4
  455.5 2.0 copy.22.a_ref.h_ref
  457.5 2.0 broadcast_select_fusion.5
  461.3 45.4 %shard_map.50 = (f32[2,512,512]{2,1,0:T(8,128)}, f32[2,512,512]{2,1,0:T(8,128)}) custom-call(s32[66]{0:T(128)} %pad_add_fusion.s, f32[1024,512]{1,0:T(8,128)} %copy.22.a_ref.h_ref, f32[1024,512]{1,0:T(8,128)} %copy.27.b_ref.h_ref), custom_call_target="tpu_custom_call" | custom-call | flops 30000001024 | bytes 6291456 | tf_op jit(solution)/shard_map/pallas_call | solution.py:137
  506.7 8.2 %shard_map.54 = (bf16[512,2048]{1,0:T(8,128)(2,1)}, bf16[512,2048]{1,0:T(8,128)(2,1)}) custom-call(s32[66]{0:T(128)} %pad_add_fusion.s, f32[512,1024]{1,0:T(8,128)} %copy-done.1, f32[512,512]{1,0:T(8,128)} %get-tuple-element.38.x_ref, f32[1024,512]{1,0:T(8,128)} %copy.22.a_ref.h_ref, f32[2,512,512]{2,1,0:T(8,128)} %get-tuple-element.21.l_ref), custom_call_target="tpu_custom_call" | custom-call | flops 3221225472 | bytes 8388608 | tf_op jit(solution)/shard_map/pallas_call | solution.py:137
  514.9 8.5 %shard_map.52 = (bf16[512,2048]{1,0:T(8,128)(2,1)}, bf16[512,2048]{1,0:T(8,128)(2,1)}) custom-call(s32[66]{0:T(128)} %pad_add_fusion.s, f32[512,1024]{1,0:T(8,128)} %broadcast_select_fusion.11.o_ref, f32[512,512]{1,0:T(8,128)} %get-tuple-element.39.x_ref, f32[1024,512]{1,0:T(8,128)} %copy.27.b_ref.h_ref, f32[2,512,512]{2,1,0:T(8,128)} %get-tuple-element.21.l_ref), custom_call_target="tpu_custom_call" | custom-call | flops 3221225472 | bytes 8388608 | tf_op jit(solution)/shard_map/pallas_call | solution.py:137
  523.4 11.1 %shard_map.53 = (bf16[3072,512]{1,0:T(8,128)(2,1)}, bf16[3072,512]{1,0:T(8,128)(2,1)}) custom-call(s32[66]{0:T(128)} %pad_add_fusion.s, f32[1024,512]{1,0:T(8,128)} %copy.29.o_ref, f32[1024,512]{1,0:T(8,128)} %copy.30.e_ref, f32[512,512]{1,0:T(8,128)} %copy.31.x_ref, f32[1024,512]{1,0:T(8,128)} %copy.22.a_ref.h_ref, f32[2,512,512]{2,1,0:T(8,128)} %get-tuple-element.18.l_ref), custom_call_target="tpu_custom_call" | custom-call | flops 4831838208 | bytes 12582912 | tf_op jit(solution)/shard_map/pallas_call | solution.py:137
  534.5 11.1 %shard_map.51 = (bf16[3072,512]{1,0:T(8,128)(2,1)}, bf16[3072,512]{1,0:T(8,128)(2,1)}) custom-call(s32[66]{0:T(128)} %pad_add_fusion.s, f32[1024,512]{1,0:T(8,128)} %copy.24.o_ref, f32[1024,512]{1,0:T(8,128)} %copy.25.e_ref, f32[512,512]{1,0:T(8,128)} %copy.26.x_ref, f32[1024,512]{1,0:T(8,128)} %copy.27.b_ref.h_ref, f32[2,512,512]{2,1,0:T(8,128)} %get-tuple-element.18.l_ref), custom_call_target="tpu_custom_call" | custom-call | flops 4831838208 | bytes 12582912 | tf_op jit(solution)/shard_map/pallas_call | solution.py:137
  545.6 35.4 %shard_map.60 = (f32[1,512,512]{2,1,0:T(8,128)}, f32[1,512,512]{2,1,0:T(8,128)}) custom-call(s32[66]{0:T(128)} %pad_add_fusion.s, f32[512,512]{1,0:T(8,128)} %copy.34.p_ref, bf16[3072,512]{1,0:T(8,128)(2,1)} %get-tuple-element.24.lh.ah, bf16[3072,512]{1,0:T(8,128)(2,1)} %get-tuple-element.25.ll.al, bf16[3072,512]{1,0:T(8,128)(2,1)} %get-tuple-element.19.lh.bh, ...), custom_call_target="tpu_custom_call" | custom-call | flops 24999999488 | bytes 6291456 | tf_op jit(solution)/shard_map/pallas_call | solution.py:137
  581.0 13.8 %shard_map.62 = (bf16[512,1024]{1,0:T(8,128)(2,1)}, bf16[512,1024]{1,0:T(8,128)(2,1)}) custom-call(s32[66]{0:T(128)} %pad_add_fusion.s, f32[512,1024]{1,0:T(8,128)} %copy-done, bf16[3072,512]{1,0:T(8,128)(2,1)} %get-tuple-element.24.lh.ah, bf16[3072,512]{1,0:T(8,128)(2,1)} %get-tuple-element.25.ll.al, bf16[3072,512]{1,0:T(8,128)(2,1)} %get-tuple-element.19.lh.bh, ...), custom_call_target="tpu_custom_call" | custom-call | flops 4831838208 | bytes 8388608 | tf_op jit(solution)/shard_map/pallas_call | solution.py:137
  594.8 14.5 %shard_map.55.rest_0_ = f32[2,2048,1024]{2,1,0:T(8,128)} custom-call(s32[66]{0:T(128)} %pad_add_fusion.s, f32[2,2048,1024]{2,1,0:T(8,128)} %b_ref.7, bf16[3072,512]{1,0:T(8,128)(2,1)} %get-tuple-element.24.lh.ah, bf16[3072,512]{1,0:T(8,128)(2,1)} %get-tuple-element.25.ll.al, bf16[512,2048]{1,0:T(8,128)(2,1)} %get-tuple-element.26.rh.cah, ...), custom_call_target="tpu_custom_call" | custom-call | flops 6442450944 | bytes 16777216 | tf_op jit(solution)/shard_map/pallas_call | solution.py:137
  609.3 14.3 %shard_map.56 = f32[2,2048,1024]{2,1,0:T(8,128)} custom-call(s32[66]{0:T(128)} %pad_add_fusion.s, f32[2,2048,1024]{2,1,0:T(8,128)} %b_ref.7, bf16[3072,512]{1,0:T(8,128)(2,1)} %get-tuple-element.19.lh.bh, bf16[3072,512]{1,0:T(8,128)(2,1)} %get-tuple-element.20.ll.bl, bf16[512,2048]{1,0:T(8,128)(2,1)} %get-tuple-element.22.rh.cbh, ...), custom_call_target="tpu_custom_call", output_to_operand_aliasing={{}: (6, {})} | custom-call | flops 6442450944 | bytes 16777216 | tf_op jit(solution)/shard_map/pallas_call | solution.py:137
  623.5 17.5 %shard_map.61 = (bf16[2048,512]{1,0:T(8,128)(2,1)}, bf16[2048,512]{1,0:T(8,128)(2,1)}) custom-call(s32[66]{0:T(128)} %pad_add_fusion.s, f32[1024,512]{1,0:T(8,128)} %copy.35.o_ref, f32[1024,512]{1,0:T(8,128)} %copy.36.e_ref, bf16[3072,512]{1,0:T(8,128)(2,1)} %get-tuple-element.24.lh.ah, bf16[3072,512]{1,0:T(8,128)(2,1)} %get-tuple-element.25.ll.al, ...), custom_call_target="tpu_custom_call" | custom-call | flops 9663676416 | bytes 16777216 | tf_op jit(solution)/shard_map/pallas_call | solution.py:137
  641.1 37.3 %shard_map.63 = f32[2048,1024]{1,0:T(8,128)} custom-call(s32[66]{0:T(128)} %pad_add_fusion.s, f32[2048,1024]{1,0:T(8,128)} %e_ref.3, f32[2,2048,1024]{2,1,0:T(8,128)} %b_ref.7, f32[2,2048,1024]{2,1,0:T(8,128)} %b_ref.7, f32[2,512,1024]{2,1,0:T(8,128)} %collective-permute-done.22.rest_0_.rest_1_.xa_ref.xb_ref, ...), custom_call_target="tpu_custom_call" | custom-call | flops 19327352832 | bytes 50331648 | tf_op jit(solution)/shard_map/pallas_call | solution.py:137
  (88 shorter events, 43.8 us)
Async XLA Ops:
  0.6 7.4 %copy-start.13 = (s32[2,30]{1,0:T(2,128)S(1)}, s32[2,30]{1,0:T(2,128)}, u32[]{:S(2)}) copy-start(s32[2,30]{1,0:T(2,128)} %param.5) | copy-start | bytes 724
  5.5 43.1 %collective-permute-start.10 = (f32[512,1024]{1,0:T(8,128)}, f32[512,1024]{1,0:T(8,128)}, u32[]{:S(2)}, u32[]{:S(2)}) collective-permute-start(f32[512,1024]{1,0:T(8,128)} %get-tuple-element.36), channel_id=1, source_target_pairs={{0,16},{1,17},{2,18},{3,19},{4,20},{5,21},{6,22},{7,23}} | collective-permute-start | bytes 6291464 | tf_op jit(solution)/shard_map/ppermute | solution.py:541
  6.8 49.4 %collective-permute-start = (f32[512,1024]{1,0:T(8,128)}, f32[512,1024]{1,0:T(8,128)}, u32[]{:S(2)}, u32[]{:S(2)}) collective-permute-start(f32[512,1024]{1,0:T(8,128)} %get-tuple-element.37), channel_id=1, source_target_pairs={{0,16},{1,17},{2,18},{3,19},{4,20},{5,21},{6,22},{7,23}} | collective-permute-start | bytes 6291464 | tf_op jit(solution)/shard_map/ppermute | solution.py:541
  12.2 28.8 %collective-permute-start.23 = (f32[512,512]{1,0:T(8,128)}, f32[512,512]{1,0:T(8,128)S(1)}, u32[]{:S(2)}, u32[]{:S(2)}) collective-permute-start(f32[512,512]{1,0:T(8,128)} %shard_map.57), channel_id=1, source_target_pairs={{1,0},{2,1},{3,2},{4,3},{5,4},{6,5},{7,6},{9,8},{10,9},{11,10},{12... | collective-permute-start | bytes 3145736 | tf_op jit(solution)/shard_map/ppermute | solution.py:541
  40.9 1.0 copy-start.12
  47.2 31.5 %copy-start.5 = (f32[512,1024]{1,0:T(8,128)S(1)}, f32[512,1024]{1,0:T(8,128)}, u32[]{:S(2)}) copy-start(f32[512,1024]{1,0:T(8,128)} %shard_map.59) | copy-start | bytes 6291460
  47.2 31.5 %collective-permute-start.25 = (f32[512,1024]{1,0:T(8,128)}, f32[512,1024]{1,0:T(8,128)}, u32[]{:S(2)}, u32[]{:S(2)}) collective-permute-start(f32[512,1024]{1,0:T(8,128)} %shard_map.59), channel_id=1, source_target_pairs={{0,16},{1,17},{2,18},{3,19},{4,20},{5,21},{6,22},{7,23}} | collective-permute-start | bytes 6291464 | tf_op jit(solution)/shard_map/ppermute | solution.py:541
  63.0 21.5 %collective-permute-start.11 = (f32[512,1024]{1,0:T(8,128)}, f32[512,1024]{1,0:T(8,128)}, u32[]{:S(2)}, u32[]{:S(2)}) collective-permute-start(f32[512,1024]{1,0:T(8,128)} %get-tuple-element.34), channel_id=1, source_target_pairs={{0,8},{1,9},{2,10},{3,11},{4,12},{5,13},{6,14},{7,15},{16,24},{17,... | collective-permute-start | bytes 6291464 | tf_op jit(solution)/shard_map/ppermute | solution.py:541
  65.6 24.2 %collective-permute-start.1 = (f32[512,1024]{1,0:T(8,128)}, f32[512,1024]{1,0:T(8,128)}, u32[]{:S(2)}, u32[]{:S(2)}) collective-permute-start(f32[512,1024]{1,0:T(8,128)} %get-tuple-element.35), channel_id=1, source_target_pairs={{0,8},{1,9},{2,10},{3,11},{4,12},{5,13},{6,14},{7,15},{16,24},{17,... | collective-permute-start | bytes 6291464 | tf_op jit(solution)/shard_map/ppermute | solution.py:541
  82.0 14.7 %collective-permute-start.26 = (f32[512,1024]{1,0:T(8,128)}, f32[512,1024]{1,0:T(8,128)}, u32[]{:S(2)}, u32[]{:S(2)}) collective-permute-start(f32[512,1024]{1,0:T(8,128)} %broadcast_select_fusion.6), channel_id=1, source_target_pairs={{0,8},{1,9},{2,10},{3,11},{4,12},{5,13},{6,14},{7,15},{16,24},{17,... | collective-permute-start | bytes 6291464 | tf_op jit(solution)/shard_map/ppermute | solution.py:541
  86.5 6.8 copy-start.1
  86.5 38.2 %collective-permute-start.13 = (f32[1024,512]{0,1:T(8,128)S(1)}, f32[1024,512]{0,1:T(8,128)}, u32[]{:S(2)}, u32[]{:S(2)}) collective-permute-start(f32[1024,512]{0,1:T(8,128)S(1)} %bitcast.18), channel_id=1, source_target_pairs={{10,8},{11,9},{20,18},{21,19},{30,28},{31,29}} | collective-permute-start | bytes 6291464 | tf_op jit(solution)/shard_map/ppermute | solution.py:541
  87.8 37.7 %collective-permute-start.12 = (f32[1024,512]{0,1:T(8,128)S(1)}, f32[1024,512]{0,1:T(8,128)}, u32[]{:S(2)}, u32[]{:S(2)}) collective-permute-start(f32[1024,512]{0,1:T(8,128)S(1)} %bitcast.19), channel_id=1, source_target_pairs={{0,2},{1,3},{10,12},{11,13},{20,22},{21,23}} | collective-permute-start | bytes 6291464 | tf_op jit(solution)/shard_map/ppermute | solution.py:541
  93.3 76.4 %collective-permute-start.3 = (f32[1024,512]{0,1:T(8,128)}, f32[1024,512]{0,1:T(8,128)}, u32[]{:S(2)}, u32[]{:S(2)}) collective-permute-start(f32[1024,512]{0,1:T(8,128)} %bitcast.3), channel_id=1, source_target_pairs={{10,8},{11,9},{20,18},{21,19},{30,28},{31,29}} | collective-permute-start | bytes 6291464 | tf_op jit(solution)/shard_map/ppermute | solution.py:541
  94.6 75.1 %collective-permute-start.2 = (f32[1024,512]{0,1:T(8,128)}, f32[1024,512]{0,1:T(8,128)}, u32[]{:S(2)}, u32[]{:S(2)}) collective-permute-start(f32[1024,512]{0,1:T(8,128)} %bitcast.3), channel_id=1, source_target_pairs={{0,2},{1,3},{10,12},{11,13},{20,22},{21,23}} | collective-permute-start | bytes 6291464 | tf_op jit(solution)/shard_map/ppermute | solution.py:541
  98.6 29.0 %copy-start = (f32[512,1024]{1,0:T(8,128)}, f32[512,1024]{1,0:T(8,128)S(1)}, u32[]{:S(2)}) copy-start(f32[512,1024]{1,0:T(8,128)S(1)} %broadcast_select_fusion.9.p_ref) | copy-start | bytes 6291460
  98.6 115.9 %collective-permute-start.28 = (f32[1024,512]{0,1:T(8,128)S(1)}, f32[1024,512]{0,1:T(8,128)S(1)}, u32[]{:S(2)}, u32[]{:S(2)}) collective-permute-start(f32[1024,512]{0,1:T(8,128)S(1)} %bitcast.16), channel_id=1, source_target_pairs={{10,8},{11,9},{20,18},{21,19},{30,28},{31,29}} | collective-permute-start | bytes 6291464 | tf_op jit(solution)/shard_map/ppermute | solution.py:541
  124.8 89.8 %collective-permute-start.27 = (f32[1024,512]{0,1:T(8,128)S(1)}, f32[1024,512]{0,1:T(8,128)S(1)}, u32[]{:S(2)}, u32[]{:S(2)}) collective-permute-start(f32[1024,512]{0,1:T(8,128)S(1)} %bitcast.17), channel_id=1, source_target_pairs={{0,2},{1,3},{10,12},{11,13},{20,22},{21,23}} | collective-permute-start | bytes 6291464 | tf_op jit(solution)/shard_map/ppermute | solution.py:541
  127.6 44.1 %copy-start.7 = (f32[1024,512]{0,1:T(8,128)}, f32[1024,512]{0,1:T(8,128)S(1)}, u32[]{:S(2)}) copy-start(f32[1024,512]{0,1:T(8,128)S(1)} %broadcast_select_fusion.13) | copy-start | bytes 6291460
  127.6 90.0 %collective-permute-start.14 = (f32[1024,512]{0,1:T(8,128)S(1)}, f32[1024,512]{0,1:T(8,128)}, u32[]{:S(2)}, u32[]{:S(2)}) collective-permute-start(f32[1024,512]{0,1:T(8,128)S(1)} %broadcast_select_fusion.13), channel_id=1, source_target_pairs={{2,4},{3,5},{12,14},{13,15},{18,16},{19,17},{28,26},{29,27}} | collective-permute-start | bytes 6291464 | tf_op jit(solution)/shard_map/ppermute | solution.py:541
  171.7 43.2 %copy-start.8 = (f32[1024,512]{0,1:T(8,128)}, f32[1024,512]{0,1:T(8,128)S(1)}, u32[]{:S(2)}) copy-start(f32[1024,512]{0,1:T(8,128)S(1)} %broadcast_select_fusion.14) | copy-start | bytes 6291460
  171.8 47.9 %collective-permute-start.4 = (f32[1024,512]{0,1:T(8,128)S(1)}, f32[1024,512]{0,1:T(8,128)}, u32[]{:S(2)}, u32[]{:S(2)}) collective-permute-start(f32[1024,512]{0,1:T(8,128)S(1)} %broadcast_select_fusion.14), channel_id=1, source_target_pairs={{2,4},{3,5},{12,14},{13,15},{18,16},{19,17},{28,26},{29,27}} | collective-permute-start | bytes 6291464 | tf_op jit(solution)/shard_map/ppermute | solution.py:541
  215.0 43.0 %copy-start.6 = (f32[1024,512]{0,1:T(8,128)}, f32[1024,512]{0,1:T(8,128)S(1)}, u32[]{:S(2)}) copy-start(f32[1024,512]{0,1:T(8,128)S(1)} %broadcast_select_fusion.12) | copy-start | bytes 6291460
  215.0 41.0 %collective-permute-start.29 = (f32[1024,512]{0,1:T(8,128)S(1)}, f32[1024,512]{0,1:T(8,128)}, u32[]{:S(2)}, u32[]{:S(2)}) collective-permute-start(f32[1024,512]{0,1:T(8,128)S(1)} %broadcast_select_fusion.12), channel_id=1, source_target_pairs={{2,4},{3,5},{12,14},{13,15},{18,16},{19,17},{28,26},{29,27}} | collective-permute-start | bytes 6291464 | tf_op jit(solution)/shard_map/ppermute | solution.py:541
  217.6 40.4 %collective-permute-start.15 = (f32[1024,512]{0,1:T(8,128)}, f32[1024,512]{0,1:T(8,128)}, u32[]{:S(2)}, u32[]{:S(2)}) collective-permute-start(f32[1024,512]{0,1:T(8,128)} %collective-permute-done.14), channel_id=1, source_target_pairs={{4,6},{5,7},{26,24},{27,25}} | collective-permute-start | bytes 6291464 | tf_op jit(solution)/shard_map/ppermute | solution.py:541
  219.7 42.1 %collective-permute-start.5 = (f32[1024,512]{0,1:T(8,128)}, f32[1024,512]{0,1:T(8,128)}, u32[]{:S(2)}, u32[]{:S(2)}) collective-permute-start(f32[1024,512]{0,1:T(8,128)} %collective-permute-done.4), channel_id=1, source_target_pairs={{4,6},{5,7},{26,24},{27,25}} | collective-permute-start | bytes 6291464 | tf_op jit(solution)/shard_map/ppermute | solution.py:541
  221.7 40.1 %copy-start.9 = (f32[1024,512]{0,1:T(8,128)S(1)}, f32[1024,512]{0,1:T(8,128)}, u32[]{:S(2)}) copy-start(f32[1024,512]{0,1:T(8,128)} %copy-done.8) | copy-start | bytes 6291460
  256.0 17.9 %collective-permute-start.30 = (f32[1024,512]{0,1:T(8,128)}, f32[1024,512]{0,1:T(8,128)}, u32[]{:S(2)}, u32[]{:S(2)}) collective-permute-start(f32[1024,512]{0,1:T(8,128)} %collective-permute-done.29), channel_id=1, source_target_pairs={{4,6},{5,7},{26,24},{27,25}} | collective-permute-start | bytes 6291464 | tf_op jit(solution)/shard_map/ppermute | solution.py:541
  261.2 48.7 %collective-permute-start.16 = (f32[1024,512]{0,1:T(8,128)S(1)}, f32[1024,512]{0,1:T(8,128)}, u32[]{:S(2)}, u32[]{:S(2)}) collective-permute-start(f32[1024,512]{0,1:T(8,128)S(1)} %select_select_fusion.1), channel_id=1, source_target_pairs={{0,1},{1,0},{2,3},{3,2},{4,5},{5,4},{6,7},{7,6},{8,9},{9,8},{10,11... | collective-permute-start | bytes 6291464 | tf_op jit(solution)/shard_map/ppermute | solution.py:541
  265.6 93.9 %collective-permute-start.6 = (f32[1024,512]{0,1:T(8,128)}, f32[1024,512]{0,1:T(8,128)}, u32[]{:S(2)}, u32[]{:S(2)}) collective-permute-start(f32[1024,512]{0,1:T(8,128)} %select_select_fusion.2), channel_id=1, source_target_pairs={{0,1},{1,0},{2,3},{3,2},{4,5},{5,4},{6,7},{7,6},{8,9},{9,8},{10,11... | collective-permute-start | bytes 6291464 | tf_op jit(solution)/shard_map/ppermute | solution.py:541
  271.9 140.8 %collective-permute-start.22 = (f32[2,512,1024]{2,1,0:T(8,128)}, f32[2,512,1024]{2,1,0:T(8,128)}, u32[]{:S(2)}, u32[]{:S(2)}) collective-permute-start(f32[2,512,1024]{2,1,0:T(8,128)} %slice.41), channel_id=1, source_target_pairs={{8,0},{9,1},{10,2},{11,3},{12,4},{13,5},{14,6},{15,7},{16,8},{17,9... | collective-permute-start | bytes 12582920 | tf_op jit(solution)/shard_map/ppermute | solution.py:541
  277.1 116.6 %copy-start.3 = (f32[1024,512]{0,1:T(8,128)}, f32[1024,512]{0,1:T(8,128)S(1)}, u32[]{:S(2)}) copy-start(f32[1024,512]{0,1:T(8,128)S(1)} %select_select_fusion) | copy-start | bytes 6291460
  277.1 116.6 %collective-permute-start.31 = (f32[1024,512]{0,1:T(8,128)S(1)}, f32[1024,512]{0,1:T(8,128)S(1)}, u32[]{:S(2)}, u32[]{:S(2)}) collective-permute-start(f32[1024,512]{0,1:T(8,128)S(1)} %select_select_fusion), channel_id=1, source_target_pairs={{0,1},{1,0},{2,3},{3,2},{4,5},{5,4},{6,7},{7,6},{8,9},{9,8},{10,11... | collective-permute-start | bytes 6291464 | tf_op jit(solution)/shard_map/ppermute | solution.py:541
  311.9 51.0 %copy-start.2 = (f32[512,1024]{1,0:T(8,128)S(1)}, f32[512,1024]{1,0:T(8,128)}, u32[]{:S(2)}) copy-start(f32[512,1024]{1,0:T(8,128)} %copy-done.1) | copy-start | bytes 6291460
  311.9 83.3 %collective-permute-start.17 = (f32[1024,512]{0,1:T(8,128)S(1)}, f32[1024,512]{0,1:T(8,128)S(1)}, u32[]{:S(2)}, u32[]{:S(2)}) collective-permute-start(f32[1024,512]{0,1:T(8,128)S(1)} %broadcast_select_fusion), channel_id=1, source_target_pairs={{0,16},{1,17},{2,18},{3,19},{4,20},{5,21},{6,22},{7,23}} | collective-permute-start | bytes 6291464 | tf_op jit(solution)/shard_map/ppermute | solution.py:541
  361.6 38.5 %collective-permute-start.8 = (f32[1024,512]{0,1:T(8,128)S(1)}, f32[1024,512]{0,1:T(8,128)S(1)}, u32[]{:S(2)}, u32[]{:S(2)}) collective-permute-start(f32[1024,512]{0,1:T(8,128)S(1)} %broadcast_select_fusion.1), channel_id=1, source_target_pairs={{0,16},{1,17},{2,18},{3,19},{4,20},{5,21},{6,22},{7,23}} | collective-permute-start | bytes 6291464 | tf_op jit(solution)/shard_map/ppermute | solution.py:541
  364.3 26.9 %collective-permute-start.19 = (f32[512,512]{1,0:T(8,128)S(1)}, f32[512,512]{1,0:T(8,128)S(1)}, u32[]{:S(2)}, u32[]{:S(2)}) collective-permute-start(f32[512,512]{1,0:T(8,128)S(1)} %slice_select_fusion.2), channel_id=1, source_target_pairs={{1,0},{2,1},{3,2},{4,3},{5,4},{6,5},{7,6},{9,8},{10,9},{11,10},{12... | collective-permute-start | bytes 3145736 | tf_op jit(solution)/shard_map/ppermute | solution.py:541
  391.2 23.4 %collective-permute-start.20 = (f32[512,512]{1,0:T(8,128)S(1)}, f32[512,512]{1,0:T(8,128)S(1)}, u32[]{:S(2)}, u32[]{:S(2)}) collective-permute-start(f32[512,512]{1,0:T(8,128)S(1)} %collective-permute-done.19), channel_id=1, source_target_pairs={{0,8},{1,9},{2,10},{3,11},{4,12},{5,13},{6,14},{7,15},{8,0},{9,1},... | collective-permute-start | bytes 3145736 | tf_op jit(solution)/shard_map/ppermute | solution.py:541
  393.6 3.2 copy-start.10
  393.9 16.7 %collective-permute-start.32 = (f32[512,512]{0,1:T(8,128)S(1)}, f32[512,512]{0,1:T(8,128)S(1)}, u32[]{:S(2)}, u32[]{:S(2)}) collective-permute-start(f32[512,512]{0,1:T(8,128)S(1)} %slice_select_fusion), channel_id=1, source_target_pairs={{0,16},{1,17},{2,18},{3,19},{4,20},{5,21},{6,22},{7,23}} | collective-permute-start | bytes 3145736 | tf_op jit(solution)/shard_map/ppermute | solution.py:541
  396.9 56.6 %collective-permute-start.18 = (f32[1024,512]{0,1:T(8,128)}, f32[1024,512]{0,1:T(8,128)}, u32[]{:S(2)}, u32[]{:S(2)}) collective-permute-start(f32[1024,512]{0,1:T(8,128)} %broadcast_select_fusion.2), channel_id=1, source_target_pairs={{0,8},{1,9},{2,10},{3,11},{4,12},{5,13},{6,14},{7,15},{16,24},{17,... | collective-permute-start | bytes 6291464 | tf_op jit(solution)/shard_map/ppermute | solution.py:541
  401.8 55.7 %collective-permute-start.9 = (f32[1024,512]{0,1:T(8,128)}, f32[1024,512]{0,1:T(8,128)}, u32[]{:S(2)}, u32[]{:S(2)}) collective-permute-start(f32[1024,512]{0,1:T(8,128)} %broadcast_select_fusion.3), channel_id=1, source_target_pairs={{0,8},{1,9},{2,10},{3,11},{4,12},{5,13},{6,14},{7,15},{16,24},{17,... | collective-permute-start | bytes 6291464 | tf_op jit(solution)/shard_map/ppermute | solution.py:541
  410.6 31.9 %collective-permute-start.21 = (f32[512,512]{0,1:T(8,128)}, f32[512,512]{0,1:T(8,128)}, u32[]{:S(2)}, u32[]{:S(2)}) collective-permute-start(f32[512,512]{0,1:T(8,128)} %slice_select_fusion.1), channel_id=1, source_target_pairs={{8,0},{9,1},{10,2},{11,3},{12,4},{13,5},{14,6},{15,7},{16,8},{17,9... | collective-permute-start | bytes 3145736 | tf_op jit(solution)/shard_map/ppermute | solution.py:541
  412.7 36.7 %collective-permute-start.7 = (f32[512,512]{0,1:T(8,128)}, f32[512,512]{0,1:T(8,128)}, u32[]{:S(2)}, u32[]{:S(2)}) collective-permute-start(f32[512,512]{0,1:T(8,128)} %slice_select_fusion.3), channel_id=1, source_target_pairs={{8,0},{9,1},{10,2},{11,3},{12,4},{13,5},{14,6},{15,7},{16,8},{17,9... | collective-permute-start | bytes 3145736 | tf_op jit(solution)/shard_map/ppermute | solution.py:541
  414.6 37.2 %collective-permute-start.33 = (f32[512,512]{0,1:T(8,128)S(1)}, f32[512,512]{0,1:T(8,128)}, u32[]{:S(2)}, u32[]{:S(2)}) collective-permute-start(f32[512,512]{0,1:T(8,128)S(1)} %broadcast_select_fusion.15), channel_id=1, source_target_pairs={{0,8},{1,9},{2,10},{3,11},{4,12},{5,13},{6,14},{7,15},{16,24},{17,... | collective-permute-start | bytes 3145736 | tf_op jit(solution)/shard_map/ppermute | solution.py:541
  429.8 3.1 copy-start.4
  437.5 3.1 copy-start.11
  442.4 198.7 %collective-permute-start.24 = (f32[1536,512]{1,0:T(8,128)}, f32[1536,512]{1,0:T(8,128)}, u32[]{:S(2)}, u32[]{:S(2)}) collective-permute-start(f32[1536,512]{1,0:T(8,128)} %shard_map.58), channel_id=1, source_target_pairs={{1,0},{2,1},{3,2},{4,3},{5,4},{6,5},{7,6},{9,8},{10,9},{11,10},{12... | collective-permute-start | bytes 9437192 | tf_op jit(solution)/shard_map/ppermute | solution.py:541

commit v2 on v1

--- a/solution.py
+++ b/solution.py
@@ -92,7 +92,25 @@
     return done
 
 
-def chol_steps(work, diag, inv_ref, invt_ref):
+def pack_at(i, j):
+    return i * (i + 1) // 2 + j
+
+
+PACKED = pack_at(SEP // DB, 0) * DB
+
+
+def unpack(ref, b, transposed, high_ref, low_ref):
+    for i in range(SEP // DB):
+        for j in range(SEP // DB):
+            at = (pl.ds(j * DB, DB), pl.ds(i * DB, DB)) if transposed else (pl.ds(i * DB, DB), pl.ds(j * DB, DB))
+            if j <= i:
+                block = ref[b, pl.ds(pack_at(i, j) * DB, DB), :]
+                high_ref[at], low_ref[at] = split(block.T if transposed else block)
+            else:
+                high_ref[at] = low_ref[at] = jnp.zeros((DB, DB), BF16)
+
+
+def chol_steps(work, diag, inv_ref):
     count = work.shape[0]
     steps = SEP // DB
     eye = (
@@ -128,9 +146,9 @@
 
     lax.fori_loop(0, steps, step, 0)
     for b in range(count):
-        inv = work[b, :, pl.ds(SEP, SEP)]
-        inv_ref[b] = inv
-        invt_ref[b] = inv.T
+        for i in range(steps):
+            for j in range(i + 1):
+                inv_ref[b, pl.ds(pack_at(i, j) * DB, DB), :] = work[b, pl.ds(i * DB, DB), pl.ds(SEP + j * DB, DB)]
 
 
 def call(kernel, grid, in_specs, out_shape, out_specs, scratch, args, flops, nbytes, aliases=None):
@@ -156,6 +174,7 @@
         self.row_blocks, self.col_blocks = rows_loc // BLK, cols_loc // BLK
         self.blocks = rows * rows_loc // BLK
         self.half = cols_loc // SEP
+        self.piece = cols_loc // rows
         assert cols == 2 * rows and rows_loc == 2 * cols_loc and rows_loc >= 2 * SEP and cols_loc >= SEP
 
     def r(self, s):
@@ -182,169 +201,204 @@
         return valid, jnp.where(valid, found, 0)
 
 
-def child_factor(plan, scal, head_a, head_b):
-    def kernel(s, a_ref, b_ref, inv_ref, invt_ref, work, diag):
-        work[0, :, pl.ds(0, SEP)] = a_ref[...]
-        work[1, :, pl.ds(0, SEP)] = b_ref[...]
-        chol_steps(work, diag, inv_ref, invt_ref)
-
-    block = pl.BlockSpec((SEP, SEP), lambda g, s: (0, 0))
-    out = pl.BlockSpec((2, SEP, SEP), lambda g, s: (0, 0, 0))
-    return call(
-        kernel, (1,), [block, block], [shape_of((2, SEP, SEP))] * 2, [out, out],
-        [pltpu.VMEM((2, SEP, 2 * SEP), F32), pltpu.VMEM((2, DB, DB), F32)],
-        (scal, head_a, head_b), 3e10, 6 * 2**20,
-    )
-
-
-def parent_factor(plan, scal, pivot, rt, cols):
-    def kernel(s, p_ref, ah, al, bh, bl, cah, cal, cbh, cbl, inv_ref, invt_ref, work, diag):
-        total = p_ref[...]
-        for k, (lh, ll, rh, rl) in enumerate(((ah, al, cah, cal), (bh, bl, cbh, cbl))):
-            update = dot3((lh[...], ll[...]), (rh[...], rl[...]))
-            keep = plan.source(s, k, 1) >= 0
-            edge = lax.broadcasted_iota(jnp.int32, (SEP, SEP), 0) >= BLK
-            edge = edge | (lax.broadcasted_iota(jnp.int32, (SEP, SEP), 1) >= BLK)
-            total = total - jnp.where(edge & jnp.logical_not(keep), 0.0, update)
-        work[0, :, pl.ds(0, SEP)] = total
-        chol_steps(work, diag, inv_ref, invt_ref)
-
-    pivot_spec = pl.BlockSpec((SEP, SEP), lambda g, s: (0, 0))
-    left = pl.BlockSpec((SEP, SEP), lambda g, s: (2 * plan.half + 1, 0))
-    right = pl.BlockSpec((SEP, SEP), lambda g, s: (0, plan.half + 1))
-    out = pl.BlockSpec((1, SEP, SEP), lambda g, s: (0, 0, 0))
-    return call(
-        kernel, (1,), [pivot_spec] + [left] * 4 + [right] * 4, [shape_of((1, SEP, SEP))] * 2, [out, out],
-        [pltpu.VMEM((1, SEP, 2 * SEP), F32), pltpu.VMEM((1, DB, DB), F32)],
-        (scal, pivot, *rt[0], *rt[1], *cols[0], *cols[1]), 2.5e10, 6 * 2**20,
-    )
-
-
-def child_rows(plan, scal, k, own, other, after, head, invt):
-    half = plan.half
-    jobs = 2 * half + 2
-
-    def kernel(s, o_ref, e_ref, x_ref, h_ref, l_ref, hi_ref, lo_ref, lh, ll):
+def pack_pivots(plan, scal, fronts, ahead):
+    def kernel(s, a_ref, *rest):
+        out_ref = rest[-1]
+        for k in (0, 1):
+            for i in range(SEP // DB):
+                for j in range(i, SEP // DB):
+                    block = a_ref[k, pl.ds(i * DB, DB), pl.ds(j * DB, DB)]
+                    out_ref[k, pl.ds(pack_at(j, i) * DB, DB), :] = block
+
+    return call(
+        kernel, (1,),
+        [pl.BlockSpec((2, SEP, SEP), lambda g, s: (0, 0, 0))] + [pl.BlockSpec(memory_space=pl.ANY)] * len(ahead),
+        shape_of((2, PACKED, DB)), pl.BlockSpec((2, PACKED, DB), lambda g, s: (0, 0, 0)), [],
+        (scal, fronts, *ahead), 1, 4 * 2**20,
+    )
+
+
+def child_factor(plan, scal, pivots, ahead):
+    def kernel(s, a_ref, *rest):
+        inv_ref, work, diag = rest[-3:]
+        for k in (0, 1):
+            for i in range(SEP // DB):
+                for j in range(SEP // DB):
+                    at = (k, pl.ds(i * DB, DB), pl.ds(j * DB, DB))
+                    zero = jnp.zeros((DB, DB), F32)
+                    work[at] = a_ref[k, pl.ds(pack_at(j, i) * DB, DB), :] if j >= i else zero
+        chol_steps(work, diag, inv_ref)
+
+    block = pl.BlockSpec((2, PACKED, DB), lambda g, s: (0, 0, 0))
+    return call(
+        kernel, (1,), [block] + [pl.BlockSpec(memory_space=pl.ANY)] * len(ahead), shape_of((2, PACKED, DB)), block,
+        [pltpu.VMEM((2, SEP, 2 * SEP), F32), pltpu.VMEM((2, DB, DB), F32)], (scal, pivots, *ahead), 4e10, 4 * 2**20,
+    )
+
+
+def parent_factor(plan, scal, panel, wide, inv, ahead):
+    def kernel(s, m_ref, p_ref, l_ref, *rest):
+        out_ref, work, diag, full = rest[-4:]
+        first = (plan.r(s) == 0) & (plan.c(s) == 0)
+
+        @pl.when(first)
+        def _():
+            steps = SEP // DB
+            total = m_ref[...]
+            for k in (0, 1):
+                for i in range(steps):
+                    for j in range(steps):
+                        zero = jnp.zeros((DB, DB), F32)
+                        block = l_ref[k, pl.ds(pack_at(i, j) * DB, DB), :] if j <= i else zero
+                        full[pl.ds(i * DB, DB), pl.ds(j * DB, DB)] = block
+                head = dot_full(full[...], p_ref[k])
+                update = dot_full(head, head, ((0,), (0,)))
+                keep = plan.source(s, k, 1) >= 0
+                edge = lax.broadcasted_iota(jnp.int32, (SEP, SEP), 0) >= BLK
+                edge = edge | (lax.broadcasted_iota(jnp.int32, (SEP, SEP), 1) >= BLK)
+                total = total - jnp.where(edge & jnp.logical_not(keep), 0.0, update)
+            work[0, :, pl.ds(0, SEP)] = total
+            chol_steps(work, diag, out_ref)
+
+        @pl.when(jnp.logical_not(first))
+        def _():
+            out_ref[...] = jnp.zeros(out_ref.shape, F32)
+
+    both = pl.BlockSpec((2, PACKED, DB), lambda g, s: (0, 0, 0))
+    return call(
+        kernel, (1,),
+        [pl.BlockSpec((SEP, SEP), lambda g, s: (0, 0)), pl.BlockSpec((2, SEP, SEP), lambda g, s: (0, 0, 1)), both]
+        + [pl.BlockSpec(memory_space=pl.ANY)] * len(ahead),
+        shape_of((1, PACKED, DB)), pl.BlockSpec((1, PACKED, DB), lambda g, s: (0, 0, 0)),
+        [pltpu.VMEM((1, SEP, 2 * SEP), F32), pltpu.VMEM((1, DB, DB), F32), pltpu.VMEM((SEP, SEP), F32)],
+        (scal, panel, wide, inv, *ahead), 4e10, 8 * 2**20,
+    )
+
+
+def child_rows(plan, scal, k, rows, after, inv):
+    count = plan.rows_loc // SEP
+    slots = SEP // plan.piece
+
+    def kernel(s, o_ref, x_ref, l_ref, hi_ref, lo_ref, lh, ll):
         j = pl.program_id(0)
 
         @pl.when(j == 0)
         def _():
-            lh[...], ll[...] = split(l_ref[0])
-
-        side = j // half
-        parity = plan.c(s) % 2
-        value = jnp.where(side == parity, o_ref[...], e_ref[...])
-        value = jnp.where(j == 2 * half, x_ref[...], jnp.where(j == 2 * half + 1, h_ref[...], value))
+            unpack(l_ref, 0, True, lh, ll)
+
+        value = jnp.where(j == count, x_ref[...].reshape(SEP, SEP), o_ref[...].reshape(SEP, SEP))
         hi_ref[...], lo_ref[...] = split(dot3(split(value), (lh[...], ll[...])))
 
+    blk = (SEP, SEP)
+    cut = (slots, 1, 1, plan.piece, SEP)
+    out = pl.BlockSpec(blk, lambda j, s: (j, 0))
+
     def own_at(j, s):
-        return (jnp.clip(j - half * (plan.c(s) % 2), 0, half - 1), 0)
-
-    def other_at(j, s):
-        return (jnp.clip(j - half * (1 - plan.c(s) % 2), 0, half - 1), 0)
-
-    blk = (SEP, SEP)
-    out = pl.BlockSpec(blk, lambda j, s: (j, 0))
-    return call(
-        kernel, (jobs,),
-        [pl.BlockSpec(blk, own_at), pl.BlockSpec(blk, other_at), pl.BlockSpec(blk, lambda j, s: (0, 0)),
-         pl.BlockSpec(blk, lambda j, s: (1, 0)), pl.BlockSpec((1, SEP, SEP), lambda j, s: (k, 0, 0))],
-        [shape_of((jobs * SEP, SEP), BF16)] * 2, [out, out], [pltpu.VMEM(blk, BF16)] * 2,
-        (scal, own, other, after, head, invt), 6 * jobs * SEP**3, 8 * jobs * SEP**2,
-    )
-
-
-def child_cols(plan, scal, k, own, after, head, inv):
-    half = plan.half
-    jobs = half + 2
-
-    def kernel(s, o_ref, x_ref, h_ref, l_ref, hi_ref, lo_ref, lh, ll):
-        j = pl.program_id(0)
-
-        @pl.when(j == 0)
-        def _():
-            lh[...], ll[...] = split(l_ref[0])
-
-        @pl.when(j <= half)
-        def _():
-            value = jnp.where(j == half, x_ref[...], o_ref[...])
-            hi_ref[...], lo_ref[...] = split(dot3((lh[...], ll[...]), split(value)))
-
-        @pl.when(j == half + 1)
-        def _():
-            hi_ref[...], lo_ref[...] = split(dot3((lh[...], ll[...]), split(h_ref[...]), ((1,), (1,))))
+        at = jnp.minimum(j, count - 1)
+        return (at % plan.half, at // plan.half, k, 0, 0)
+
+    return call(
+        kernel, (count + 1,),
+        [pl.BlockSpec(cut, own_at), pl.BlockSpec(cut[:1] + cut[2:], lambda j, s: (0, k, 0, 0)),
+         pl.BlockSpec((1, PACKED, DB), lambda j, s: (k, 0, 0))],
+        [shape_of(((count + 1) * SEP, SEP), BF16)] * 2, [out, out], [pltpu.VMEM(blk, BF16)] * 2,
+        (scal, rows, after, inv), 6 * (count + 1) * SEP**3, 8 * (count + 1) * SEP**2,
+    )
+
+
+def child_heads(plan, scal, head, inv):
+    slots = SEP // plan.piece
+
+    def kernel(s, h_ref, l_ref, hi_ref, lo_ref, thi_ref, tlo_ref, lh, ll):
+        unpack(l_ref, 0, False, lh, ll)
+        value = split(h_ref[...].reshape(SEP, SEP))
+        out = dot3((lh[...], ll[...]), value, ((1,), (1,)))
+        hi_ref[0], lo_ref[0] = split(out)
+        thi_ref[0], tlo_ref[0] = split(out.T)
+
+    out = pl.BlockSpec((1, SEP, SEP), lambda k, s: (k, 0, 0))
+    return call(
+        kernel, (2,),
+        [pl.BlockSpec((slots, 1, plan.piece, SEP), lambda k, s: (0, k, 0, 0)),
+         pl.BlockSpec((1, PACKED, DB), lambda k, s: (k, 0, 0))],
+        [shape_of((2, SEP, SEP), BF16)] * 4, [out] * 4, [pltpu.VMEM((SEP, SEP), BF16)] * 2,
+        (scal, head, inv), 12 * SEP**3, 16 * SEP**2,
+    )
+
+
+def child_cols(plan, scal, k, held, sent, inv):
+    count = plan.half + 1
+
+    def kernel(s, h_ref, t_ref, l_ref, hi_ref, lo_ref, lh, ll):
+        @pl.when(pl.program_id(0) == 0)
+        def _():
+            unpack(l_ref, 0, False, lh, ll)
+
+        value = jnp.where(plan.r(s) % 2 == 1, t_ref[0], h_ref[0])
+        hi_ref[...], lo_ref[...] = split(dot3((lh[...], ll[...]), split(value)))
 
     blk = (SEP, SEP)
     out = pl.BlockSpec(blk, lambda j, s: (0, j))
     return call(
-        kernel, (jobs,),
-        [pl.BlockSpec(blk, lambda j, s: (0, jnp.minimum(j, half - 1))), pl.BlockSpec(blk, lambda j, s: (0, 0)),
-         pl.BlockSpec(blk, lambda j, s: (1, 0)), pl.BlockSpec((1, SEP, SEP), lambda j, s: (k, 0, 0))],
-        [shape_of((SEP, jobs * SEP), BF16)] * 2, [out, out], [pltpu.VMEM(blk, BF16)] * 2,
-        (scal, own, after, head, inv), 6 * jobs * SEP**3, 8 * jobs * SEP**2,
-    )
-
-
-def parent_rows(plan, scal, own, other, rt, cols, invt):
+        kernel, (count,),
+        [pl.BlockSpec((1, SEP, SEP), lambda j, s: (k, 0, jnp.where(plan.r(s) % 2 == 1, 0, j))),
+         pl.BlockSpec((1, SEP, SEP), lambda j, s: (k, 0, jnp.where(plan.r(s) % 2 == 1, j, 0))),
+         pl.BlockSpec((1, PACKED, DB), lambda j, s: (k, 0, 0))],
+        [shape_of((SEP, count * SEP), BF16)] * 2, [out, out], [pltpu.VMEM(blk, BF16)] * 2,
+        (scal, held, sent, inv), 6 * count * SEP**3, 8 * count * SEP**2,
+    )
+
+
+def parent_rows(plan, scal, panel, rt, heads, inv):
     count = plan.row_blocks
-    in_half = count // 2
-
-    def kernel(s, o_ref, e_ref, ah, al, bh, bl, cah, cal, cbh, cbl, l_ref, hi_ref, lo_ref, lh, ll, rh, rl):
+
+    def kernel(s, o_ref, ah, al, bh, bl, ch, cl, l_ref, hi_ref, lo_ref, lh, ll, rh, rl):
         i = pl.program_id(0)
 
         @pl.when(i == 0)
         def _():
-            lh[...], ll[...] = split(l_ref[0])
-            for k, (high, low) in enumerate(((cah, cal), (cbh, cbl))):
+            unpack(l_ref, 0, True, lh, ll)
+            for k in (0, 1):
                 keep = plan.source(s, k, 1) >= 0
-                lane = lax.broadcasted_iota(jnp.int32, (SEP, SEP), 1)
-                drop = (lane >= BLK) & jnp.logical_not(keep)
-                rh[k] = jnp.where(drop, 0.0, high[...].astype(F32)).astype(BF16)
-                rl[k] = jnp.where(drop, 0.0, low[...].astype(F32)).astype(BF16)
-
-        side = i // in_half
-        value = jnp.where(side == plan.c(s) % 2, o_ref[...], e_ref[...])
+                drop = (lax.broadcasted_iota(jnp.int32, (SEP, SEP), 1) >= BLK) & jnp.logical_not(keep)
+                rh[k] = jnp.where(drop, 0.0, ch[k].astype(F32)).astype(BF16)
+                rl[k] = jnp.where(drop, 0.0, cl[k].astype(F32)).astype(BF16)
+
+        value = o_ref[...].reshape(BLK, SEP)
         for k, (high, low) in enumerate(((ah, al), (bh, bl))):
             valid, _ = plan.row_at(s, k, i)
             value = value - jnp.where(valid, dot3((high[...], low[...]), (rh[k], rl[k])), 0.0)
         hi_ref[...], lo_ref[...] = split(dot3(split(value), (lh[...], ll[...])))
 
-    def own_at(i, s):
-        return (jnp.clip(i - in_half * (plan.c(s) % 2), 0, in_half - 1), 0)
-
-    def other_at(i, s):
-        return (jnp.clip(i - in_half * (1 - plan.c(s) % 2), 0, in_half - 1), 0)
-
     blk = (BLK, SEP)
+    slots = BLK // plan.piece
+    in_panel = count // 2
+    own = pl.BlockSpec((slots, 1, plan.piece, SEP), lambda i, s: (i % in_panel, i // in_panel, 0, 0))
     rows = [pl.BlockSpec(blk, lambda i, s, k=k: (plan.row_at(s, k, i)[1], 0)) for k in (0, 0, 1, 1)]
-    head = pl.BlockSpec((SEP, SEP), lambda i, s: (0, plan.half + 1))
+    head = pl.BlockSpec((2, SEP, SEP), lambda i, s: (0, 0, 0))
     out = pl.BlockSpec(blk, lambda i, s: (i, 0))
     return call(
-        kernel, (count,),
-        [pl.BlockSpec(blk, own_at), pl.BlockSpec(blk, other_at)] + rows + [head] * 4
-        + [pl.BlockSpec((1, SEP, SEP), lambda i, s: (0, 0, 0))],
+        kernel, (count,), [own] + rows + [head] * 2 + [pl.BlockSpec((1, PACKED, DB), lambda i, s: (0, 0, 0))],
         [shape_of((plan.rows_loc, SEP), BF16)] * 2, [out, out],
         [pltpu.VMEM((SEP, SEP), BF16)] * 2 + [pltpu.VMEM((2, SEP, SEP), BF16)] * 2,
-        (scal, own, other, *rt[0], *rt[1], *cols[0], *cols[1], invt),
-        18 * plan.rows_loc * SEP**2, 16 * plan.rows_loc * SEP,
-    )
-
-
-def parent_cols(plan, scal, panel, rt, cols, inv):
+        (scal, panel, *rt[0], *rt[1], *heads[:2], inv), 18 * plan.rows_loc * SEP**2, 16 * plan.rows_loc * SEP,
+    )
+
+
+def parent_cols(plan, scal, panel, heads, cols, inv):
     count = plan.col_blocks
 
-    def kernel(s, p_ref, ah, al, bh, bl, cah, cal, cbh, cbl, l_ref, hi_ref, lo_ref, lh, ll, rh, rl):
+    def kernel(s, p_ref, th, tl, cah, cal, cbh, cbl, l_ref, hi_ref, lo_ref, lh, ll, rh, rl):
         j = pl.program_id(0)
 
         @pl.when(j == 0)
         def _():
-            lh[...], ll[...] = split(l_ref[0])
-            for k, (high, low) in enumerate(((ah, al), (bh, bl))):
+            unpack(l_ref, 0, False, lh, ll)
+            for k in (0, 1):
                 keep = plan.source(s, k, 1) >= 0
-                line = lax.broadcasted_iota(jnp.int32, (SEP, SEP), 0)
-                drop = (line >= BLK) & jnp.logical_not(keep)
-                rh[k] = jnp.where(drop, 0.0, high[...].astype(F32)).astype(BF16)
-                rl[k] = jnp.where(drop, 0.0, low[...].astype(F32)).astype(BF16)
+                drop = (lax.broadcasted_iota(jnp.int32, (SEP, SEP), 0) >= BLK) & jnp.logical_not(keep)
+                rh[k] = jnp.where(drop, 0.0, th[k].astype(F32)).astype(BF16)
+                rl[k] = jnp.where(drop, 0.0, tl[k].astype(F32)).astype(BF16)
 
         value = p_ref[...]
         for k, (high, low) in enumerate(((cah, cal), (cbh, cbl))):
@@ -353,15 +407,14 @@
         hi_ref[...], lo_ref[...] = split(dot3((lh[...], ll[...]), split(value)))
 
     blk = (SEP, BLK)
-    head = pl.BlockSpec((SEP, SEP), lambda j, s: (2 * plan.half + 1, 0))
+    head = pl.BlockSpec((2, SEP, SEP), lambda j, s: (0, 0, 0))
     right = [pl.BlockSpec(blk, lambda j, s, k=k: (0, plan.col_at(s, k, j)[1])) for k in (0, 0, 1, 1)]
     out = pl.BlockSpec(blk, lambda j, s: (0, j))
     return call(
-        kernel, (count,),
-        [out] + [head] * 4 + right + [pl.BlockSpec((1, SEP, SEP), lambda j, s: (0, 0, 0))],
+        kernel, (count,), [out] + [head] * 2 + right + [pl.BlockSpec((1, PACKED, DB), lambda j, s: (0, 0, 0))],
         [shape_of((SEP, plan.cols_loc), BF16)] * 2, [out, out],
         [pltpu.VMEM((SEP, SEP), BF16)] * 2 + [pltpu.VMEM((2, SEP, SEP), BF16)] * 2,
-        (scal, panel, *rt[0], *rt[1], *cols[0], *cols[1], inv),
+        (scal, panel, *heads[2:], *cols[0], *cols[1], inv),
         18 * plan.cols_loc * SEP**2, 16 * plan.cols_loc * SEP,
     )
 
@@ -545,13 +598,19 @@
     return [(a, b) for a in range(plan.rows) for b in range(plan.cols)]
 
 
-def row_broadcast(plan, r, value):
+def row_stages(plan, r, value):
     stride = plan.rows // 2
     while stride:
         sent = send(plan, value, [((a, b), (a + stride, b)) for a, b in grid_of(plan) if a % (2 * stride) == 0])
-        value = jnp.where(r % (2 * stride) == stride, sent, value)
+        if stride > 1:
+            value = jnp.where(r % (2 * stride) == stride, sent, value)
         stride //= 2
-    return value
+    return value, sent
+
+
+def row_broadcast(plan, r, value):
+    held, sent = row_stages(plan, r, value)
+    return jnp.where(r % 2 == 1, sent, held)
 
 
 def from_next_row(plan, value):
@@ -562,36 +621,36 @@
     return send(plan, value, [((a, b + 1), (a, b)) for a, b in grid_of(plan) if b + 1 < plan.cols])
 
 
-def swap_cols(plan, value):
-    return send(plan, value, [((a, b), (a, b ^ 1)) for a, b in grid_of(plan)])
-
-
-def swap_rows(plan, value):
-    return send(plan, value, [((a, b), (a ^ 1, b)) for a, b in grid_of(plan)])
-
-
-def spread(plan, r, c, value):
-    place = c // 2
-    up = send(plan, value, [((a, b), (a, b + 2)) for a, b in grid_of(plan) if b // 2 == a and b + 2 < plan.cols])
-    down = send(plan, value, [((a, b), (a, b - 2)) for a, b in grid_of(plan) if b // 2 == a and b >= 2])
-    now = jnp.where(place > r, up, down)
-    out = jnp.where(place == r, value, now)
-    for step in range(2, plan.rows):
-        pairs = []
-        for a, b in grid_of(plan):
-            if b // 2 == a + step - 1 and b + 2 < plan.cols:
-                pairs.append(((a, b), (a, b + 2)))
-            if b // 2 == a - step + 1 and b >= 2:
-                pairs.append(((a, b), (a, b - 2)))
-        now = send(plan, now, pairs)
-        out = jnp.where(jnp.abs(place - r) == step, now, out)
-    return out
-
-
-def lead(plan, c, own, other, count):
-    if count <= plan.cols_loc:
-        return jnp.where(c % 2 == 0, own[:count], other[:count])
-    return jnp.where(c % 2 == 0, jnp.concatenate([own, other]), jnp.concatenate([other, own]))[:count]
+def from_first(plan, r, c, value):
+    strides, stride = [1], plan.cols // 2
+    while stride > 1:
+        strides.append(stride)
+        stride //= 2
+    held = [0]
+    for stride in strides:
+        sent = send(plan, value, [((0, b), (0, b + stride)) for b in held])
+        new = [b + stride for b in held]
+        take = c == new[0]
+        for b in new[1:]:
+            take = take | (c == b)
+        value = jnp.where(take, sent, value)
+        held = held + new
+    return row_broadcast(plan, r, value)
+
+
+def cut_panels(plan, panels):
+    rows, place, axis = plan.rows, lax.axis_index("col") // 2, panels.ndim - 2
+    at = [(place + d) % rows * plan.piece for d in range(rows)]
+    return [lax.dynamic_slice_in_dim(panels, start, plan.piece, axis) for start in at]
+
+
+def gather_rows(plan, parts):
+    rows, mine = plan.rows, 0.0
+    for d, part in enumerate(parts):
+        pairs = [((0, b), (b // 2, (b // 2 + d) % rows * 2 + b % 2)) for b in range(plan.cols)]
+        mine = mine + send(plan, part, pairs)
+    gathered = lax.all_gather(mine, "col", axis=0, tiled=False)
+    return gathered.reshape((rows, 2) + mine.shape)
 
 
 def local(plan, child_fronts, parent_entries, block_map):
@@ -601,39 +660,41 @@
     source = jnp.max(jnp.where(block_map[:, None, :] == targets, slots, -1), axis=2)
     scal = jnp.concatenate([source.reshape(-1), jnp.stack([r, c]).astype(jnp.int32)])
 
+    top = child_fronts[:, :SEP, :]
+    parts = cut_panels(plan, jnp.swapaxes(top, 1, 2))
+    rows = gather_rows(plan, parts)
+    pivots = from_first(plan, r, c, pack_pivots(plan, scal, child_fronts, parts))
     edge_top = from_next_col(plan, edge_sum(plan, scal, child_fronts, None, 0, GAP))
-    after_rows = from_next_row(plan, child_fronts[:, :SEP, :])
-
-    panels, own, other, heads, next_rows = [], [], [], [], []
-    for k in (0, 1):
-        panel = row_broadcast(plan, r, child_fronts[k, :SEP, :])
-        panels.append(panel)
-        own.append(spread(plan, r, c, panel.T))
-        other.append(swap_cols(plan, own[k]))
-        heads.append(row_broadcast(plan, r, lead(plan, c, own[k], other[k], 2 * SEP)))
-        next_rows.append(from_next_row(plan, lead(plan, c, own[k], other[k], SEP)))
-    mine = from_next_col(plan, jnp.where(r % 2 == 0, panels[0][:, :SEP], panels[1][:, :SEP]))
-    theirs = swap_rows(plan, mine)
-    next_cols = [jnp.where(r % 2 == 0, mine, theirs), jnp.where(r % 2 == 0, theirs, mine)]
-
-    panel = row_broadcast(plan, r, panel_start(plan, scal, parent_entries, child_fronts, edge_top))
-    parent_own = spread(plan, r, c, panel.T)
-    parent_other = swap_cols(plan, parent_own)
-    pivot = row_broadcast(plan, r, lead(plan, c, parent_own, parent_other, SEP))
+    after_rows = from_next_row(plan, top)
+    next_cols = send(plan, top[:, :, :SEP], [((0, b + 1), (0, b)) for b in range(plan.cols - 1)])
+    wide = jnp.concatenate([top, next_cols], axis=2)
+    panel = panel_start(plan, scal, parent_entries, child_fronts, edge_top)
+    parent_parts = cut_panels(plan, panel.T)
+
+    inv = child_factor(plan, scal, pivots, (wide, *parent_parts))
+    parent_lines = gather_rows(plan, parent_parts)
+    pinv = from_first(plan, r, c, parent_factor(plan, scal, panel, wide, inv, ()))
+
+    held, sent = row_stages(plan, r, wide)
+    panel = row_broadcast(plan, r, panel)
+    slots = SEP // plan.piece
+    second = divmod(1, plan.half)
+    second = (second[1], second[0])
+    head = row_broadcast(plan, r, rows[second[0] * slots : (second[0] + 1) * slots, second[1]])
+    next_rows = from_next_row(plan, rows[:slots, 0])
 
     edge_rest = from_next_col(
         plan, edge_sum(plan, scal, child_fronts, after_rows, GAP, plan.row_blocks - GAP)
     )
 
-    inv, invt = child_factor(plan, scal, heads[0], heads[1])
-    rt = [child_rows(plan, scal, k, own[k], other[k], next_rows[k], heads[k], invt) for k in (0, 1)]
-    cols = [child_cols(plan, scal, k, panels[k], next_cols[k], heads[k], inv) for k in (0, 1)]
+    rt = [child_rows(plan, scal, k, rows, next_rows, inv) for k in (0, 1)]
+    cols = [child_cols(plan, scal, k, held, sent, inv) for k in (0, 1)]
+    heads = child_heads(plan, scal, head, inv)
     result = child_result(plan, scal, 0, child_fronts, rt[0], cols[0], None)
     result = child_result(plan, scal, 1, child_fronts, rt[1], cols[1], result)
 
-    pinv, pinvt = parent_factor(plan, scal, pivot, rt, cols)
-    prt = parent_rows(plan, scal, parent_own, parent_other, rt, cols, pinvt)
-    pcols = parent_cols(plan, scal, panel, rt, cols, pinv)
+    prt = parent_rows(plan, scal, parent_lines, rt, heads, pinv)
+    pcols = parent_cols(plan, scal, panel, heads, cols, pinv)
     parent = parent_result(
         plan, scal, parent_entries, child_fronts, after_rows, edge_top, edge_rest, rt, cols, prt, pcols
     )

time: 689 us -> 514 us (0.75)
  waiting for transfers between devices: 290 us -> 133 us
  Pallas kernels: 232 us -> 202 us
  other arithmetic: 53.3 us -> 38.8 us
  between operations: 1.52 us -> 14.8 us
  starting transfers between devices: 66.4 us -> 74.7 us
  local copies, waits for them, and re-layouts: 35.7 us -> 42.7 us
    ppermute x34 -> x29, waiting for transfers between devices: 290 us -> 133 us  [send(): return lax.ppermute(value, ('row', 'col'), flat)]
    pallas_call x14 -> x16, Pallas kernels: 232 us -> 202 us  [call(): pl.pallas_call(kernel, out_shape=out_shape, grid_spec=pltpu.PrefetchScala...]
    select_n x24 -> x15, other arithmetic: 52.5 us -> 28.1 us  [the longest x5 15.1 us: row_stages(): value = jnp.where(r % (2 * stride) == stride, sent, value)]
    dynamic_slice x0 -> x5, local copies, waits for them, and re-layouts: none -> 14.6 us  [cut_panels(): lax.dynamic_slice_in_dim(panels, start, plan.piece, axis)]
    ppermute x5 -> x0, local copies, waits for them, and re-layouts: 12.9 us -> none  [send(): return lax.ppermute(value, ('row', 'col'), flat)]
    select_n x6 -> x0, local copies, waits for them, and re-layouts: 11.9 us -> none  [the longest x3 6.7 us: spread(): out = jnp.where(jnp.abs(place - r) == step, now, out)]
    unnamed x29 -> x19, local copies, waits for them, and re-layouts: 1.17 us -> 10 us
    ppermute x34 -> x29, starting transfers between devices: 66.4 us -> 74.6 us  [send(): return lax.ppermute(value, ('row', 'col'), flat)]
  transfers between devices with their start and end apart: 34 -> 31, of which waited for: 11 -> 6; matrix products, arithmetic and copies ran while one was open for 12% -> 11% of each run, Pallas kernels for 29% -> 32%
where the time goes in v2:
time: 514 us; the launch traced here: 506 us
  Pallas kernels  202 us (39%)
  waiting for transfers between devices  133 us (26%)
  starting transfers between devices  74.7 us (15%)
  local copies, waits for them, and re-layouts  42.7 us (8%)
  other arithmetic  38.8 us (8%)
  between operations  14.8 us (3%)
    pallas_call x16, Pallas kernels, call(): pl.pallas_call(kernel, out_shape=out_shape, grid_spec=pltpu.PrefetchScala...  202 us
    ppermute x29, waiting for transfers between devices, send(): return lax.ppermute(value, ('row', 'col'), flat)  133 us
    ppermute x29, starting transfers between devices, send(): return lax.ppermute(value, ('row', 'col'), flat)  74.6 us
    select_n x5, other arithmetic, row_stages(): value = jnp.where(r % (2 * stride) == stride, sent, value)  15.1 us
    dynamic_slice x5, local copies, waits for them, and re-layouts, cut_panels(): lax.dynamic_slice_in_dim(panels, start, plan.piece, axis)  14.6 us
  transfers between devices with their start and end apart: 31, of which 6 were waited for; matrix products, arithmetic and copies ran while one was open for 11% of the time, Pallas kernels for 32%

profile of v2, /device:TPU:14, one launch (start us, length us, event | category | flops | bytes accessed | tf_op | source)
XLA Modules:
  0.0 505.8 jit_solution(16026968273001307262)
XLA Ops:
  7.3 4.8 slice.13
  12.1 4.4 dynamic-slice_bitcast_fusion.2
  16.5 2.5 copy.43.rest_0_
  19.0 2.5 copy.44.rest_1_
  21.6 2.5 copy.45.rest_2_
  25.0 2.6 copy.46.rest_3_
  27.6 3.4 shard_map.50
  31.8 1.5 broadcast_select_fusion.5
  33.3 1.7 collective-permute-start.6
  35.0 1.6 collective-permute-start
  36.6 1.7 collective-permute-start.1
  38.3 1.6 collective-permute-start.2
  41.4 1.7 collective-permute-start.7
  43.2 3.1 slice.15
  47.1 42.4 %collective-permute-done.3 = f32[2,256,512]{1,2,0:T(8,128)} collective-permute-done((f32[2,256,512]{1,2,0:T(8,128)}, f32[2,256,512]{1,2,0:T(8,128)}, u32[]{:S(2)}, u32[]{:S(2)}) %collective-permute-start.3) | collective-permute-done | bytes 1048608 | tf_op jit(solution)/shard_map/ppermute | solution.py:594
  89.5 3.4 add_add_fusion
  92.9 2.5 copy.41
  95.5 2.5 broadcast_select_fusion.7
  99.3 5.5 %pad_maximum_fusion.rest_0_.p_ref = f32[2,512,1536]{2,1,0:T(8,128)} fusion(f32[2,512,512]{2,1,0:T(8,128)S(1)} %collective-permute-done.10, f32[2,512,1024]{2,1,0:T(8,128)} %slice.13), kind=kLoop, calls=%fused_computation | loop fusion | flops 1572864 | bytes 12582912 | tf_op jit(solution)/shard_map/concatenate | solution.py:670
  106.1 30.3 %collective-permute-done.8 = f32[2,1280,128]{2,1,0:T(8,128)} collective-permute-done((f32[2,1280,128]{2,1,0:T(8,128)}, f32[2,1280,128]{2,1,0:T(8,128)}, u32[]{:S(2)}, u32[]{:S(2)}) %collective-permute-start.8) | collective-permute-done | bytes 1310752 | tf_op jit(solution)/shard_map/ppermute | solution.py:594
  136.5 1.4 broadcast_select_fusion.8
  137.9 2.4 collective-permute-start.9
  140.3 3.1 shard_map.51
  143.4 3.0 collective-permute-start.11
  146.4 18.9 %collective-permute-done.11.x_ref.t_ref = f32[512,512]{1,0:T(8,128)} collective-permute-done((f32[512,512]{1,0:T(8,128)}, f32[512,512]{1,0:T(8,128)}, u32[]{:S(2)}, u32[]{:S(2)}) %collective-permute-start.11) | collective-permute-done | bytes 1048608 | tf_op jit(solution)/shard_map/ppermute | solution.py:594
  165.3 5.5 %shard_map.52.m_ref = f32[512,1024]{1,0:T(8,128)} custom-call(s32[66]{0:T(128)} %pad_add_fusion.s, f32[2048,1024]{1,0:T(8,128)} %e_ref.3, f32[2,2048,1024]{2,1,0:T(8,128)} %b_ref.7, f32[2,2048,1024]{2,1,0:T(8,128)} %b_ref.7, f32[512,512]{1,0:T(8,128)} %collective-permute-done.11.x_ref.t_ref), custom_call_target="tpu_custom_call" | custom-call | flops 1000000 | bytes 8388608 | tf_op jit(solution)/shard_map/pallas_call | solution.py:155
  170.8 2.9 constant_dynamic-slice_fusion
  173.7 2.0 copy.55
  175.8 2.0 copy.56
  177.8 2.1 copy.53
  179.9 2.1 copy.54
  183.1 44.0 %shard_map.53.l_ref = f32[2,1280,128]{2,1,0:T(8,128)} custom-call(s32[66]{0:T(128)} %pad_add_fusion.s, f32[2,1280,128]{2,1,0:T(8,128)} %broadcast_select_fusion.9.a_ref, f32[2,512,1536]{2,1,0:T(8,128)} %pad_maximum_fusion.rest_0_.p_ref, f32[256,512]{1,0:T(8,128)} %bitcast.36, f32[256,512]{1,0:T(8,128)} %bitcast.34, f32[256,512]{1,0:T(8,128)} %bitcast.32, ...), custom_call_target="tpu_custom_call" | custom-call | flops 40000000000 | bytes 4194304 | tf_op jit(solution)/shard_map/pallas_call | solution.py:155
  227.1 8.1 %broadcast_select_fusion.h_ref = f32[2,512,1536]{2,1,0:T(8,128)} fusion(f32[2,512,1536]{2,1,0:T(8,128)} %collective-permute-done.12, pred[]{:T(512)S(6)} %eq.76, f32[2,512,512]{2,1,0:T(8,128)S(1)} %collective-permute-done.10, f32[2,512,1024]{2,1,0:T(8,128)} %slice.13), kind=kLoop, calls=%fused_computation.1 | loop fusion | flops 3145728 | bytes 18874368 | tf_op jit(solution)/shard_map/jit(_where)/select_n | solution.py:606
  235.2 4.2 collective-permute-start.13
  239.4 4.2 shard_map.62
  245.7 1.3 collective-permute-start.27
  247.0 29.8 %collective-permute-start.14 = (f32[2,512,1024]{2,1,0:T(8,128)}, f32[2,512,1024]{2,1,0:T(8,128)}, u32[]{:S(2)}, u32[]{:S(2)}) collective-permute-start(f32[2,512,1024]{2,1,0:T(8,128)} %slice.13), channel_id=1, source_target_pairs={{8,0},{9,1},{10,2},{11,3},{12,4},{13,5},{14,6},{15,7},{16,8},{17,9... | collective-permute-start | bytes 12582920 | tf_op jit(solution)/shard_map/ppermute | solution.py:594
  277.6 1.5 collective-permute-start.19
  281.0 8.7 %collective-permute-done.19 = f32[256,512]{1,0:T(8,128)S(1)} collective-permute-done((f32[256,512]{1,0:T(8,128)S(1)}, f32[256,512]{1,0:T(8,128)S(1)}, u32[]{:S(2)}, u32[]{:S(2)}) %collective-permute-start.19) | collective-permute-done | bytes 524320 | tf_op jit(solution)/shard_map/ppermute | solution.py:594
  291.6 14.7 %collective-permute-done.27 = f32[512,1024]{1,0:T(8,128)} collective-permute-done((f32[512,1024]{1,0:T(8,128)S(1)}, f32[512,1024]{1,0:T(8,128)}, u32[]{:S(2)}, u32[]{:S(2)}) %collective-permute-start.27) | collective-permute-done | bytes 2097184 | tf_op jit(solution)/shard_map/ppermute | solution.py:594
  306.3 3.4 broadcast_select_fusion.1
  309.7 2.7 collective-permute-start.28
  312.5 1.3 collective-permute-start.25
  313.8 4.6 slice_bitcast_fusion
  319.7 17.6 %collective-permute-done.25 = f32[1,1280,128]{2,1,0:T(8,128)S(1)} collective-permute-done((f32[1,1280,128]{2,1,0:T(8,128)S(1)}, f32[1,1280,128]{2,1,0:T(8,128)S(1)}, u32[]{:S(2)}, u32[]{:S(2)}) %collective-permute-start.25) | collective-permute-done | bytes 655392 | tf_op jit(solution)/shard_map/ppermute | solution.py:594
  337.3 1.9 collective-permute-start.4
  339.3 3.8 collective-permute-start.26
  343.1 7.0 %shard_map.60 = f32[1536,512]{1,0:T(8,128)} custom-call(s32[66]{0:T(128)} %pad_add_fusion.s, f32[2,2048,1024]{2,1,0:T(8,128)} %b_ref.7, f32[2,2048,1024]{2,1,0:T(8,128)} %b_ref.7, f32[2,512,1024]{2,1,0:T(8,128)} %collective-permute-done.14.rest_0_.rest_1_.xa_ref.xb_ref, f32[2,512,1024]{2,1,0:T(8,128)} %collective-permute-done.14.rest_0_.rest_1_.xa_ref.xb_ref), custom_call_target="tpu_custom_call" | custom-call | flops 1000000 | bytes 12582912 | tf_op jit(solution)/shard_map/pallas_call | solution.py:155
  350.1 1.9 collective-permute-start.15
  352.0 3.6 broadcast_select_fusion.2.p_ref
  356.5 7.3 %shard_map.57 = (bf16[512,1536]{1,0:T(8,128)(2,1)}, bf16[512,1536]{1,0:T(8,128)(2,1)}) custom-call(s32[66]{0:T(128)} %pad_add_fusion.s, f32[2,512,1536]{2,1,0:T(8,128)} %broadcast_select_fusion.h_ref, f32[2,512,1536]{2,1,0:T(8,128)} %collective-permute-done.13.t_ref, f32[2,1280,128]{2,1,0:T(8,128)} %shard_map.53.l_ref), custom_call_target="tpu_custom_call" | custom-call | flops 2415919104 | bytes 6291456 | tf_op jit(solution)/shard_map/pallas_call | solution.py:155
  363.8 2.1 broadcast_select_fusion.3
  365.9 1.7 collective-permute-start.21
  367.6 7.2 %shard_map.55 = (bf16[512,1536]{1,0:T(8,128)(2,1)}, bf16[512,1536]{1,0:T(8,128)(2,1)}) custom-call(s32[66]{0:T(128)} %pad_add_fusion.s, f32[2,512,1536]{2,1,0:T(8,128)} %broadcast_select_fusion.h_ref, f32[2,512,1536]{2,1,0:T(8,128)} %collective-permute-done.13.t_ref, f32[2,1280,128]{2,1,0:T(8,128)} %shard_map.53.l_ref), custom_call_target="tpu_custom_call" | custom-call | flops 2415919104 | bytes 6291456 | tf_op jit(solution)/shard_map/pallas_call | solution.py:155
  374.8 9.5 %shard_map.56 = (bf16[2560,512]{1,0:T(8,128)(2,1)}, bf16[2560,512]{1,0:T(8,128)(2,1)}) custom-call(s32[66]{0:T(128)} %pad_add_fusion.s, f32[4,2,2,256,512]{4,3,2,1,0:T(8,128)} %bitcast.28, f32[2,2,256,512]{3,2,1,0:T(8,128)} %collective-permute-done.4.x_ref, f32[2,1280,128]{2,1,0:T(8,128)} %shard_map.53.l_ref), custom_call_target="tpu_custom_call" | custom-call | flops 4026531840 | bytes 10485760 | tf_op jit(solution)/shard_map/pallas_call | solution.py:155
  384.3 9.5 %shard_map.54 = (bf16[2560,512]{1,0:T(8,128)(2,1)}, bf16[2560,512]{1,0:T(8,128)(2,1)}) custom-call(s32[66]{0:T(128)} %pad_add_fusion.s, f32[4,2,2,256,512]{4,3,2,1,0:T(8,128)} %bitcast.29, f32[2,2,256,512]{3,2,1,0:T(8,128)} %collective-permute-done.4.x_ref, f32[2,1280,128]{2,1,0:T(8,128)} %shard_map.53.l_ref), custom_call_target="tpu_custom_call" | custom-call | flops 4026531840 | bytes 10485760 | tf_op jit(solution)/shard_map/pallas_call | solution.py:155
  393.9 14.3 %shard_map.58.rest_0_ = f32[2,2048,1024]{2,1,0:T(8,128)} custom-call(s32[66]{0:T(128)} %pad_add_fusion.s, f32[2,2048,1024]{2,1,0:T(8,128)} %b_ref.7, bf16[2560,512]{1,0:T(8,128)(2,1)} %get-tuple-element.22.lh.ah, bf16[2560,512]{1,0:T(8,128)(2,1)} %get-tuple-element.23.ll.al, bf16[512,1536]{1,0:T(8,128)(2,1)} %get-tuple-element.24.rh.cah, ...), custom_call_target="tpu_custom_call" | custom-call | flops 6442450944 | bytes 16777216 | tf_op jit(solution)/shard_map/pallas_call | solution.py:155
  408.1 14.3 %shard_map.59 = f32[2,2048,1024]{2,1,0:T(8,128)} custom-call(s32[66]{0:T(128)} %pad_add_fusion.s, f32[2,2048,1024]{2,1,0:T(8,128)} %b_ref.7, bf16[2560,512]{1,0:T(8,128)(2,1)} %get-tuple-element.18.lh.bh, bf16[2560,512]{1,0:T(8,128)(2,1)} %get-tuple-element.19.ll.bl, bf16[512,1536]{1,0:T(8,128)(2,1)} %get-tuple-element.20.rh.cbh, ...), custom_call_target="tpu_custom_call", output_to_operand_aliasing={{}: (6, {})} | custom-call | flops 6442450944 | bytes 16777216 | tf_op jit(solution)/shard_map/pallas_call | solution.py:155
  422.4 1.8 broadcast_select_fusion.4.h_ref
  424.2 5.8 %shard_map.61 = (bf16[2,512,512]{2,1,0:T(8,128)(2,1)}, bf16[2,512,512]{2,1,0:T(8,128)(2,1)}, bf16[2,512,512]{2,1,0:T(8,128)(2,1)}, bf16[2,512,512]{2,1,0:T(8,128)(2,1)}) custom-call(s32[66]{0:T(128)} %pad_add_fusion.s, f32[2,2,256,512]{3,2,1,0:T(8,128)} %broadcast_select_fusion.4.h_ref, f32[2,1280,128]{2,1,0:T(8,128)} %shard_map.53.l_ref), custom_call_target="tpu_custom_call" | custom-call | flops 1610612736 | bytes 4194304 | tf_op jit(solution)/shard_map/pallas_call | solution.py:155
  430.0 13.5 %shard_map.64 = (bf16[512,1024]{1,0:T(8,128)(2,1)}, bf16[512,1024]{1,0:T(8,128)(2,1)}) custom-call(s32[66]{0:T(128)} %pad_add_fusion.s, f32[512,1024]{1,0:T(8,128)} %broadcast_select_fusion.2.p_ref, bf16[2,512,512]{2,1,0:T(8,128)(2,1)} %get-tuple-element.30.th, bf16[2,512,512]{2,1,0:T(8,128)(2,1)} %get-tuple-element.31.tl, ...), custom_call_target="tpu_custom_call" | custom-call | flops 4831838208 | bytes 8388608 | tf_op jit(solution)/shard_map/pallas_call | solution.py:155
  443.5 17.3 %shard_map.63 = (bf16[2048,512]{1,0:T(8,128)(2,1)}, bf16[2048,512]{1,0:T(8,128)(2,1)}) custom-call(s32[66]{0:T(128)} %pad_add_fusion.s, f32[4,2,256,512]{3,2,1,0:T(8,128)} %bitcast.38, bf16[2560,512]{1,0:T(8,128)(2,1)} %get-tuple-element.22.lh.ah, bf16[2560,512]{1,0:T(8,128)(2,1)} %get-tuple-element.23.ll.al, bf16[2560,512]{1,0:T(8,128)(2,1)} %get-tuple-element.18.lh.bh, ...), custom_call_target="tpu_custom_call" | custom-call | flops 9663676416 | bytes 16777216 | tf_op jit(solution)/shard_map/pallas_call | solution.py:155
  460.8 1.7 copy-done.1
  462.5 36.2 %shard_map.65 = f32[2048,1024]{1,0:T(8,128)} custom-call(s32[66]{0:T(128)} %pad_add_fusion.s, f32[2048,1024]{1,0:T(8,128)} %e_ref.3, f32[2,2048,1024]{2,1,0:T(8,128)} %b_ref.7, f32[2,2048,1024]{2,1,0:T(8,128)} %b_ref.7, f32[2,512,1024]{2,1,0:T(8,128)} %collective-permute-done.14.rest_0_.rest_1_.xa_ref.xb_ref, ...), custom_call_target="tpu_custom_call" | custom-call | flops 19327352832 | bytes 50331648 | tf_op jit(solution)/shard_map/pallas_call | solution.py:155
  (67 shorter events, 16.7 us)
Async XLA Ops:
  7.2 306.6 %all-gather.5.cloned.1.call-start = ((), (), s32[]{:S(2)}) async-start(), calls=%async_computation | async-start | bytes 9437184 | tf_op jit(solution)/shard_map/all_gather | solution.py:652
  19.0 5.1 %copy-start.6 = (s32[2,30]{1,0:T(2,128)S(1)}, s32[2,30]{1,0:T(2,128)}, u32[]{:S(2)}) copy-start(s32[2,30]{1,0:T(2,128)} %param.5) | copy-start | bytes 724
  31.1 0.7 collective-permute-start.5
  33.3 8.0 %collective-permute-start.6 = (f32[2,1280,128]{2,1,0:T(8,128)S(1)}, f32[2,1280,128]{2,1,0:T(8,128)}, u32[]{:S(2)}, u32[]{:S(2)}) collective-permute-start(f32[2,1280,128]{2,1,0:T(8,128)S(1)} %broadcast_select_fusion.5), channel_id=1, source_target_pairs={{0,4},{1,5}} | collective-permute-start | bytes 3932168 | tf_op jit(solution)/shard_map/ppermute | solution.py:594
  35.0 11.3 %collective-permute-start = (f32[2,256,512]{1,2,0:T(8,128)}, f32[2,256,512]{1,2,0:T(8,128)}, u32[]{:S(2)}, u32[]{:S(2)}) collective-permute-start(f32[2,256,512]{1,2,0:T(8,128)} %get-tuple-element.39), channel_id=1, source_target_pairs={{0,0},{1,1},{2,10},{3,11},{4,20},{5,21},{6,30},{7,31}} | collective-permute-start | bytes 3145736 | tf_op jit(solution)/shard_map/ppermute | solution.py:594
  36.6 10.4 %collective-permute-start.1 = (f32[2,256,512]{1,2,0:T(8,128)}, f32[2,256,512]{1,2,0:T(8,128)}, u32[]{:S(2)}, u32[]{:S(2)}) collective-permute-start(f32[2,256,512]{1,2,0:T(8,128)} %get-tuple-element.36), channel_id=1, source_target_pairs={{0,2},{1,3},{2,12},{3,13},{4,22},{5,23},{6,24},{7,25}} | collective-permute-start | bytes 3145736 | tf_op jit(solution)/shard_map/ppermute | solution.py:594
  38.3 8.7 %collective-permute-start.2 = (f32[2,256,512]{1,2,0:T(8,128)}, f32[2,256,512]{1,2,0:T(8,128)}, u32[]{:S(2)}, u32[]{:S(2)}) collective-permute-start(f32[2,256,512]{1,2,0:T(8,128)} %get-tuple-element.38), channel_id=1, source_target_pairs={{0,4},{1,5},{2,14},{3,15},{4,16},{5,17},{6,26},{7,27}} | collective-permute-start | bytes 3145736 | tf_op jit(solution)/shard_map/ppermute | solution.py:594
  40.0 49.5 %collective-permute-start.3 = (f32[2,256,512]{1,2,0:T(8,128)}, f32[2,256,512]{1,2,0:T(8,128)}, u32[]{:S(2)}, u32[]{:S(2)}) collective-permute-start(f32[2,256,512]{1,2,0:T(8,128)} %get-tuple-element.37), channel_id=1, source_target_pairs={{0,6},{1,7},{2,8},{3,9},{4,18},{5,19},{6,28},{7,29}} | collective-permute-start | bytes 3145736 | tf_op jit(solution)/shard_map/ppermute | solution.py:594
  41.4 54.1 %collective-permute-start.7 = (f32[2,1280,128]{2,1,0:T(8,128)S(1)}, f32[2,1280,128]{2,1,0:T(8,128)}, u32[]{:S(2)}, u32[]{:S(2)}) collective-permute-start(f32[2,1280,128]{2,1,0:T(8,128)S(1)} %broadcast_select_fusion.6), channel_id=1, source_target_pairs={{0,2},{1,3},{4,6},{5,7}} | collective-permute-start | bytes 3932168 | tf_op jit(solution)/shard_map/ppermute | solution.py:594
  46.3 53.1 %collective-permute-start.10 = (f32[2,512,512]{2,1,0:T(8,128)}, f32[2,512,512]{2,1,0:T(8,128)S(1)}, u32[]{:S(2)}, u32[]{:S(2)}) collective-permute-start(f32[2,512,512]{2,1,0:T(8,128)} %slice.15), channel_id=1, source_target_pairs={{1,0},{2,1},{3,2},{4,3},{5,4},{6,5},{7,6}} | collective-permute-start | bytes 6291464 | tf_op jit(solution)/shard_map/ppermute | solution.py:594
  95.5 348.1 %all-gather.7.cloned.1.call-start = ((), (), s32[]{:S(2)}) async-start(), calls=%async_computation.1 | async-start | bytes 4718592 | tf_op jit(solution)/shard_map/all_gather | solution.py:652
  98.0 38.4 %collective-permute-start.8 = (f32[2,1280,128]{2,1,0:T(8,128)}, f32[2,1280,128]{2,1,0:T(8,128)}, u32[]{:S(2)}, u32[]{:S(2)}) collective-permute-start(f32[2,1280,128]{2,1,0:T(8,128)} %broadcast_select_fusion.7), channel_id=1, source_target_pairs={{0,16},{1,17},{2,18},{3,19},{4,20},{5,21},{6,22},{7,23}} | collective-permute-start | bytes 3932168 | tf_op jit(solution)/shard_map/ppermute | solution.py:594
  104.8 122.3 %collective-permute-start.12 = (f32[2,512,1536]{2,1,0:T(8,128)}, f32[2,512,1536]{2,1,0:T(8,128)}, u32[]{:S(2)}, u32[]{:S(2)}) collective-permute-start(f32[2,512,1536]{2,1,0:T(8,128)} %pad_maximum_fusion.rest_0_.p_ref), channel_id=1, source_target_pairs={{0,16},{1,17},{2,18},{3,19},{4,20},{5,21},{6,22},{7,23}} | collective-permute-start | bytes 18874376 | tf_op jit(solution)/shard_map/ppermute | solution.py:594
  137.9 44.0 %collective-permute-start.9 = (f32[2,1280,128]{2,1,0:T(8,128)S(1)}, f32[2,1280,128]{2,1,0:T(8,128)}, u32[]{:S(2)}, u32[]{:S(2)}) collective-permute-start(f32[2,1280,128]{2,1,0:T(8,128)S(1)} %broadcast_select_fusion.8), channel_id=1, source_target_pairs={{0,8},{1,9},{2,10},{3,11},{4,12},{5,13},{6,14},{7,15},{16,24},{17,... | collective-permute-start | bytes 3932168 | tf_op jit(solution)/shard_map/ppermute | solution.py:594
  143.4 21.9 %collective-permute-start.11 = (f32[512,512]{1,0:T(8,128)}, f32[512,512]{1,0:T(8,128)}, u32[]{:S(2)}, u32[]{:S(2)}) collective-permute-start(f32[512,512]{1,0:T(8,128)} %shard_map.51), channel_id=1, source_target_pairs={{1,0},{2,1},{3,2},{4,3},{5,4},{6,5},{7,6},{9,8},{10,9},{11,10},{12... | collective-permute-start | bytes 3145736 | tf_op jit(solution)/shard_map/ppermute | solution.py:594
  235.2 9.1 %copy-start.5 = (f32[512,256]{0,1:T(8,128)S(1)}, f32[512,256]{0,1:T(8,128)}, u32[]{:S(2)}) copy-start(f32[512,256]{0,1:T(8,128)} %copy.53) | copy-start | bytes 1572868
  235.2 9.8 %copy-start.4 = (f32[512,256]{0,1:T(8,128)S(1)}, f32[512,256]{0,1:T(8,128)}, u32[]{:S(2)}) copy-start(f32[512,256]{0,1:T(8,128)} %copy.54) | copy-start | bytes 1572868
  235.2 10.5 %copy-start = (f32[512,1024]{1,0:T(8,128)S(1)}, f32[512,1024]{1,0:T(8,128)}, u32[]{:S(2)}) copy-start(f32[512,1024]{1,0:T(8,128)} %shard_map.52.m_ref) | copy-start | bytes 6291460
  235.2 41.7 %copy-start.3 = (f32[512,256]{0,1:T(8,128)S(1)}, f32[512,256]{0,1:T(8,128)}, u32[]{:S(2)}) copy-start(f32[512,256]{0,1:T(8,128)} %copy.55) | copy-start | bytes 1572868
  235.2 42.4 %copy-start.2 = (f32[512,256]{0,1:T(8,128)S(1)}, f32[512,256]{0,1:T(8,128)}, u32[]{:S(2)}) copy-start(f32[512,256]{0,1:T(8,128)} %copy.56) | copy-start | bytes 1572868
  235.2 121.3 %collective-permute-start.13 = (f32[2,512,1536]{2,1,0:T(8,128)}, f32[2,512,1536]{2,1,0:T(8,128)}, u32[]{:S(2)}, u32[]{:S(2)}) collective-permute-start(f32[2,512,1536]{2,1,0:T(8,128)} %broadcast_select_fusion.h_ref), channel_id=1, source_target_pairs={{0,8},{1,9},{2,10},{3,11},{4,12},{5,13},{6,14},{7,15},{16,24},{17,... | collective-permute-start | bytes 18874376 | tf_op jit(solution)/shard_map/ppermute | solution.py:594
  243.6 34.0 %collective-permute-start.22 = (f32[1,1280,128]{2,1,0:T(8,128)}, f32[1,1280,128]{2,1,0:T(8,128)S(1)}, u32[]{:S(2)}, u32[]{:S(2)}) collective-permute-start(f32[1,1280,128]{2,1,0:T(8,128)} %shard_map.62), channel_id=1, source_target_pairs={{0,1}} | collective-permute-start | bytes 1966088 | tf_op jit(solution)/shard_map/ppermute | solution.py:594
  244.3 2.7 collective-permute-start.16
  245.0 31.9 %collective-permute-start.17 = (f32[256,512]{1,0:T(8,128)S(1)}, f32[256,512]{1,0:T(8,128)S(1)}, u32[]{:S(2)}, u32[]{:S(2)}) collective-permute-start(f32[256,512]{1,0:T(8,128)S(1)} %bitcast.35), channel_id=1, source_target_pairs={{0,2},{1,3},{2,12},{3,13},{4,22},{5,23},{6,24},{7,25}} | collective-permute-start | bytes 1572872 | tf_op jit(solution)/shard_map/ppermute | solution.py:594
  245.7 60.6 %collective-permute-start.27 = (f32[512,1024]{1,0:T(8,128)S(1)}, f32[512,1024]{1,0:T(8,128)}, u32[]{:S(2)}, u32[]{:S(2)}) collective-permute-start(f32[512,1024]{1,0:T(8,128)S(1)} %copy-done), channel_id=1, source_target_pairs={{0,16},{1,17},{2,18},{3,19},{4,20},{5,21},{6,22},{7,23}} | collective-permute-start | bytes 6291464 | tf_op jit(solution)/shard_map/ppermute | solution.py:594
  247.0 92.3 %collective-permute-start.14 = (f32[2,512,1024]{2,1,0:T(8,128)}, f32[2,512,1024]{2,1,0:T(8,128)}, u32[]{:S(2)}, u32[]{:S(2)}) collective-permute-start(f32[2,512,1024]{2,1,0:T(8,128)} %slice.13), channel_id=1, source_target_pairs={{8,0},{9,1},{10,2},{11,3},{12,4},{13,5},{14,6},{15,7},{16,8},{17,9... | collective-permute-start | bytes 12582920 | tf_op jit(solution)/shard_map/ppermute | solution.py:594
  276.9 3.4 collective-permute-start.18
  277.6 12.1 %collective-permute-start.19 = (f32[256,512]{1,0:T(8,128)S(1)}, f32[256,512]{1,0:T(8,128)S(1)}, u32[]{:S(2)}, u32[]{:S(2)}) collective-permute-start(f32[256,512]{1,0:T(8,128)S(1)} %bitcast.31), channel_id=1, source_target_pairs={{0,6},{1,7},{2,8},{3,9},{4,18},{5,19},{6,28},{7,29}} | collective-permute-start | bytes 1572872 | tf_op jit(solution)/shard_map/ppermute | solution.py:594
  280.3 10.5 %collective-permute-start.23 = (f32[1,1280,128]{2,1,0:T(8,128)S(1)}, f32[1,1280,128]{2,1,0:T(8,128)S(1)}, u32[]{:S(2)}, u32[]{:S(2)}) collective-permute-start(f32[1,1280,128]{2,1,0:T(8,128)S(1)} %broadcast_select_fusion.10), channel_id=1, source_target_pairs={{0,4},{1,5}} | collective-permute-start | bytes 1966088 | tf_op jit(solution)/shard_map/ppermute | solution.py:594
  290.9 21.5 %collective-permute-start.24 = (f32[1,1280,128]{2,1,0:T(8,128)S(1)}, f32[1,1280,128]{2,1,0:T(8,128)S(1)}, u32[]{:S(2)}, u32[]{:S(2)}) collective-permute-start(f32[1,1280,128]{2,1,0:T(8,128)S(1)} %broadcast_select_fusion.11), channel_id=1, source_target_pairs={{0,2},{1,3},{4,6},{5,7}} | collective-permute-start | bytes 1966088 | tf_op jit(solution)/shard_map/ppermute | solution.py:594
  309.7 40.4 %collective-permute-start.28 = (f32[512,1024]{1,0:T(8,128)}, f32[512,1024]{1,0:T(8,128)}, u32[]{:S(2)}, u32[]{:S(2)}) collective-permute-start(f32[512,1024]{1,0:T(8,128)} %broadcast_select_fusion.1), channel_id=1, source_target_pairs={{0,8},{1,9},{2,10},{3,11},{4,12},{5,13},{6,14},{7,15},{16,24},{17,... | collective-permute-start | bytes 6291464 | tf_op jit(solution)/shard_map/ppermute | solution.py:594
  312.5 24.9 %collective-permute-start.25 = (f32[1,1280,128]{2,1,0:T(8,128)S(1)}, f32[1,1280,128]{2,1,0:T(8,128)S(1)}, u32[]{:S(2)}, u32[]{:S(2)}) collective-permute-start(f32[1,1280,128]{2,1,0:T(8,128)S(1)} %broadcast_select_fusion.12), channel_id=1, source_target_pairs={{0,16},{1,17},{2,18},{3,19},{4,20},{5,21},{6,22},{7,23}} | collective-permute-start | bytes 1966088 | tf_op jit(solution)/shard_map/ppermute | solution.py:594
  318.4 45.4 %collective-permute-start.20 = (f32[2,2,256,512]{3,2,1,0:T(8,128)}, f32[2,2,256,512]{3,2,1,0:T(8,128)S(1)}, u32[]{:S(2)}, u32[]{:S(2)}) collective-permute-start(f32[2,2,256,512]{3,2,1,0:T(8,128)} %get-tuple-element.34), channel_id=1, source_target_pairs={{0,16},{1,17},{2,18},{3,19},{4,20},{5,21},{6,22},{7,23}} | collective-permute-start | bytes 6291464 | tf_op jit(solution)/shard_map/ppermute | solution.py:594
  337.3 37.5 %collective-permute-start.4 = (f32[2,2,256,512]{3,2,1,0:T(8,128)}, f32[2,2,256,512]{3,2,1,0:T(8,128)}, u32[]{:S(2)}, u32[]{:S(2)}) collective-permute-start(f32[2,2,256,512]{3,2,1,0:T(8,128)} %get-tuple-element.35), channel_id=1, source_target_pairs={{8,0},{9,1},{10,2},{11,3},{12,4},{13,5},{14,6},{15,7},{16,8},{17,9... | collective-permute-start | bytes 6291464 | tf_op jit(solution)/shard_map/ppermute | solution.py:594
  339.3 16.3 %collective-permute-start.26 = (f32[1,1280,128]{2,1,0:T(8,128)S(1)}, f32[1,1280,128]{2,1,0:T(8,128)S(1)}, u32[]{:S(2)}, u32[]{:S(2)}) collective-permute-start(f32[1,1280,128]{2,1,0:T(8,128)S(1)} %broadcast_select_fusion.13), channel_id=1, source_target_pairs={{0,8},{1,9},{2,10},{3,11},{4,12},{5,13},{6,14},{7,15},{16,24},{17,... | collective-permute-start | bytes 1966088 | tf_op jit(solution)/shard_map/ppermute | solution.py:594
  350.1 110.7 %collective-permute-start.15 = (f32[1536,512]{1,0:T(8,128)}, f32[1536,512]{1,0:T(8,128)S(1)}, u32[]{:S(2)}, u32[]{:S(2)}) collective-permute-start(f32[1536,512]{1,0:T(8,128)} %shard_map.60), channel_id=1, source_target_pairs={{1,0},{2,1},{3,2},{4,3},{5,4},{6,5},{7,6},{9,8},{10,9},{11,10},{12... | collective-permute-start | bytes 9437192 | tf_op jit(solution)/shard_map/ppermute | solution.py:594
  365.9 56.4 %collective-permute-start.21 = (f32[2,2,256,512]{3,2,1,0:T(8,128)S(1)}, f32[2,2,256,512]{3,2,1,0:T(8,128)S(1)}, u32[]{:S(2)}, u32[]{:S(2)}) collective-permute-start(f32[2,2,256,512]{3,2,1,0:T(8,128)S(1)} %broadcast_select_fusion.3), channel_id=1, source_target_pairs={{0,8},{1,9},{2,10},{3,11},{4,12},{5,13},{6,14},{7,15},{16,24},{17,... | collective-permute-start | bytes 6291464 | tf_op jit(solution)/shard_map/ppermute | solution.py:594
  460.8 1.7 copy-start.1
Sparse Core Ops, SparseCore 0:
  95.6 140.2 all-gather.4
  290.9 108.7 all-gather.6

commit v3 on v2

--- a/solution.py
+++ b/solution.py
@@ -425,12 +425,11 @@
     def kernel(s, a_ref, lh, ll, rh, rl, *rest):
         out_ref = rest[-1]
         i = pl.program_id(0)
-        top = (plan.r(s) == 0) & (i < GAP)
+        top = (plan.r(s) == 0) & (i == 0)
 
         @pl.when(top)
         def _():
-            rows = pl.ds(pl.multiple_of(jnp.minimum(i, GAP - 1) * BLK, BLK), BLK)
-            out_ref[0] = rh[rows, :].astype(F32) + rl[rows, :].astype(F32)
+            out_ref[0] = rh[...].astype(F32) + rl[...].astype(F32)
 
         @pl.when(jnp.logical_not(top))
         def _():
@@ -438,15 +437,15 @@
 
             @pl.when(plan.c(s) == 0)
             def _():
-                out_ref[0, :, pl.ds(0, SEP)] = jnp.zeros((BLK, SEP), F32)
-
-    block = pl.BlockSpec((1, BLK, wide), lambda i, s: (k, i, 0))
-    left = pl.BlockSpec((BLK, SEP), lambda i, s: (i, 0))
+                out_ref[0, :, pl.ds(0, SEP)] = jnp.zeros((SEP, SEP), F32)
+
+    block = pl.BlockSpec((1, SEP, wide), lambda i, s: (k, i, 0))
+    left = pl.BlockSpec((SEP, SEP), lambda i, s: (i, 0))
     right = pl.BlockSpec((SEP, wide), lambda i, s: (0, 0))
     extra_specs = [] if result is None else [pl.BlockSpec(memory_space=pl.ANY)]
     extra = [] if result is None else [result]
     return call(
-        kernel, (plan.row_blocks,), [block, left, left, right, right] + extra_specs,
+        kernel, (plan.rows_loc // SEP,), [block, left, left, right, right] + extra_specs,
         shape_of(fronts.shape), block, [], (scal, fronts, *rt, *cols, *extra),
         6 * plan.rows_loc * wide * SEP, 8 * plan.rows_loc * wide,
         aliases={} if result is None else {6: 0},
@@ -663,7 +662,7 @@
     top = child_fronts[:, :SEP, :]
     parts = cut_panels(plan, jnp.swapaxes(top, 1, 2))
     rows = gather_rows(plan, parts)
-    pivots = from_first(plan, r, c, pack_pivots(plan, scal, child_fronts, parts))
+    pivots = from_first(plan, r, c, pack_pivots(plan, scal, child_fronts, parts[:1]))
     edge_top = from_next_col(plan, edge_sum(plan, scal, child_fronts, None, 0, GAP))
     after_rows = from_next_row(plan, top)
     next_cols = send(plan, top[:, :, :SEP], [((0, b + 1), (0, b)) for b in range(plan.cols - 1)])
@@ -671,7 +670,7 @@
     panel = panel_start(plan, scal, parent_entries, child_fronts, edge_top)
     parent_parts = cut_panels(plan, panel.T)
 
-    inv = child_factor(plan, scal, pivots, (wide, *parent_parts))
+    inv = child_factor(plan, scal, pivots, (wide, parent_parts[0]))
     parent_lines = gather_rows(plan, parent_parts)
     pinv = from_first(plan, r, c, parent_factor(plan, scal, panel, wide, inv, ()))
 

time: 514 us -> 503 us (0.979)
  local copies, waits for them, and re-layouts: 42.7 us -> 32.9 us
    dynamic_slice x5 -> x2, local copies, waits for them, and re-layouts: 14.6 us -> 6.91 us  [cut_panels(): lax.dynamic_slice_in_dim(panels, start, plan.piece, axis)]
where the time goes in v3:
time: 503 us; the launch traced here: 497 us
  Pallas kernels  201 us (40%)
  waiting for transfers between devices  134 us (27%)
  starting transfers between devices  75.3 us (15%)
  other arithmetic  38.6 us (8%)
  local copies, waits for them, and re-layouts  32.9 us (7%)
  between operations  14.8 us (3%)
    pallas_call x16, Pallas kernels, call(): pl.pallas_call(kernel, out_shape=out_shape, grid_spec=pltpu.PrefetchScala...  201 us
    ppermute x29, waiting for transfers between devices, send(): return lax.ppermute(value, ('row', 'col'), flat)  134 us
    ppermute x29, starting transfers between devices, send(): return lax.ppermute(value, ('row', 'col'), flat)  75.2 us
    select_n x5, other arithmetic, row_stages(): value = jnp.where(r % (2 * stride) == stride, sent, value)  13.8 us
  transfers between devices with their start and end apart: 31, of which 6 were waited for; matrix products, arithmetic and copies ran while one was open for 11% of the time, Pallas kernels for 32%

profile of v3, /device:TPU:14, one launch (start us, length us, event | category | flops | bytes accessed | tf_op | source)
XLA Modules:
  0.0 497.0 jit_solution(14699428886037479203)
XLA Ops:
  7.3 4.8 slice.13
  13.0 4.4 dynamic-slice_bitcast_fusion.2
  17.4 2.5 copy.34.rest_0_
  19.9 3.4 shard_map.50
  24.1 1.5 broadcast_select_fusion.5
  25.6 1.7 collective-permute-start.6
  27.3 1.6 collective-permute-start
  28.9 1.7 collective-permute-start.1
  30.6 1.6 collective-permute-start.2
  32.2 1.3 collective-permute-start.3
  33.7 1.7 collective-permute-start.7
  35.4 3.1 slice.15
  39.3 42.4 %collective-permute-done.3 = f32[2,256,512]{1,2,0:T(8,128)} collective-permute-done((f32[2,256,512]{1,2,0:T(8,128)}, f32[2,256,512]{1,2,0:T(8,128)}, u32[]{:S(2)}, u32[]{:S(2)}) %collective-permute-start.3) | collective-permute-done | bytes 1048608 | tf_op jit(solution)/shard_map/ppermute | solution.py:593
  81.8 3.4 add_add_fusion
  85.2 2.5 copy.32
  87.8 2.5 broadcast_select_fusion.7
  91.6 5.5 %pad_maximum_fusion.rest_0_.p_ref = f32[2,512,1536]{2,1,0:T(8,128)} fusion(f32[2,512,512]{2,1,0:T(8,128)S(1)} %collective-permute-done.10, f32[2,512,1024]{2,1,0:T(8,128)} %slice.13), kind=kLoop, calls=%fused_computation | loop fusion | flops 1572864 | bytes 12582912 | tf_op jit(solution)/shard_map/concatenate | solution.py:669
  98.4 30.4 %collective-permute-done.8 = f32[2,1280,128]{2,1,0:T(8,128)} collective-permute-done((f32[2,1280,128]{2,1,0:T(8,128)}, f32[2,1280,128]{2,1,0:T(8,128)}, u32[]{:S(2)}, u32[]{:S(2)}) %collective-permute-start.8) | collective-permute-done | bytes 1310752 | tf_op jit(solution)/shard_map/ppermute | solution.py:593
  128.8 1.4 broadcast_select_fusion.8
  130.2 2.4 collective-permute-start.9
  132.6 3.1 shard_map.51
  135.7 3.0 collective-permute-start.11
  138.7 18.9 %collective-permute-done.11.x_ref.t_ref = f32[512,512]{1,0:T(8,128)} collective-permute-done((f32[512,512]{1,0:T(8,128)}, f32[512,512]{1,0:T(8,128)}, u32[]{:S(2)}, u32[]{:S(2)}) %collective-permute-start.11) | collective-permute-done | bytes 1048608 | tf_op jit(solution)/shard_map/ppermute | solution.py:593
  157.6 5.5 %shard_map.52.m_ref = f32[512,1024]{1,0:T(8,128)} custom-call(s32[66]{0:T(128)} %pad_add_fusion.s, f32[2048,1024]{1,0:T(8,128)} %e_ref.3, f32[2,2048,1024]{2,1,0:T(8,128)} %b_ref.7, f32[2,2048,1024]{2,1,0:T(8,128)} %b_ref.7, f32[512,512]{1,0:T(8,128)} %collective-permute-done.11.x_ref.t_ref), custom_call_target="tpu_custom_call" | custom-call | flops 1000000 | bytes 8388608 | tf_op jit(solution)/shard_map/pallas_call | solution.py:155
  163.1 2.9 constant_dynamic-slice_fusion.2
  165.9 2.0 copy.41
  169.2 44.5 %shard_map.53.l_ref = f32[2,1280,128]{2,1,0:T(8,128)} custom-call(s32[66]{0:T(128)} %pad_add_fusion.s, f32[2,1280,128]{2,1,0:T(8,128)} %broadcast_select_fusion.9.a_ref, f32[2,512,1536]{2,1,0:T(8,128)} %pad_maximum_fusion.rest_0_.p_ref, f32[256,512]{1,0:T(8,128)} %bitcast.8.rest_1_), custom_call_target="tpu_custom_call" | custom-call | flops 40000000000 | bytes 4194304 | tf_op jit(solution)/shard_map/pallas_call | solution.py:155
  213.7 6.9 %broadcast_select_fusion.h_ref = f32[2,512,1536]{2,1,0:T(8,128)} fusion(f32[2,512,1536]{2,1,0:T(8,128)} %collective-permute-done.12, pred[]{:T(512)S(6)} %eq.76, f32[2,512,512]{2,1,0:T(8,128)S(1)} %collective-permute-done.10, f32[2,512,1024]{2,1,0:T(8,128)S(1)} %copy-done), kind=kLoop, calls=%fused_computation.1 | loop fusion | flops 3145728 | bytes 18874368 | tf_op jit(solution)/shard_map/jit(_where)/select_n | solution.py:605
  220.6 4.2 collective-permute-start.13
  224.8 4.2 shard_map.62
  229.1 1.7 collective-permute-start.22
  230.7 1.5 collective-permute-start.16
  232.2 2.0 copy.42
  234.2 1.5 collective-permute-start.17
  235.7 1.3 collective-permute-start.27
  237.0 25.7 %collective-permute-start.14 = (f32[2,512,1024]{2,1,0:T(8,128)}, f32[2,512,1024]{2,1,0:T(8,128)}, u32[]{:S(2)}, u32[]{:S(2)}) collective-permute-start(f32[2,512,1024]{2,1,0:T(8,128)} %slice.13), channel_id=1, source_target_pairs={{8,0},{9,1},{10,2},{11,3},{12,4},{13,5},{14,6},{15,7},{16,8},{17,9... | collective-permute-start | bytes 12582920 | tf_op jit(solution)/shard_map/ppermute | solution.py:593
  265.5 1.3 collective-permute-start.19
  268.7 9.1 %collective-permute-done.19 = f32[256,512]{1,0:T(8,128)S(1)} collective-permute-done((f32[256,512]{1,0:T(8,128)}, f32[256,512]{1,0:T(8,128)S(1)}, u32[]{:S(2)}, u32[]{:S(2)}) %collective-permute-start.19) | collective-permute-done | bytes 524320 | tf_op jit(solution)/shard_map/ppermute | solution.py:593
  277.8 2.3 add_add_fusion.1
  280.9 13.8 %collective-permute-done.27 = f32[512,1024]{1,0:T(8,128)} collective-permute-done((f32[512,1024]{1,0:T(8,128)S(1)}, f32[512,1024]{1,0:T(8,128)}, u32[]{:S(2)}, u32[]{:S(2)}) %collective-permute-start.27) | collective-permute-done | bytes 2097184 | tf_op jit(solution)/shard_map/ppermute | solution.py:593
  294.6 3.3 broadcast_select_fusion.1
  297.9 2.6 collective-permute-start.28
  300.6 1.3 collective-permute-start.25
  301.9 4.7 slice_bitcast_fusion
  307.9 19.8 %collective-permute-done.25 = f32[1,1280,128]{2,1,0:T(8,128)S(1)} collective-permute-done((f32[1,1280,128]{2,1,0:T(8,128)S(1)}, f32[1,1280,128]{2,1,0:T(8,128)S(1)}, u32[]{:S(2)}, u32[]{:S(2)}) %collective-permute-start.25) | collective-permute-done | bytes 655392 | tf_op jit(solution)/shard_map/ppermute | solution.py:593
  327.7 1.9 collective-permute-start.4
  329.7 3.8 collective-permute-start.26
  333.5 7.0 %shard_map.60 = f32[1536,512]{1,0:T(8,128)} custom-call(s32[66]{0:T(128)} %pad_add_fusion.s, f32[2,2048,1024]{2,1,0:T(8,128)} %b_ref.7, f32[2,2048,1024]{2,1,0:T(8,128)} %b_ref.7, f32[2,512,1024]{2,1,0:T(8,128)} %collective-permute-done.14.rest_0_.rest_1_.xa_ref.xb_ref, f32[2,512,1024]{2,1,0:T(8,128)} %collective-permute-done.14.rest_0_.rest_1_.xa_ref.xb_ref), custom_call_target="tpu_custom_call" | custom-call | flops 1000000 | bytes 12582912 | tf_op jit(solution)/shard_map/pallas_call | solution.py:155
  340.4 4.3 collective-permute-start.15
  344.8 3.5 broadcast_select_fusion.2.p_ref
  349.2 7.2 %shard_map.57 = (bf16[512,1536]{1,0:T(8,128)(2,1)}, bf16[512,1536]{1,0:T(8,128)(2,1)}) custom-call(s32[66]{0:T(128)} %pad_add_fusion.s, f32[2,512,1536]{2,1,0:T(8,128)} %broadcast_select_fusion.h_ref, f32[2,512,1536]{2,1,0:T(8,128)} %collective-permute-done.13.t_ref, f32[2,1280,128]{2,1,0:T(8,128)} %shard_map.53.l_ref), custom_call_target="tpu_custom_call" | custom-call | flops 2415919104 | bytes 6291456 | tf_op jit(solution)/shard_map/pallas_call | solution.py:155
  356.4 2.1 broadcast_select_fusion.3
  358.5 1.6 collective-permute-start.21
  360.2 7.2 %shard_map.55 = (bf16[512,1536]{1,0:T(8,128)(2,1)}, bf16[512,1536]{1,0:T(8,128)(2,1)}) custom-call(s32[66]{0:T(128)} %pad_add_fusion.s, f32[2,512,1536]{2,1,0:T(8,128)} %broadcast_select_fusion.h_ref, f32[2,512,1536]{2,1,0:T(8,128)} %collective-permute-done.13.t_ref, f32[2,1280,128]{2,1,0:T(8,128)} %shard_map.53.l_ref), custom_call_target="tpu_custom_call" | custom-call | flops 2415919104 | bytes 6291456 | tf_op jit(solution)/shard_map/pallas_call | solution.py:155
  367.3 9.5 %shard_map.56 = (bf16[2560,512]{1,0:T(8,128)(2,1)}, bf16[2560,512]{1,0:T(8,128)(2,1)}) custom-call(s32[66]{0:T(128)} %pad_add_fusion.s, f32[4,2,2,256,512]{4,3,2,1,0:T(8,128)} %bitcast.28, f32[2,2,256,512]{3,2,1,0:T(8,128)} %collective-permute-done.4.x_ref, f32[2,1280,128]{2,1,0:T(8,128)} %shard_map.53.l_ref), custom_call_target="tpu_custom_call" | custom-call | flops 4026531840 | bytes 10485760 | tf_op jit(solution)/shard_map/pallas_call | solution.py:155
  376.8 9.5 %shard_map.54 = (bf16[2560,512]{1,0:T(8,128)(2,1)}, bf16[2560,512]{1,0:T(8,128)(2,1)}) custom-call(s32[66]{0:T(128)} %pad_add_fusion.s, f32[4,2,2,256,512]{4,3,2,1,0:T(8,128)} %bitcast.29, f32[2,2,256,512]{3,2,1,0:T(8,128)} %collective-permute-done.4.x_ref, f32[2,1280,128]{2,1,0:T(8,128)} %shard_map.53.l_ref), custom_call_target="tpu_custom_call" | custom-call | flops 4026531840 | bytes 10485760 | tf_op jit(solution)/shard_map/pallas_call | solution.py:155
  386.3 12.9 %shard_map.58.rest_0_ = f32[2,2048,1024]{2,1,0:T(8,128)} custom-call(s32[66]{0:T(128)} %pad_add_fusion.s, f32[2,2048,1024]{2,1,0:T(8,128)} %b_ref.7, bf16[2560,512]{1,0:T(8,128)(2,1)} %get-tuple-element.22.lh.ah, bf16[2560,512]{1,0:T(8,128)(2,1)} %get-tuple-element.23.ll.al, bf16[512,1536]{1,0:T(8,128)(2,1)} %get-tuple-element.24.rh.cah, ...), custom_call_target="tpu_custom_call" | custom-call | flops 6442450944 | bytes 16777216 | tf_op jit(solution)/shard_map/pallas_call | solution.py:155
  399.2 12.9 %shard_map.59 = f32[2,2048,1024]{2,1,0:T(8,128)} custom-call(s32[66]{0:T(128)} %pad_add_fusion.s, f32[2,2048,1024]{2,1,0:T(8,128)} %b_ref.7, bf16[2560,512]{1,0:T(8,128)(2,1)} %get-tuple-element.18.lh.bh, bf16[2560,512]{1,0:T(8,128)(2,1)} %get-tuple-element.19.ll.bl, bf16[512,1536]{1,0:T(8,128)(2,1)} %get-tuple-element.20.rh.cbh, ...), custom_call_target="tpu_custom_call", output_to_operand_aliasing={{}: (6, {})} | custom-call | flops 6442450944 | bytes 16777216 | tf_op jit(solution)/shard_map/pallas_call | solution.py:155
  412.1 1.9 broadcast_select_fusion.4.h_ref
  414.1 5.8 %shard_map.61 = (bf16[2,512,512]{2,1,0:T(8,128)(2,1)}, bf16[2,512,512]{2,1,0:T(8,128)(2,1)}, bf16[2,512,512]{2,1,0:T(8,128)(2,1)}, bf16[2,512,512]{2,1,0:T(8,128)(2,1)}) custom-call(s32[66]{0:T(128)} %pad_add_fusion.s, f32[2,2,256,512]{3,2,1,0:T(8,128)} %broadcast_select_fusion.4.h_ref, f32[2,1280,128]{2,1,0:T(8,128)} %shard_map.53.l_ref), custom_call_target="tpu_custom_call" | custom-call | flops 1610612736 | bytes 4194304 | tf_op jit(solution)/shard_map/pallas_call | solution.py:155
  419.8 13.6 %shard_map.64 = (bf16[512,1024]{1,0:T(8,128)(2,1)}, bf16[512,1024]{1,0:T(8,128)(2,1)}) custom-call(s32[66]{0:T(128)} %pad_add_fusion.s, f32[512,1024]{1,0:T(8,128)} %broadcast_select_fusion.2.p_ref, bf16[2,512,512]{2,1,0:T(8,128)(2,1)} %get-tuple-element.30.th, bf16[2,512,512]{2,1,0:T(8,128)(2,1)} %get-tuple-element.31.tl, ...), custom_call_target="tpu_custom_call" | custom-call | flops 4831838208 | bytes 8388608 | tf_op jit(solution)/shard_map/pallas_call | solution.py:155
  433.5 17.2 %shard_map.63 = (bf16[2048,512]{1,0:T(8,128)(2,1)}, bf16[2048,512]{1,0:T(8,128)(2,1)}) custom-call(s32[66]{0:T(128)} %pad_add_fusion.s, f32[4,2,256,512]{3,2,1,0:T(8,128)} %bitcast.32, bf16[2560,512]{1,0:T(8,128)(2,1)} %get-tuple-element.22.lh.ah, bf16[2560,512]{1,0:T(8,128)(2,1)} %get-tuple-element.23.ll.al, bf16[2560,512]{1,0:T(8,128)(2,1)} %get-tuple-element.18.lh.bh, ...), custom_call_target="tpu_custom_call" | custom-call | flops 9663676416 | bytes 16777216 | tf_op jit(solution)/shard_map/pallas_call | solution.py:155
  450.7 1.7 copy-done.2
  452.4 37.5 %shard_map.65 = f32[2048,1024]{1,0:T(8,128)} custom-call(s32[66]{0:T(128)} %pad_add_fusion.s, f32[2048,1024]{1,0:T(8,128)} %e_ref.3, f32[2,2048,1024]{2,1,0:T(8,128)} %b_ref.7, f32[2,2048,1024]{2,1,0:T(8,128)} %b_ref.7, f32[2,512,1024]{2,1,0:T(8,128)} %collective-permute-done.14.rest_0_.rest_1_.xa_ref.xb_ref, ...), custom_call_target="tpu_custom_call" | custom-call | flops 19327352832 | bytes 50331648 | tf_op jit(solution)/shard_map/pallas_call | solution.py:155
  (62 shorter events, 14.2 us)
Async XLA Ops:
  7.2 294.7 %all-gather.5.cloned.1.call-start = ((), (), s32[]{:S(2)}) async-start(), calls=%async_computation | async-start | bytes 9437184 | tf_op jit(solution)/shard_map/all_gather | solution.py:651
  7.3 4.8 copy-start.5
  23.4 0.7 collective-permute-start.5
  25.6 8.0 %collective-permute-start.6 = (f32[2,1280,128]{2,1,0:T(8,128)S(1)}, f32[2,1280,128]{2,1,0:T(8,128)}, u32[]{:S(2)}, u32[]{:S(2)}) collective-permute-start(f32[2,1280,128]{2,1,0:T(8,128)S(1)} %broadcast_select_fusion.5), channel_id=1, source_target_pairs={{0,4},{1,5}} | collective-permute-start | bytes 3932168 | tf_op jit(solution)/shard_map/ppermute | solution.py:593
  27.3 11.2 %collective-permute-start = (f32[2,256,512]{1,2,0:T(8,128)}, f32[2,256,512]{1,2,0:T(8,128)}, u32[]{:S(2)}, u32[]{:S(2)}) collective-permute-start(f32[2,256,512]{1,2,0:T(8,128)} %get-tuple-element.39), channel_id=1, source_target_pairs={{0,0},{1,1},{2,10},{3,11},{4,20},{5,21},{6,30},{7,31}} | collective-permute-start | bytes 3145736 | tf_op jit(solution)/shard_map/ppermute | solution.py:593
  28.9 10.4 %collective-permute-start.1 = (f32[2,256,512]{1,2,0:T(8,128)}, f32[2,256,512]{1,2,0:T(8,128)}, u32[]{:S(2)}, u32[]{:S(2)}) collective-permute-start(f32[2,256,512]{1,2,0:T(8,128)} %get-tuple-element.36), channel_id=1, source_target_pairs={{0,2},{1,3},{2,12},{3,13},{4,22},{5,23},{6,24},{7,25}} | collective-permute-start | bytes 3145736 | tf_op jit(solution)/shard_map/ppermute | solution.py:593
  30.6 8.7 %collective-permute-start.2 = (f32[2,256,512]{1,2,0:T(8,128)}, f32[2,256,512]{1,2,0:T(8,128)}, u32[]{:S(2)}, u32[]{:S(2)}) collective-permute-start(f32[2,256,512]{1,2,0:T(8,128)} %get-tuple-element.38), channel_id=1, source_target_pairs={{0,4},{1,5},{2,14},{3,15},{4,16},{5,17},{6,26},{7,27}} | collective-permute-start | bytes 3145736 | tf_op jit(solution)/shard_map/ppermute | solution.py:593
  32.2 49.5 %collective-permute-start.3 = (f32[2,256,512]{1,2,0:T(8,128)}, f32[2,256,512]{1,2,0:T(8,128)}, u32[]{:S(2)}, u32[]{:S(2)}) collective-permute-start(f32[2,256,512]{1,2,0:T(8,128)} %get-tuple-element.37), channel_id=1, source_target_pairs={{0,6},{1,7},{2,8},{3,9},{4,18},{5,19},{6,28},{7,29}} | collective-permute-start | bytes 3145736 | tf_op jit(solution)/shard_map/ppermute | solution.py:593
  33.7 54.1 %collective-permute-start.7 = (f32[2,1280,128]{2,1,0:T(8,128)S(1)}, f32[2,1280,128]{2,1,0:T(8,128)}, u32[]{:S(2)}, u32[]{:S(2)}) collective-permute-start(f32[2,1280,128]{2,1,0:T(8,128)S(1)} %broadcast_select_fusion.6), channel_id=1, source_target_pairs={{0,2},{1,3},{4,6},{5,7}} | collective-permute-start | bytes 3932168 | tf_op jit(solution)/shard_map/ppermute | solution.py:593
  38.5 53.1 %collective-permute-start.10 = (f32[2,512,512]{2,1,0:T(8,128)}, f32[2,512,512]{2,1,0:T(8,128)S(1)}, u32[]{:S(2)}, u32[]{:S(2)}) collective-permute-start(f32[2,512,512]{2,1,0:T(8,128)} %slice.15), channel_id=1, source_target_pairs={{1,0},{2,1},{3,2},{4,3},{5,4},{6,5},{7,6}} | collective-permute-start | bytes 6291464 | tf_op jit(solution)/shard_map/ppermute | solution.py:593
  87.7 345.7 %all-gather.7.cloned.1.call-start = ((), (), s32[]{:S(2)}) async-start(), calls=%async_computation.1 | async-start | bytes 4718592 | tf_op jit(solution)/shard_map/all_gather | solution.py:651
  90.3 38.4 %collective-permute-start.8 = (f32[2,1280,128]{2,1,0:T(8,128)}, f32[2,1280,128]{2,1,0:T(8,128)}, u32[]{:S(2)}, u32[]{:S(2)}) collective-permute-start(f32[2,1280,128]{2,1,0:T(8,128)} %broadcast_select_fusion.7), channel_id=1, source_target_pairs={{0,16},{1,17},{2,18},{3,19},{4,20},{5,21},{6,22},{7,23}} | collective-permute-start | bytes 3932168 | tf_op jit(solution)/shard_map/ppermute | solution.py:593
  97.1 116.6 %collective-permute-start.12 = (f32[2,512,1536]{2,1,0:T(8,128)}, f32[2,512,1536]{2,1,0:T(8,128)}, u32[]{:S(2)}, u32[]{:S(2)}) collective-permute-start(f32[2,512,1536]{2,1,0:T(8,128)} %pad_maximum_fusion.rest_0_.p_ref), channel_id=1, source_target_pairs={{0,16},{1,17},{2,18},{3,19},{4,20},{5,21},{6,22},{7,23}} | collective-permute-start | bytes 18874376 | tf_op jit(solution)/shard_map/ppermute | solution.py:593
  130.2 37.8 %collective-permute-start.9 = (f32[2,1280,128]{2,1,0:T(8,128)S(1)}, f32[2,1280,128]{2,1,0:T(8,128)}, u32[]{:S(2)}, u32[]{:S(2)}) collective-permute-start(f32[2,1280,128]{2,1,0:T(8,128)S(1)} %broadcast_select_fusion.8), channel_id=1, source_target_pairs={{0,8},{1,9},{2,10},{3,11},{4,12},{5,13},{6,14},{7,15},{16,24},{17,... | collective-permute-start | bytes 3932168 | tf_op jit(solution)/shard_map/ppermute | solution.py:593
  135.7 21.9 %collective-permute-start.11 = (f32[512,512]{1,0:T(8,128)}, f32[512,512]{1,0:T(8,128)}, u32[]{:S(2)}, u32[]{:S(2)}) collective-permute-start(f32[512,512]{1,0:T(8,128)} %shard_map.51), channel_id=1, source_target_pairs={{1,0},{2,1},{3,2},{4,3},{5,4},{6,5},{7,6},{9,8},{10,9},{11,10},{12... | collective-permute-start | bytes 3145736 | tf_op jit(solution)/shard_map/ppermute | solution.py:593
  169.2 44.5 %copy-start = (f32[2,512,1024]{2,1,0:T(8,128)S(1)}, f32[2,512,1024]{2,1,0:T(8,128)}, u32[]{:S(2)}) copy-start(f32[2,512,1024]{2,1,0:T(8,128)} %slice.13) | copy-start | bytes 12582916
  220.6 15.1 %copy-start.1 = (f32[512,1024]{1,0:T(8,128)S(1)}, f32[512,1024]{1,0:T(8,128)}, u32[]{:S(2)}) copy-start(f32[512,1024]{1,0:T(8,128)} %shard_map.52.m_ref) | copy-start | bytes 6291460
  220.6 42.2 %copy-start.4 = (f32[512,256]{1,0:T(8,128)S(1)}, f32[512,256]{1,0:T(8,128)}, u32[]{:S(2)}) copy-start(f32[512,256]{1,0:T(8,128)} %get-tuple-element.41) | copy-start | bytes 1572868
  220.6 128.6 %collective-permute-start.13 = (f32[2,512,1536]{2,1,0:T(8,128)}, f32[2,512,1536]{2,1,0:T(8,128)}, u32[]{:S(2)}, u32[]{:S(2)}) collective-permute-start(f32[2,512,1536]{2,1,0:T(8,128)} %broadcast_select_fusion.h_ref), channel_id=1, source_target_pairs={{0,8},{1,9},{2,10},{3,11},{4,12},{5,13},{6,14},{7,15},{16,24},{17,... | collective-permute-start | bytes 18874376 | tf_op jit(solution)/shard_map/ppermute | solution.py:593
  229.1 34.7 %copy-start.3 = (f32[512,256]{1,0:T(8,128)S(1)}, f32[512,256]{1,0:T(8,128)}, u32[]{:S(2)}) copy-start(f32[512,256]{1,0:T(8,128)} %get-tuple-element.43) | copy-start | bytes 1572868
  229.1 36.4 %collective-permute-start.22 = (f32[1,1280,128]{2,1,0:T(8,128)}, f32[1,1280,128]{2,1,0:T(8,128)}, u32[]{:S(2)}, u32[]{:S(2)}) collective-permute-start(f32[1,1280,128]{2,1,0:T(8,128)} %shard_map.62), channel_id=1, source_target_pairs={{0,1}} | collective-permute-start | bytes 1966088 | tf_op jit(solution)/shard_map/ppermute | solution.py:593
  230.7 6.3 %collective-permute-start.16 = (f32[256,512]{1,0:T(8,128)}, f32[256,512]{1,0:T(8,128)}, u32[]{:S(2)}, u32[]{:S(2)}) collective-permute-start(f32[256,512]{1,0:T(8,128)} %bitcast.8.rest_1_), channel_id=1, source_target_pairs={{0,0},{1,1},{2,10},{3,11},{4,20},{5,21},{6,30},{7,31}} | collective-permute-start | bytes 1572872 | tf_op jit(solution)/shard_map/ppermute | solution.py:593
  234.2 30.6 %collective-permute-start.17 = (f32[256,512]{1,0:T(8,128)}, f32[256,512]{1,0:T(8,128)}, u32[]{:S(2)}, u32[]{:S(2)}) collective-permute-start(f32[256,512]{1,0:T(8,128)} %bitcast.31), channel_id=1, source_target_pairs={{0,2},{1,3},{2,12},{3,13},{4,22},{5,23},{6,24},{7,25}} | collective-permute-start | bytes 1572872 | tf_op jit(solution)/shard_map/ppermute | solution.py:593
  235.7 58.9 %collective-permute-start.27 = (f32[512,1024]{1,0:T(8,128)S(1)}, f32[512,1024]{1,0:T(8,128)}, u32[]{:S(2)}, u32[]{:S(2)}) collective-permute-start(f32[512,1024]{1,0:T(8,128)S(1)} %copy-done.1), channel_id=1, source_target_pairs={{0,16},{1,17},{2,18},{3,19},{4,20},{5,21},{6,22},{7,23}} | collective-permute-start | bytes 6291464 | tf_op jit(solution)/shard_map/ppermute | solution.py:593
  237.0 92.6 %collective-permute-start.14 = (f32[2,512,1024]{2,1,0:T(8,128)}, f32[2,512,1024]{2,1,0:T(8,128)}, u32[]{:S(2)}, u32[]{:S(2)}) collective-permute-start(f32[2,512,1024]{2,1,0:T(8,128)} %slice.13), channel_id=1, source_target_pairs={{8,0},{9,1},{10,2},{11,3},{12,4},{13,5},{14,6},{15,7},{16,8},{17,9... | collective-permute-start | bytes 12582920 | tf_op jit(solution)/shard_map/ppermute | solution.py:593
  264.8 3.2 collective-permute-start.18
  265.5 12.3 %collective-permute-start.19 = (f32[256,512]{1,0:T(8,128)}, f32[256,512]{1,0:T(8,128)S(1)}, u32[]{:S(2)}, u32[]{:S(2)}) collective-permute-start(f32[256,512]{1,0:T(8,128)} %bitcast.11), channel_id=1, source_target_pairs={{0,6},{1,7},{2,8},{3,9},{4,18},{5,19},{6,28},{7,29}} | collective-permute-start | bytes 1572872 | tf_op jit(solution)/shard_map/ppermute | solution.py:593
  268.0 12.1 %collective-permute-start.23 = (f32[1,1280,128]{2,1,0:T(8,128)S(1)}, f32[1,1280,128]{2,1,0:T(8,128)S(1)}, u32[]{:S(2)}, u32[]{:S(2)}) collective-permute-start(f32[1,1280,128]{2,1,0:T(8,128)S(1)} %broadcast_select_fusion.10), channel_id=1, source_target_pairs={{0,4},{1,5}} | collective-permute-start | bytes 1966088 | tf_op jit(solution)/shard_map/ppermute | solution.py:593
  280.2 20.4 %collective-permute-start.24 = (f32[1,1280,128]{2,1,0:T(8,128)S(1)}, f32[1,1280,128]{2,1,0:T(8,128)S(1)}, u32[]{:S(2)}, u32[]{:S(2)}) collective-permute-start(f32[1,1280,128]{2,1,0:T(8,128)S(1)} %broadcast_select_fusion.11), channel_id=1, source_target_pairs={{0,2},{1,3},{4,6},{5,7}} | collective-permute-start | bytes 1966088 | tf_op jit(solution)/shard_map/ppermute | solution.py:593
  297.9 42.5 %collective-permute-start.28 = (f32[512,1024]{1,0:T(8,128)}, f32[512,1024]{1,0:T(8,128)}, u32[]{:S(2)}, u32[]{:S(2)}) collective-permute-start(f32[512,1024]{1,0:T(8,128)} %broadcast_select_fusion.1), channel_id=1, source_target_pairs={{0,8},{1,9},{2,10},{3,11},{4,12},{5,13},{6,14},{7,15},{16,24},{17,... | collective-permute-start | bytes 6291464 | tf_op jit(solution)/shard_map/ppermute | solution.py:593
  300.6 27.1 %collective-permute-start.25 = (f32[1,1280,128]{2,1,0:T(8,128)S(1)}, f32[1,1280,128]{2,1,0:T(8,128)S(1)}, u32[]{:S(2)}, u32[]{:S(2)}) collective-permute-start(f32[1,1280,128]{2,1,0:T(8,128)S(1)} %broadcast_select_fusion.12), channel_id=1, source_target_pairs={{0,16},{1,17},{2,18},{3,19},{4,20},{5,21},{6,22},{7,23}} | collective-permute-start | bytes 1966088 | tf_op jit(solution)/shard_map/ppermute | solution.py:593
  306.6 49.8 %collective-permute-start.20 = (f32[2,2,256,512]{3,2,1,0:T(8,128)}, f32[2,2,256,512]{3,2,1,0:T(8,128)S(1)}, u32[]{:S(2)}, u32[]{:S(2)}) collective-permute-start(f32[2,2,256,512]{3,2,1,0:T(8,128)} %get-tuple-element.34), channel_id=1, source_target_pairs={{0,16},{1,17},{2,18},{3,19},{4,20},{5,21},{6,22},{7,23}} | collective-permute-start | bytes 6291464 | tf_op jit(solution)/shard_map/ppermute | solution.py:593
  327.7 39.7 %collective-permute-start.4 = (f32[2,2,256,512]{3,2,1,0:T(8,128)}, f32[2,2,256,512]{3,2,1,0:T(8,128)}, u32[]{:S(2)}, u32[]{:S(2)}) collective-permute-start(f32[2,2,256,512]{3,2,1,0:T(8,128)} %get-tuple-element.35), channel_id=1, source_target_pairs={{8,0},{9,1},{10,2},{11,3},{12,4},{13,5},{14,6},{15,7},{16,8},{17,9... | collective-permute-start | bytes 6291464 | tf_op jit(solution)/shard_map/ppermute | solution.py:593
  329.7 18.6 %collective-permute-start.26 = (f32[1,1280,128]{2,1,0:T(8,128)S(1)}, f32[1,1280,128]{2,1,0:T(8,128)S(1)}, u32[]{:S(2)}, u32[]{:S(2)}) collective-permute-start(f32[1,1280,128]{2,1,0:T(8,128)S(1)} %broadcast_select_fusion.13), channel_id=1, source_target_pairs={{0,8},{1,9},{2,10},{3,11},{4,12},{5,13},{6,14},{7,15},{16,24},{17,... | collective-permute-start | bytes 1966088 | tf_op jit(solution)/shard_map/ppermute | solution.py:593
  340.4 110.2 %collective-permute-start.15 = (f32[1536,512]{1,0:T(8,128)}, f32[1536,512]{1,0:T(8,128)S(1)}, u32[]{:S(2)}, u32[]{:S(2)}) collective-permute-start(f32[1536,512]{1,0:T(8,128)} %shard_map.60), channel_id=1, source_target_pairs={{1,0},{2,1},{3,2},{4,3},{5,4},{6,5},{7,6},{9,8},{10,9},{11,10},{12... | collective-permute-start | bytes 9437192 | tf_op jit(solution)/shard_map/ppermute | solution.py:593
  358.5 53.6 %collective-permute-start.21 = (f32[2,2,256,512]{3,2,1,0:T(8,128)S(1)}, f32[2,2,256,512]{3,2,1,0:T(8,128)S(1)}, u32[]{:S(2)}, u32[]{:S(2)}) collective-permute-start(f32[2,2,256,512]{3,2,1,0:T(8,128)S(1)} %broadcast_select_fusion.3), channel_id=1, source_target_pairs={{0,8},{1,9},{2,10},{3,11},{4,12},{5,13},{6,14},{7,15},{16,24},{17,... | collective-permute-start | bytes 6291464 | tf_op jit(solution)/shard_map/ppermute | solution.py:593
  450.7 1.7 copy-start.2
Sparse Core Ops, SparseCore 0:
  87.9 140.2 all-gather.4
  280.2 109.0 all-gather.6
